TPU v7x, 512 devices: a whole 4x4x16 slice. The times are simulated.
512 devices in a mesh: row: 16 (over z), col: 8 (over y, core), rep: 4 (over x).
Axes of the slice: x: 4, y: 4, z: 16, core: 2. Of those that a mesh axis runs over, the one named last changes fastest.
Arguments:
- momentum: bfloat16 [8192, 32768], P('row', ('col', 'rep')), may hold values from -16 to 16
- gradient: bfloat16 [8192, 32768], P('row', ('col', 'rep')), may hold values from -16 to 16
- right_prev: bfloat16 [32768, 256], P(('col', 'rep')), may hold values from -0.03125 to 0.03125
Outputs:
- momentum_next: bfloat16 [8192, 32768], P('row', ('col', 'rep'))
- left_factor: float32 [8192, 256], P('row')
- right_factor: float32 [32768, 256], P(('col', 'rep'))
All inputs are finite; a program needn't handle non-finite values.
Results may differ from a plain program's by a relative error of at most 0.013.
Values may be sent and summed in bfloat16 or wider, within the bound.
No kernel may reach another device: no remote copies, remote signals or barrier semaphores. Data moves between devices by JAX's collectives and lax.ppermute only.
A program may use at most 64 MiB of HBM per device.

v0:
```python
import jax
import jax.numpy as jnp
from jax import lax
from jax.sharding import PartitionSpec as P


def orthonormal(left_raw, gram_matrix):
    factor = jnp.linalg.cholesky(gram_matrix)
    return jax.scipy.linalg.solve_triangular(factor, left_raw.T, lower=True).T


def gram_local(left_raw):
    return jnp.dot(
        left_raw.T, left_raw, precision=lax.Precision.HIGHEST, preferred_element_type=jnp.float32
    )


def local(momentum, gradient, right_prev):
    buffer = (momentum.astype(jnp.float32) + gradient.astype(jnp.float32)).astype(jnp.bfloat16)
    left_partial = jnp.dot(buffer, right_prev, preferred_element_type=jnp.float32)
    left_raw = lax.psum(left_partial, ("col", "rep"))
    gram_matrix = lax.psum(gram_local(left_raw), "row")
    left_factor = orthonormal(left_raw, gram_matrix)
    left_low = left_factor.astype(jnp.bfloat16)
    right_partial = lax.dot_general(
        buffer, left_low, (((0,), (0,)), ((), ())), preferred_element_type=jnp.float32
    )
    right_low = lax.psum(right_partial, "row").astype(jnp.bfloat16)
    right_wide = right_low.astype(jnp.float32)
    column_sums = lax.psum(jnp.sum(right_wide * right_wide, axis=0), ("col", "rep"))
    outer = lax.dot_general(
        left_low, right_low, (((1,), (1,)), ((), ())), preferred_element_type=jnp.float32
    )
    momentum_next = (buffer.astype(jnp.float32) - 0.1 * outer).astype(jnp.bfloat16)
    right_factor = right_wide / (jnp.sqrt(column_sums) + 1e-08)
    return (momentum_next, left_factor, right_factor)


def solution(mesh):
    placed = (P("row", ("col", "rep")), P("row", ("col", "rep")), P(("col", "rep"), None))
    return jax.shard_map(
        local,
        mesh=mesh,
        in_specs=placed,
        out_specs=(P("row", ("col", "rep")), P("row", None), P(("col", "rep"), None)),
        check_vma=False,
    )
```

profile of v0, /device:TPU:1, one launch (start us, length us, event | category | flops | bytes accessed | tf_op | source)
XLA Modules:
  0.0 496.9 jit_solution(13986211449006081119)
XLA Ops:
  7.2 1.0 copy-done
  8.2 2.8 fusion.13
  11.1 140.2 %all-reduce.5.cloned.1.call-done = f32[512,256]{1,0:T(8,128)} async-done(((f32[512,256]{1,0:T(8,128)}), f32[512,256]{1,0:T(8,128)}) %all-reduce.5.cloned.1.call-update) | async-done | bytes 524304 | tf_op jit(solution)/shard_map/psum | solution.py:21
  151.3 2.9 fusion.15
  154.2 126.0 %all-reduce.7.cloned.1.call-done = f32[256,256]{0,1:T(8,128)} async-done(((f32[256,256]{0,1:T(8,128)}), f32[256,256]{0,1:T(8,128)}) %all-reduce.7.cloned.1.call-update) | async-done | bytes 262160 | tf_op jit(solution)/shard_map/psum | solution.py:22
  280.3 1.1 copy.7
  281.4 1.0 fusion.3
  282.4 11.7 %cholesky.50 = f32[128,128]{1,0:T(8,128)S(1)} custom-call(f32[128,128]{1,0:T(8,128)S(1)} %cholesky.118), custom_call_target="Cholesky" | custom-call | tf_op jit(solution)/shard_map/jit(cholesky)/cholesky | solution.py:8
  294.1 9.8 %custom-call.15 = f32[1,128,128]{1,2,0:T(8,128)S(1)} custom-call(f32[1,128,128]{2,1,0:T(8,128)S(1)} %get-tuple-element.27), custom_call_target="InvertDiagBlocksLowerTriangular" | custom-call | tf_op jit(solution)/shard_map/jit(cholesky)/cholesky | solution.py:8
  304.5 11.7 %cholesky.105 = f32[128,128]{1,0:T(8,128)S(1)} custom-call(f32[128,128]{1,0:T(8,128)S(1)} %convolution_subtract_fusion.1), custom_call_target="Cholesky" | custom-call | tf_op jit(solution)/shard_map/jit(cholesky)/cholesky | solution.py:8
  316.2 0.6 compare_reduce_fusion
  318.3 4.1 while.1
  318.4 0.6 fusion.25
  319.0 1.4 bitcast_dynamic-update-slice_fusion.2
  321.0 1.4 bitcast_dynamic-update-slice_fusion.2
  322.4 19.7 %custom-call.16 = f32[2,128,128]{1,2,0:T(8,128)S(1)} custom-call(f32[2,128,128]{2,1,0:T(8,128)S(1)} %get-tuple-element.10), custom_call_target="InvertDiagBlocksLowerTriangular" | custom-call | tf_op jit(solution)/shard_map/jit(_solve_triangular)/triangular_solve | solution.py:9
  342.6 1.6 convolution_subtract_fusion
  344.6 0.9 maximum_bitcast_fusion
  345.4 1.6 fusion.5
  347.1 54.9 %all-reduce.8 = bf16[1024,256]{1,0:T(8,128)(2,1)S(1)} all-reduce(f32[1024,256]{1,0:T(8,128)} %fusion.5), channel_id=1, replica_groups=mesh['row'=16,'col'=8,'rep'=4] {'row'}, use_global_device_ids=true, to_apply=%region_6.7 | all-reduce | flops 262144 | bytes 1572864 | tf_op jit(solution)/shard_map/psum | solution.py:28
  402.1 2.5 subtract_convert_fusion
  404.6 2.0 copy.8
  406.6 82.3 %psum.31 = f32[256]{0:T(256)S(1)} all-reduce(f32[256]{0:T(256)S(1)} %fusion), channel_id=1, replica_groups=mesh['row'=16,'col'=8,'rep'=4] {'col','rep'}, use_global_device_ids=true, to_apply=%region_8.9 | all-reduce | flops 256 | bytes 2048 | tf_op jit(solution)/shard_map/psum | solution.py:30
  489.0 1.1 convert_divide_fusion
  (32 shorter events, 2.4 us)
Async XLA Ops:
  7.2 1.0 copy-start
  7.2 144.1 %all-reduce.5.cloned.1.call-start = ((), (), s32[]{:S(2)}) async-start(), calls=%async_computation | async-start | bytes 1048576 | tf_op jit(solution)/shard_map/psum | solution.py:21
  11.0 269.3 %all-reduce.7.cloned.1.call-start = ((), (), s32[]{:S(2)}) async-start(), calls=%async_computation.1 | async-start | bytes 524288 | tf_op jit(solution)/shard_map/psum | solution.py:22
  304.0 38.1 %copy-start.3 = (f32[512,256]{1,0:T(8,128)S(1)}, f32[512,256]{1,0:T(8,128)}, u32[]{:S(2)}) copy-start(f32[512,256]{1,0:T(8,128)} %all-reduce.5.cloned.1.call-done) | copy-start | bytes 1572868
  322.4 19.7 %copy-start.5 = (f32[256,256]{1,0:T(8,128)}, f32[256,256]{1,0:T(8,128)S(1)}, u32[]{:S(2)}) copy-start(f32[256,256]{1,0:T(8,128)S(1)} %get-tuple-element.81) | copy-start | bytes 786436
  342.5 2.9 copy-start.1
  342.5 2.9 copy-start.2
  344.6 0.9 copy-start.4
Sparse Core Ops, SparseCore 0:
  11.8 139.4 all-reduce.4
  154.3 125.8 all-reduce.6
where the time goes:
time: 500 us; the launch traced here: 497 us
  waiting for transfers between devices  266 us (53%)
  blocking collectives  137 us (27%)
  other arithmetic  56.7 us (11%)
  between operations  15.5 us (3%)
  matrix products  12.6 us (3%)
  local copies, waits for them, and re-layouts  8.18 us (2%)
    psum x1, waiting for transfers between devices, local(): left_raw = lax.psum(left_partial, ('col', 'rep'))  140 us
    psum x1, waiting for transfers between devices, local(): gram_matrix = lax.psum(gram_local(left_raw), 'row')  126 us
    psum x1, blocking collectives, local(): lax.psum(jnp.sum(right_wide * right_wide, axis=0), ('col', 'rep'))  82.3 us
    psum x1, blocking collectives, local(): right_low = lax.psum(right_partial, 'row').astype(jnp.bfloat16)  54.9 us
    another operation x6, other arithmetic, orthonormal(): factor = jnp.linalg.cholesky(gram_matrix)  34 us
    another operation x3, other arithmetic, orthonormal(): return jax.scipy.linalg.solve_triangular(factor, left_raw.T, lower=True).T  19.7 us
  transfers between devices with their start and end apart: 2, of which 2 were waited for; matrix products, arithmetic and copies ran while one was open for 0% of the time, Pallas kernels for 0%

commit v1 on v0

v1 whole, which is shorter than its diff:
```python
import jax
import jax.numpy as jnp
from jax import lax
from jax.experimental import pallas as pl
from jax.experimental.pallas import tpu as pltpu
from jax.sharding import PartitionSpec as P

RANK = 256
BLOCK = 64
WIDE = ("col", "rep")


def dot32(a, b, a_dim, b_dim):
    return lax.dot_general(
        a,
        b,
        (((a_dim,), (b_dim,)), ((), ())),
        precision=lax.Precision.HIGHEST,
        preferred_element_type=jnp.float32,
    )


def eliminate(rows, offset, sub):
    count = len(rows)
    done = []
    for group in range(count):
        first = offset + 8 * group
        cols = [
            [
                jnp.broadcast_to(rows[r][:, first + k : first + k + 1], (8, 128))
                for k in range(8)
            ]
            for r in range(group, count)
        ]
        scale = jnp.zeros((8, 128), jnp.float32)
        for k in range(8):
            pivot = jnp.broadcast_to(cols[0][k][k : k + 1, :], (8, 128))
            inverse = 1.0 / pivot
            scale = jnp.where(sub == k, lax.rsqrt(pivot), scale)
            pivot_row = jnp.broadcast_to(rows[group][k : k + 1, :], (8, 128)) * inverse
            pivot_cols = [
                jnp.broadcast_to(cols[0][j][k : k + 1, :], (8, 128)) * inverse
                for j in range(k + 1, 8)
            ]
            for r in range(group, count):
                factor = cols[r - group][k]
                if r == group:
                    if k == 7:
                        continue
                    factor = jnp.where(sub > k, factor, 0.0)
                rows[r] = rows[r] - factor * pivot_row
                for j in range(k + 1, 8):
                    cols[r - group][j] = cols[r - group][j] - factor * pivot_cols[j - k - 1]
        done.append(rows[group] * scale)
    return done


def inverse_factor_kernel(gram_ref, out_ref, rest_ref):
    sub = lax.broadcasted_iota(jnp.int32, (8, 128), 0)
    lane = lax.broadcasted_iota(jnp.int32, (8, 128), 1)
    rest_ref[...] = gram_ref[...]
    out_ref[...] = jnp.zeros((RANK, RANK), jnp.float32)
    for low in range(0, RANK, BLOCK):
        high = low + BLOCK
        base = low // 128 * 128
        offset = low - base
        other = BLOCK - offset
        rows = []
        for r in range(BLOCK // 8):
            held = rest_ref[low + 8 * r : low + 8 * r + 8, base : base + 128]
            unit = jnp.where(lane == other + 8 * r + sub, 1.0, 0.0)
            rows.append(jnp.where((lane >= offset) & (lane < offset + BLOCK), held, unit))
        block = jnp.concatenate(eliminate(rows, offset, sub), axis=0)
        inverse = block[:, other : other + BLOCK]
        if low:
            out_ref[low:high, 0:low] = dot32(inverse, out_ref[low:high, 0:low], 1, 0)
        out_ref[low:high, low:high] = inverse
        if high < RANK:
            upper = dot32(inverse, rest_ref[low:high, high:RANK], 1, 0)
            solved = out_ref[low:high, 0:high]
            rest_ref[high:RANK, high:RANK] = rest_ref[high:RANK, high:RANK] - dot32(
                upper, upper, 0, 0
            )
            out_ref[high:RANK, 0:high] = out_ref[high:RANK, 0:high] - dot32(upper, solved, 0, 0)


def inverse_factor(gram_matrix):
    return pl.pallas_call(
        inverse_factor_kernel,
        out_shape=jax.ShapeDtypeStruct((RANK, RANK), jnp.float32),
        in_specs=[pl.BlockSpec(memory_space=pltpu.VMEM)],
        out_specs=pl.BlockSpec(memory_space=pltpu.VMEM),
        scratch_shapes=[pltpu.VMEM((RANK, RANK), jnp.float32)],
        cost_estimate=pl.CostEstimate(flops=400_000_000, bytes_accessed=524288, transcendentals=0),
        name="inverse_factor",
    )(gram_matrix)


def scatter_sum(x, axes, count):
    parts = x.reshape(count, x.shape[0] // count, x.shape[1])
    return jnp.sum(lax.all_to_all(parts, axes, 0, 0, tiled=True), axis=0)


def gather(x, axes, count):
    return lax.all_to_all(
        jnp.broadcast_to(x[None], (count,) + x.shape), axes, 0, 0, tiled=True
    )


def split3(x):
    high = lax.reduce_precision(x, 8, 7)
    rest = x - high
    middle = lax.reduce_precision(rest, 8, 7)
    return [v.astype(jnp.bfloat16) for v in (high, middle, rest - middle)]


def local(wide, tall, momentum, gradient, right_prev):
    place = lax.axis_index(WIDE)
    buffer = (momentum.astype(jnp.float32) + gradient.astype(jnp.float32)).astype(jnp.bfloat16)
    left_partial = jnp.dot(buffer, right_prev, preferred_element_type=jnp.float32)
    rows = left_partial.shape[0]
    left_rows = scatter_sum(left_partial, WIDE, wide)
    left_raw = gather(left_rows, WIDE, wide).reshape(rows, RANK)

    share = RANK // wide
    own = lax.dynamic_slice(left_raw, (0, place * share), (rows, share))
    gram_rows = jnp.sum(gather(dot32(own, left_raw, 0, 0), "row", tall), axis=0)
    gram_matrix = gather(gram_rows, WIDE, wide).reshape(RANK, RANK)
    inverse = inverse_factor(gram_matrix)

    pieces = jnp.concatenate(split3(left_raw), axis=1)
    product = lax.dot_general(
        buffer, pieces, (((0,), (0,)), ((), ())), preferred_element_type=jnp.float32
    )
    wide_partial = product[:, :RANK] + (product[:, RANK : 2 * RANK] + product[:, 2 * RANK :])
    right_raw = scatter_sum(wide_partial, "row", tall)

    left_factor = dot32(left_raw, inverse, 1, 1)
    left_low = left_factor.astype(jnp.bfloat16)
    right_rows = dot32(right_raw, inverse, 1, 1).astype(jnp.bfloat16)
    right_low = gather(right_rows, "row", tall).reshape(buffer.shape[1], RANK)
    right_wide = right_low.astype(jnp.float32)
    own_sums = jnp.sum(right_wide * right_wide, axis=0, keepdims=True)
    column_sums = jnp.sum(gather(own_sums, WIDE, wide), axis=0)
    outer = lax.dot_general(
        left_low, right_low, (((1,), (1,)), ((), ())), preferred_element_type=jnp.float32
    )
    momentum_next = (buffer.astype(jnp.float32) - 0.1 * outer).astype(jnp.bfloat16)
    right_factor = right_wide / (jnp.sqrt(column_sums) + 1e-08)
    return (momentum_next, left_factor, right_factor)


def solution(mesh):
    wide = mesh.shape["col"] * mesh.shape["rep"]
    tall = mesh.shape["row"]
    placed = (P("row", WIDE), P("row", WIDE), P(WIDE, None))

    def run(momentum, gradient, right_prev):
        return local(wide, tall, momentum, gradient, right_prev)

    return jax.shard_map(
        run,
        mesh=mesh,
        in_specs=placed,
        out_specs=(P("row", WIDE), P("row", None), P(WIDE, None)),
        check_vma=False,
    )
```

time: 500 us -> 193 us (0.39)
  waiting for transfers between devices: 266 us -> 89.5 us
  blocking collectives: 137 us -> 21 us
  other arithmetic: 56.7 us -> 4.62 us
  starting transfers between devices: 0.08 us -> 50.5 us
  between operations: 15.5 us -> 0.78 us
  Pallas kernels: 0 us -> 10.8 us
    psum x2 -> x0, waiting for transfers between devices: 266 us -> none  [the longest x1 140 us: local(): left_raw = lax.psum(left_partial, ('col', 'rep'))]
    psum x2 -> x0, blocking collectives: 137 us -> none  [the longest x1 82.3 us: local(): lax.psum(jnp.sum(right_wide * right_wide, axis=0), ('col', 'rep'))]
    all_to_all x0 -> x6, waiting for transfers between devices: none -> 89.5 us  [the longest x5 53.3 us: gather(): lax.all_to_all(jnp.broadcast_to(x[None], (count,) + x.shape), axes, 0, 0,...]
    another operation x9 -> x0, other arithmetic: 53.7 us -> none  [the longest x6 34 us: orthonormal(): factor = jnp.linalg.cholesky(gram_matrix)]
    all_to_all x0 -> x6, starting transfers between devices: none -> 50.5 us  [the longest x5 46.8 us: gather(): lax.all_to_all(jnp.broadcast_to(x[None], (count,) + x.shape), axes, 0, 0,...]
    all_to_all x0 -> x1, blocking collectives: none -> 21 us  [scatter_sum(): return jnp.sum(lax.all_to_all(parts, axes, 0, 0, tiled=True), axis=0)]
    pallas_call x0 -> x1, Pallas kernels: none -> 10.8 us  [inverse_factor(): pl.pallas_call(inverse_factor_kernel, out_shape=jax.ShapeDtypeStruct((RAN...]
  transfers between devices with their start and end apart: 2 -> 6, of which waited for: 2 -> 6; matrix products, arithmetic and copies ran while one was open for 0% -> 5% of each run, Pallas kernels for 0% -> 6%
where the time goes in v1:
time: 193 us; the launch traced here: 192 us
  waiting for transfers between devices  89.5 us (46%)
  starting transfers between devices  50.5 us (26%)
  blocking collectives  21 us (11%)
  Pallas kernels  10.8 us (6%)
  matrix products  10 us (5%)
  local copies, waits for them, and re-layouts  4.8 us (2%)
  other arithmetic  4.62 us (2%)
    all_to_all x5, waiting for transfers between devices, gather(): lax.all_to_all(jnp.broadcast_to(x[None], (count,) + x.shape), axes, 0, 0,...  53.3 us
    all_to_all x5, starting transfers between devices, gather(): lax.all_to_all(jnp.broadcast_to(x[None], (count,) + x.shape), axes, 0, 0,...  46.8 us
    all_to_all x1, waiting for transfers between devices, scatter_sum(): return jnp.sum(lax.all_to_all(parts, axes, 0, 0, tiled=True), axis=0)  36.3 us
    all_to_all x1, blocking collectives, scatter_sum(): return jnp.sum(lax.all_to_all(parts, axes, 0, 0, tiled=True), axis=0)  21 us
    pallas_call x1, Pallas kernels, inverse_factor(): pl.pallas_call(inverse_factor_kernel, out_shape=jax.ShapeDtypeStruct((RAN...  10.8 us
  transfers between devices with their start and end apart: 6, of which 6 were waited for; matrix products, arithmetic and copies ran while one was open for 5% of the time, Pallas kernels for 6%

profile of v1, /device:TPU:1, one launch (start us, length us, event | category | flops | bytes accessed | tf_op | source)
XLA Modules:
  0.0 192.0 jit_solution(2539184016695031623)
XLA Ops:
  0.6 1.0 copy-done
  1.7 2.0 %fusion.13 = f32[512,256]{1,0:T(8,128)S(1)} fusion(bf16[1024,256]{1,0:T(8,128)(2,1)S(1)} %copy-done, bf16[512,1024]{1,0:T(8,128)(2,1)} %param.4, bf16[512,1024]{1,0:T(8,128)(2,1)} %param.3), kind=kOutput, calls=%fused_computation.24 | convolution fusion | flops 270532608 | bytes 3145728 | tf_op jit(solution)/shard_map/dot_general | solution.py:120
  3.7 21.0 %all_to_all.35 = f32[32,16,256]{2,1,0:T(8,128)S(1)} all-to-all(f32[32,16,256]{2,1,0:T(8,128)S(1)} %bitcast.20), channel_id=1, replica_groups=mesh['row'=16,'col'=8,'rep'=4] {'col','rep'}, dimensions={0} | all-to-all | bytes 1048576 | tf_op jit(solution)/shard_map/all_to_all | solution.py:101
  24.7 0.9 broadcast_in_dim.10
  25.6 4.3 %all-to-all-start.1 = ((f32[32,16,256]{2,1,0:T(8,128)}), f32[32,16,256]{2,1,0:T(8,128)S(1)}, u32[]{:S(2)}, u32[]{:S(2)}) async-start(f32[32,16,256]{2,1,0:T(8,128)} %broadcast_in_dim.10), calls=%async_computation.1 | async-start | bytes 1048576 | tf_op jit(solution)/shard_map/all_to_all | solution.py:105
  30.0 11.4 %all-to-all-done.1 = f32[32,16,256]{2,1,0:T(8,128)S(1)} async-done(((f32[32,16,256]{2,1,0:T(8,128)}), f32[32,16,256]{2,1,0:T(8,128)S(1)}, u32[]{:S(2)}, u32[]{:S(2)}) %all-to-all-start.1) | async-done | bytes 524320 | tf_op jit(solution)/shard_map/all_to_all | solution.py:105
  42.7 13.7 %all-to-all-start.2 = ((f32[16,8,256]{2,1,0:T(8,128)}), f32[16,8,256]{2,1,0:T(8,128)S(1)}, u32[]{:S(2)}, u32[]{:S(2)}) async-start(f32[16,8,256]{2,1,0:T(8,128)} %broadcast_in_dim.11), calls=%async_computation.2 | async-start | bytes 262144 | tf_op jit(solution)/shard_map/all_to_all | solution.py:105
  56.5 2.7 %fusion.1 = f32[1024,768]{1,0:T(8,128)} fusion(bf16[512,256]{1,0:T(8,128)(2,1)S(1)} %get-tuple-element.4, bf16[512,256]{1,0:T(8,128)(2,1)S(1)} %get-tuple-element.5, bf16[512,256]{1,0:T(8,128)(2,1)S(1)} %get-tuple-element.3, bf16[512,1024]{1,0:T(8,128)(2,1)S(1)} %copy-done.1, bf16[512,1024]{1,0:T(8,128)(2,1)S(1)} %copy-done.2), kind=kOutput, calls=%fused_computation.7 | convolution fusion | flops 809762816 | bytes 6029312 | tf_op jit(solution)/shard_map/dot_general | solution.py:132
  59.2 9.2 %all-to-all-done.2 = f32[16,8,256]{2,1,0:T(8,128)S(1)} async-done(((f32[16,8,256]{2,1,0:T(8,128)}), f32[16,8,256]{2,1,0:T(8,128)S(1)}, u32[]{:S(2)}, u32[]{:S(2)}) %all-to-all-start.2) | async-done | bytes 131104 | tf_op jit(solution)/shard_map/all_to_all | solution.py:105
  68.4 0.7 broadcast_in_dim.12
  69.2 7.2 %all-to-all-start.3 = ((f32[32,8,256]{2,1,0:T(8,128)}), f32[32,8,256]{2,1,0:T(8,128)S(1)}, u32[]{:S(2)}, u32[]{:S(2)}) async-start(f32[32,8,256]{2,1,0:T(8,128)} %broadcast_in_dim.12), calls=%async_computation.3 | async-start | bytes 524288 | tf_op jit(solution)/shard_map/all_to_all | solution.py:105
  76.3 3.0 %fusion = f32[1024,256]{1,0:T(8,128)} fusion(f32[1024,768]{1,0:T(8,128)} %fusion.1), kind=kLoop, calls=%fused_computation.4 | loop fusion | flops 524288 | bytes 4194304 | tf_op jit(solution)/shard_map/add | solution.py:135
  79.4 5.9 %all-to-all-done.3 = f32[32,8,256]{2,1,0:T(8,128)S(1)} async-done(((f32[32,8,256]{2,1,0:T(8,128)}), f32[32,8,256]{2,1,0:T(8,128)S(1)}, u32[]{:S(2)}, u32[]{:S(2)}) %all-to-all-start.3) | async-done | bytes 262176 | tf_op jit(solution)/shard_map/all_to_all | solution.py:105
  85.3 3.7 %all-to-all-start.4 = ((f32[16,64,256]{2,1,0:T(8,128)}), f32[16,64,256]{2,1,0:T(8,128)S(1)}, u32[]{:S(2)}, u32[]{:S(2)}) async-start(f32[16,64,256]{2,1,0:T(8,128)} %bitcast.19), calls=%async_computation.4 | async-start | bytes 2097152 | tf_op jit(solution)/shard_map/all_to_all | solution.py:101
  89.0 10.8 %inverse_factor.1 = f32[256,256]{1,0:T(8,128)} custom-call(f32[256,256]{1,0:T(8,128)} %bitcast.21), custom_call_target="tpu_custom_call" | custom-call | flops 400000000 | bytes 524288 | tf_op jit(solution)/shard_map/inverse_factor/pallas_call | solution.py:88
  99.8 36.3 %all-to-all-done.4 = f32[16,64,256]{2,1,0:T(8,128)S(1)} async-done(((f32[16,64,256]{2,1,0:T(8,128)}), f32[16,64,256]{2,1,0:T(8,128)S(1)}, u32[]{:S(2)}, u32[]{:S(2)}) %all-to-all-start.4) | async-done | bytes 1048608 | tf_op jit(solution)/shard_map/all_to_all | solution.py:101
  136.1 1.3 convolution_convert_fusion
  137.4 0.8 broadcast_in_dim.13
  138.3 10.9 %all-to-all-start.5 = ((bf16[16,64,256]{2,1,0:T(8,128)(2,1)}), bf16[16,64,256]{2,1,0:T(8,128)(2,1)S(1)}, u32[]{:S(2)}, u32[]{:S(2)}) async-start(bf16[16,64,256]{2,1,0:T(8,128)(2,1)} %broadcast_in_dim.13), calls=%async_computation.5 | async-start | bytes 1048576 | tf_op jit(solution)/shard_map/all_to_all | solution.py:105
  149.9 22.2 %all-to-all-done.5 = bf16[16,64,256]{2,1,0:T(8,128)(2,1)S(1)} async-done(((bf16[16,64,256]{2,1,0:T(8,128)(2,1)}), bf16[16,64,256]{2,1,0:T(8,128)(2,1)S(1)}, u32[]{:S(2)}, u32[]{:S(2)}) %all-to-all-start.5) | async-done | bytes 524320 | tf_op jit(solution)/shard_map/all_to_all | solution.py:105
  172.9 10.7 %all-to-all-start.6 = ((f32[32,1,256]{2,1,0:T(1,128)}), f32[32,1,256]{2,1,0:T(1,128)S(1)}, u32[]{:S(2)}, u32[]{:S(2)}) async-start(f32[32,1,256]{2,1,0:T(1,128)} %broadcast_in_dim.14), calls=%async_computation.6 | async-start | bytes 65536 | tf_op jit(solution)/shard_map/all_to_all | solution.py:105
  183.5 2.7 %subtract_convert_fusion = bf16[512,1024]{1,0:T(8,128)(2,1)} fusion(bf16[1024,256]{1,0:T(8,128)(2,1)S(1)} %bitcast.18, f32[512,256]{1,0:T(8,128)S(1)} %fusion.14, bf16[512,1024]{1,0:T(8,128)(2,1)S(1)} %copy-done.1, bf16[512,1024]{1,0:T(8,128)(2,1)} %param.3), kind=kOutput, calls=%fused_computation | convolution fusion | flops 272760832 | bytes 4194304 | tf_op jit(solution)/shard_map/dot_general | solution.py:145
  186.3 4.6 %all-to-all-done.6 = f32[32,1,256]{2,1,0:T(1,128)S(1)} async-done(((f32[32,1,256]{2,1,0:T(1,128)}), f32[32,1,256]{2,1,0:T(1,128)S(1)}, u32[]{:S(2)}, u32[]{:S(2)}) %all-to-all-start.6) | async-done | bytes 32800 | tf_op jit(solution)/shard_map/all_to_all | solution.py:105
  190.9 1.1 convert_divide_fusion
  (22 shorter events, 3.1 us)
Async XLA Ops:
  0.6 1.0 copy-start
  24.7 31.8 %copy-start.1 = (bf16[512,1024]{1,0:T(8,128)(2,1)S(1)}, bf16[512,1024]{1,0:T(8,128)(2,1)}, u32[]{:S(2)}) copy-start(bf16[512,1024]{1,0:T(8,128)(2,1)} %param.4) | copy-start | bytes 3145732
  24.7 31.8 %copy-start.2 = (bf16[512,1024]{1,0:T(8,128)(2,1)S(1)}, bf16[512,1024]{1,0:T(8,128)(2,1)}, u32[]{:S(2)}) copy-start(bf16[512,1024]{1,0:T(8,128)(2,1)} %param.3) | copy-start | bytes 3145732
  25.6 15.7 %all-to-all-start.1 = ((f32[32,16,256]{2,1,0:T(8,128)}), f32[32,16,256]{2,1,0:T(8,128)S(1)}, u32[]{:S(2)}, u32[]{:S(2)}) async-start(f32[32,16,256]{2,1,0:T(8,128)} %broadcast_in_dim.10), calls=%async_computation.1 | async-start | bytes 1048576 | tf_op jit(solution)/shard_map/all_to_all | solution.py:105
  42.7 25.7 %all-to-all-start.2 = ((f32[16,8,256]{2,1,0:T(8,128)}), f32[16,8,256]{2,1,0:T(8,128)S(1)}, u32[]{:S(2)}, u32[]{:S(2)}) async-start(f32[16,8,256]{2,1,0:T(8,128)} %broadcast_in_dim.11), calls=%async_computation.2 | async-start | bytes 262144 | tf_op jit(solution)/shard_map/all_to_all | solution.py:105
  69.2 16.2 %all-to-all-start.3 = ((f32[32,8,256]{2,1,0:T(8,128)}), f32[32,8,256]{2,1,0:T(8,128)S(1)}, u32[]{:S(2)}, u32[]{:S(2)}) async-start(f32[32,8,256]{2,1,0:T(8,128)} %broadcast_in_dim.12), calls=%async_computation.3 | async-start | bytes 524288 | tf_op jit(solution)/shard_map/all_to_all | solution.py:105
  85.3 3.7 %copy-start.5 = (f32[32,8,256]{2,1,0:T(8,128)}, f32[32,8,256]{2,1,0:T(8,128)S(1)}, u32[]{:S(2)}) copy-start(f32[32,8,256]{2,1,0:T(8,128)S(1)} %all-to-all-done.3) | copy-start | bytes 786436
  85.3 50.7 %all-to-all-start.4 = ((f32[16,64,256]{2,1,0:T(8,128)}), f32[16,64,256]{2,1,0:T(8,128)S(1)}, u32[]{:S(2)}, u32[]{:S(2)}) async-start(f32[16,64,256]{2,1,0:T(8,128)} %bitcast.19), calls=%async_computation.4 | async-start | bytes 2097152 | tf_op jit(solution)/shard_map/all_to_all | solution.py:101
  99.8 49.5 %copy-start.4 = (f32[256,256]{1,0:T(8,128)S(1)}, f32[256,256]{1,0:T(8,128)}, u32[]{:S(2)}) copy-start(f32[256,256]{1,0:T(8,128)} %inverse_factor.1) | copy-start | bytes 786436
  138.3 33.8 %all-to-all-start.5 = ((bf16[16,64,256]{2,1,0:T(8,128)(2,1)}), bf16[16,64,256]{2,1,0:T(8,128)(2,1)S(1)}, u32[]{:S(2)}, u32[]{:S(2)}) async-start(bf16[16,64,256]{2,1,0:T(8,128)(2,1)} %broadcast_in_dim.13), calls=%async_computation.5 | async-start | bytes 1048576 | tf_op jit(solution)/shard_map/all_to_all | solution.py:105
  149.9 36.4 %copy-start.3 = (f32[512,256]{1,0:T(8,128)}, f32[512,256]{1,0:T(8,128)S(1)}, u32[]{:S(2)}) copy-start(f32[512,256]{1,0:T(8,128)S(1)} %fusion.14) | copy-start | bytes 1572868
  172.9 18.0 %all-to-all-start.6 = ((f32[32,1,256]{2,1,0:T(1,128)}), f32[32,1,256]{2,1,0:T(1,128)S(1)}, u32[]{:S(2)}, u32[]{:S(2)}) async-start(f32[32,1,256]{2,1,0:T(1,128)} %broadcast_in_dim.14), calls=%async_computation.6 | async-start | bytes 65536 | tf_op jit(solution)/shard_map/all_to_all | solution.py:105

commit v2 on v1

--- a/solution.py
+++ b/solution.py
@@ -122,23 +122,24 @@
     left_rows = scatter_sum(left_partial, WIDE, wide)
     left_raw = gather(left_rows, WIDE, wide).reshape(rows, RANK)
 
+    wide_partial = sum(
+        lax.dot_general(
+            buffer, piece, (((0,), (0,)), ((), ())), preferred_element_type=jnp.float32
+        )
+        for piece in split3(left_raw)
+    )
     share = RANK // wide
     own = lax.dynamic_slice(left_raw, (0, place * share), (rows, share))
+    own, wide_partial = lax.optimization_barrier((own, wide_partial))
+    right_raw = lax.psum_scatter(wide_partial, "row", scatter_dimension=0, tiled=True)
     gram_rows = jnp.sum(gather(dot32(own, left_raw, 0, 0), "row", tall), axis=0)
     gram_matrix = gather(gram_rows, WIDE, wide).reshape(RANK, RANK)
     inverse = inverse_factor(gram_matrix)
 
-    pieces = jnp.concatenate(split3(left_raw), axis=1)
-    product = lax.dot_general(
-        buffer, pieces, (((0,), (0,)), ((), ())), preferred_element_type=jnp.float32
-    )
-    wide_partial = product[:, :RANK] + (product[:, RANK : 2 * RANK] + product[:, 2 * RANK :])
-    right_raw = scatter_sum(wide_partial, "row", tall)
-
     left_factor = dot32(left_raw, inverse, 1, 1)
     left_low = left_factor.astype(jnp.bfloat16)
     right_rows = dot32(right_raw, inverse, 1, 1).astype(jnp.bfloat16)
-    right_low = gather(right_rows, "row", tall).reshape(buffer.shape[1], RANK)
+    right_low = lax.all_gather(right_rows, "row", axis=0, tiled=True)
     right_wide = right_low.astype(jnp.float32)
     own_sums = jnp.sum(right_wide * right_wide, axis=0, keepdims=True)
     column_sums = jnp.sum(gather(own_sums, WIDE, wide), axis=0)

time: 193 us -> 176 us (0.912)
  blocking collectives: 21 us -> 87.4 us
  waiting for transfers between devices: 89.5 us -> 24.1 us
  starting transfers between devices: 50.5 us -> 26.7 us
  between operations: 0.78 us -> 14.1 us
  local copies, waits for them, and re-layouts: 4.8 us -> 1.69 us
  matrix products: 10 us -> 7.72 us
    all_to_all x0 -> x2, blocking collectives: none -> 42.3 us  [gather(): lax.all_to_all(jnp.broadcast_to(x[None], (count,) + x.shape), axes, 0, 0,...]
    all_to_all x1 -> x0, waiting for transfers between devices: 36.3 us -> none  [scatter_sum(): return jnp.sum(lax.all_to_all(parts, axes, 0, 0, tiled=True), axis=0)]
    all_to_all x5 -> x2, waiting for transfers between devices: 53.3 us -> 17.1 us  [gather(): lax.all_to_all(jnp.broadcast_to(x[None], (count,) + x.shape), axes, 0, 0,...]
    all_gather x0 -> x1, blocking collectives: none -> 24.2 us  [local(): right_low = lax.all_gather(right_rows, 'row', axis=0, tiled=True)]
    all_to_all x5 -> x2, starting transfers between devices: 46.8 us -> 26.7 us  [gather(): lax.all_to_all(jnp.broadcast_to(x[None], (count,) + x.shape), axes, 0, 0,...]
    reduce_scatter x0 -> x1, waiting for transfers between devices: none -> 7.01 us  [local(): lax.psum_scatter(wide_partial, 'row', scatter_dimension=0, tiled=True)]
    all_to_all x1 -> x0, starting transfers between devices: 3.66 us -> none  [scatter_sum(): return jnp.sum(lax.all_to_all(parts, axes, 0, 0, tiled=True), axis=0)]
    add x1 -> x0, other arithmetic: 3.05 us -> none  [local(): product[:, :RANK] + (product[:, RANK:2 * RANK] + product[:, 2 * RANK:])]
  transfers between devices with their start and end apart: 6 -> 3, of which waited for: 6 -> 3; matrix products, arithmetic and copies ran while one was open for 5% -> 2% of each run, Pallas kernels for 6% -> 6%
where the time goes in v2:
time: 176 us
  blocking collectives  87.4 us (50%)
  starting transfers between devices  26.7 us (15%)
  waiting for transfers between devices  24.1 us (14%)
  between operations  14.1 us (8%)
  Pallas kernels  10.8 us (6%)
  matrix products  7.72 us (4%)
  other arithmetic  3.35 us (2%)
    all_to_all x2, blocking collectives, gather(): lax.all_to_all(jnp.broadcast_to(x[None], (count,) + x.shape), axes, 0, 0,...  42.3 us
    all_to_all x2, starting transfers between devices, gather(): lax.all_to_all(jnp.broadcast_to(x[None], (count,) + x.shape), axes, 0, 0,...  26.7 us
    all_gather x1, blocking collectives, local(): right_low = lax.all_gather(right_rows, 'row', axis=0, tiled=True)  24.2 us
    all_to_all x1, blocking collectives, scatter_sum(): return jnp.sum(lax.all_to_all(parts, axes, 0, 0, tiled=True), axis=0)  21 us
    all_to_all x2, waiting for transfers between devices, gather(): lax.all_to_all(jnp.broadcast_to(x[None], (count,) + x.shape), axes, 0, 0,...  17.1 us
    pallas_call x1, Pallas kernels, inverse_factor(): pl.pallas_call(inverse_factor_kernel, out_shape=jax.ShapeDtypeStruct((RAN...  10.8 us
    reduce_scatter x1, waiting for transfers between devices, local(): lax.psum_scatter(wide_partial, 'row', scatter_dimension=0, tiled=True)  7.01 us
  transfers between devices with their start and end apart: 3, of which 3 were waited for; matrix products, arithmetic and copies ran while one was open for 2% of the time, Pallas kernels for 6%

profile of v2, /device:TPU:1, one launch (start us, length us, event | category | flops | bytes accessed | tf_op | source)
XLA Modules:
  0.0 176.0 jit_solution(16896841906607120780)
XLA Ops:
  7.2 2.0 %add_convert_fusion = bf16[512,1024]{1,0:T(8,128)(2,1)S(1)} fusion(bf16[512,1024]{1,0:T(8,128)(2,1)} %param.4, bf16[512,1024]{1,0:T(8,128)(2,1)} %param.3), kind=kLoop, calls=%fused_computation.1 | loop fusion | flops 2097152 | bytes 3145728 | tf_op jit(solution)/shard_map/convert_element_type | solution.py:119
  9.2 0.4 fusion.5
  9.6 21.0 %all_to_all.25 = f32[32,16,256]{2,1,0:T(8,128)S(1)} all-to-all(f32[32,16,256]{2,1,0:T(8,128)S(1)} %bitcast.21), channel_id=1, replica_groups=mesh['row'=16,'col'=8,'rep'=4] {'col','rep'}, dimensions={0} | all-to-all | bytes 1048576 | tf_op jit(solution)/shard_map/all_to_all | solution.py:101
  30.7 0.9 broadcast_in_dim.8
  31.6 4.4 %all-to-all-start.1 = ((f32[32,16,256]{2,1,0:T(8,128)}), f32[32,16,256]{2,1,0:T(8,128)S(1)}, u32[]{:S(2)}, u32[]{:S(2)}) async-start(f32[32,16,256]{2,1,0:T(8,128)} %broadcast_in_dim.8), calls=%async_computation.1 | async-start | bytes 1048576 | tf_op jit(solution)/shard_map/all_to_all | solution.py:105
  36.0 11.3 %all-to-all-done.1 = f32[32,16,256]{2,1,0:T(8,128)S(1)} async-done(((f32[32,16,256]{2,1,0:T(8,128)}), f32[32,16,256]{2,1,0:T(8,128)S(1)}, u32[]{:S(2)}, u32[]{:S(2)}) %all-to-all-start.1) | async-done | bytes 524320 | tf_op jit(solution)/shard_map/all_to_all | solution.py:105
  47.3 0.5 fusion.3
  47.8 0.1 constant_dynamic-slice_fusion
  47.9 0.5 convolution_add_fusion.1
  48.4 1.5 convolution_add_fusion
  49.9 0.5 fusion.6
  50.5 25.5 %all_to_all.26 = f32[16,8,256]{2,1,0:T(8,128)S(1)} all-to-all(f32[16,8,256]{2,1,0:T(8,128)S(1)} %broadcast_in_dim.9), channel_id=1, replica_groups=mesh['row'=16,'col'=8,'rep'=4] {'row'}, dimensions={0} | all-to-all | bytes 262144 | tf_op jit(solution)/shard_map/all_to_all | solution.py:105
  76.1 16.7 %all_to_all.27 = f32[32,8,256]{2,1,0:T(8,128)} all-to-all(f32[32,8,256]{2,1,0:T(8,128)S(1)} %broadcast_in_dim.10), channel_id=1, replica_groups=mesh['row'=16,'col'=8,'rep'=4] {'col','rep'}, dimensions={0} | all-to-all | bytes 524288 | tf_op jit(solution)/shard_map/all_to_all | solution.py:105
  92.8 10.8 %inverse_factor.1 = f32[256,256]{1,0:T(8,128)} custom-call(f32[256,256]{1,0:T(8,128)} %bitcast.22), custom_call_target="tpu_custom_call" | custom-call | flops 400000000 | bytes 524288 | tf_op jit(solution)/shard_map/inverse_factor/pallas_call | solution.py:88
  103.6 1.6 fusion.7
  105.2 7.0 %reduce-scatter.2.cloned.1.call-done = f32[64,256]{1,0:T(8,128)} async-done(((f32[1024,256]{1,0:T(8,128)}), f32[64,256]{1,0:T(8,128)}) %reduce-scatter.2.cloned.1.call-update) | async-done | bytes 65552 | tf_op jit(solution)/shard_map/reduce_scatter | solution.py:134
  112.2 1.2 convolution_convert_fusion
  113.5 24.2 %all_gather.3 = bf16[1024,256]{1,0:T(8,128)(2,1)S(1)} all-gather(bf16[64,256]{1,0:T(8,128)(2,1)S(1)} %convolution_convert_fusion), channel_id=1, replica_groups=mesh['row'=16,'col'=8,'rep'=4] {'row'}, dimensions={0}, use_global_device_ids=true | all-gather | bytes 557056 | tf_op jit(solution)/shard_map/all_gather | solution.py:142
  137.6 0.2 fusion
  137.8 0.6 broadcast_in_dim.11
  138.4 22.3 %all-to-all-start.4 = ((f32[32,1,256]{2,1,0:T(1,128)}), f32[32,1,256]{2,1,0:T(1,128)S(1)}, u32[]{:S(2)}, u32[]{:S(2)}) async-start(f32[32,1,256]{2,1,0:T(1,128)} %broadcast_in_dim.11), calls=%async_computation.5 | async-start | bytes 65536 | tf_op jit(solution)/shard_map/all_to_all | solution.py:105
  160.8 1.4 subtract_convert_fusion
  162.2 5.8 %all-to-all-done.4 = f32[32,1,256]{2,1,0:T(1,128)S(1)} async-done(((f32[32,1,256]{2,1,0:T(1,128)}), f32[32,1,256]{2,1,0:T(1,128)S(1)}, u32[]{:S(2)}, u32[]{:S(2)}) %all-to-all-start.4) | async-done | bytes 32800 | tf_op jit(solution)/shard_map/all_to_all | solution.py:105
  168.1 1.1 convert_divide_fusion
  (14 shorter events, 0.2 us)
Async XLA Ops:
  7.2 2.0 %copy-start = (bf16[1024,256]{1,0:T(8,128)(2,1)S(1)}, bf16[1024,256]{1,0:T(8,128)(2,1)}, u32[]{:S(2)}) copy-start(bf16[1024,256]{1,0:T(8,128)(2,1)} %param.5) | copy-start | bytes 1572868
  31.6 15.7 %all-to-all-start.1 = ((f32[32,16,256]{2,1,0:T(8,128)}), f32[32,16,256]{2,1,0:T(8,128)S(1)}, u32[]{:S(2)}, u32[]{:S(2)}) async-start(f32[32,16,256]{2,1,0:T(8,128)} %broadcast_in_dim.8), calls=%async_computation.1 | async-start | bytes 1048576 | tf_op jit(solution)/shard_map/all_to_all | solution.py:105
  35.9 76.3 %reduce-scatter.2.cloned.1.call-start = ((), (), s32[]{:S(2)}) async-start(), calls=%async_computation.6 | async-start | bytes 1114112 | tf_op jit(solution)/shard_map/reduce_scatter | solution.py:134
  103.6 8.7 %copy-start.2 = (f32[256,256]{1,0:T(8,128)S(1)}, f32[256,256]{1,0:T(8,128)}, u32[]{:S(2)}) copy-start(f32[256,256]{1,0:T(8,128)} %inverse_factor.1) | copy-start | bytes 786436
  105.2 57.0 %copy-start.1 = (f32[512,256]{1,0:T(8,128)}, f32[512,256]{1,0:T(8,128)S(1)}, u32[]{:S(2)}) copy-start(f32[512,256]{1,0:T(8,128)S(1)} %fusion.7) | copy-start | bytes 1572868
  138.4 29.6 %all-to-all-start.4 = ((f32[32,1,256]{2,1,0:T(1,128)}), f32[32,1,256]{2,1,0:T(1,128)S(1)}, u32[]{:S(2)}, u32[]{:S(2)}) async-start(f32[32,1,256]{2,1,0:T(1,128)} %broadcast_in_dim.11), calls=%async_computation.5 | async-start | bytes 65536 | tf_op jit(solution)/shard_map/all_to_all | solution.py:105
Sparse Core Ops, SparseCore 0:
  50.0 62.1 reduce-scatter.1

commit v3 on v2

--- a/solution.py
+++ b/solution.py
@@ -7,6 +7,7 @@
 
 RANK = 256
 BLOCK = 64
+SPAN = 64
 WIDE = ("col", "rep")
 
 
@@ -107,32 +108,70 @@
     )
 
 
-def split3(x):
-    high = lax.reduce_precision(x, 8, 7)
-    rest = x - high
-    middle = lax.reduce_precision(rest, 8, 7)
-    return [v.astype(jnp.bfloat16) for v in (high, middle, rest - middle)]
+def project_kernel(buffer_ref, left_ref, gram_ref, out_ref):
+    left = left_ref[...]
+    high = left.astype(jnp.bfloat16)
+    rest = left - high.astype(jnp.float32)
+    middle = rest.astype(jnp.bfloat16)
+    low = (rest - middle.astype(jnp.float32)).astype(jnp.bfloat16)
+    far, near = buffer_ref.shape[1] // SPAN // out_ref.shape[0], out_ref.shape[0]
+    for i in range(far):
+        block = buffer_ref[:, i * near * SPAN : (i + 1) * near * SPAN]
+        part = sum(
+            lax.dot_general(
+                block, piece, (((0,), (0,)), ((), ())), preferred_element_type=jnp.float32
+            )
+            for piece in (low, middle, high)
+        )
+        for j in range(near):
+            out_ref[j, i * SPAN : (i + 1) * SPAN, :] = part[j * SPAN : (j + 1) * SPAN, :]
+    for j in range(near):
+        out_ref[j, far * SPAN :, :] = gram_ref[...]
+
+
+def project(buffer, left_raw, gram_rows, near):
+    columns = buffer.shape[1]
+    share = gram_rows.shape[0]
+    return pl.pallas_call(
+        project_kernel,
+        out_shape=jax.ShapeDtypeStruct((near, columns // near + share, RANK), jnp.float32),
+        in_specs=[pl.BlockSpec(memory_space=pltpu.VMEM)] * 3,
+        out_specs=pl.BlockSpec(memory_space=pltpu.VMEM),
+        compiler_params=pltpu.CompilerParams(vmem_limit_bytes=32 * 1024 * 1024),
+        cost_estimate=pl.CostEstimate(
+            flops=6 * buffer.size * RANK, bytes_accessed=3_000_000, transcendentals=0
+        ),
+        name="project",
+    )(buffer, left_raw, gram_rows)
 
 
 def local(wide, tall, momentum, gradient, right_prev):
     place = lax.axis_index(WIDE)
+    near = 4
+    far = tall // near
+    adjacent = [[i * near + j for j in range(near)] for i in range(far)]
+    strided = [[i * near + j for i in range(far)] for j in range(near)]
     buffer = (momentum.astype(jnp.float32) + gradient.astype(jnp.float32)).astype(jnp.bfloat16)
     left_partial = jnp.dot(buffer, right_prev, preferred_element_type=jnp.float32)
     rows = left_partial.shape[0]
     left_rows = scatter_sum(left_partial, WIDE, wide)
     left_raw = gather(left_rows, WIDE, wide).reshape(rows, RANK)
 
-    wide_partial = sum(
-        lax.dot_general(
-            buffer, piece, (((0,), (0,)), ((), ())), preferred_element_type=jnp.float32
-        )
-        for piece in split3(left_raw)
-    )
     share = RANK // wide
     own = lax.dynamic_slice(left_raw, (0, place * share), (rows, share))
-    own, wide_partial = lax.optimization_barrier((own, wide_partial))
-    right_raw = lax.psum_scatter(wide_partial, "row", scatter_dimension=0, tiled=True)
-    gram_rows = jnp.sum(gather(dot32(own, left_raw, 0, 0), "row", tall), axis=0)
+    blocks = project(buffer, left_raw, dot32(own, left_raw, 0, 0), near)
+    blocks = lax.all_to_all(blocks, "row", 0, 0, axis_index_groups=adjacent, tiled=True)
+    summed = jnp.sum(blocks, axis=0)
+    blocks = jnp.concatenate(
+        [
+            summed[: far * SPAN].reshape(far, SPAN, RANK),
+            jnp.broadcast_to(summed[None, far * SPAN :], (far, share, RANK)),
+        ],
+        axis=1,
+    )
+    blocks = lax.all_to_all(blocks, "row", 0, 0, axis_index_groups=strided, tiled=True)
+    right_raw = jnp.sum(blocks[:, :SPAN], axis=0)
+    gram_rows = jnp.sum(blocks[:, SPAN:], axis=0)
     gram_matrix = gather(gram_rows, WIDE, wide).reshape(RANK, RANK)
     inverse = inverse_factor(gram_matrix)
 

time: 176 us -> 179 us (1.017)
  blocking collectives: 87.4 us -> 105 us
  between operations: 14.1 us -> 0.78 us
  matrix products: 7.72 us -> 4.55 us
  starting transfers between devices: 26.7 us -> 24.1 us
  waiting for transfers between devices: 24.1 us -> 26.1 us
    all_to_all x2, blocking collectives: 42.3 us -> 59.3 us  [the longest x1 30.1 us: local(): lax.all_to_all(blocks, 'row', 0, 0, axis_index_groups=adjacent, tiled=True)]
    all_to_all x2 -> x3, waiting for transfers between devices: 17.1 us -> 26.1 us  [gather(): lax.all_to_all(jnp.broadcast_to(x[None], (count,) + x.shape), axes, 0, 0,...]
    reduce_scatter x1 -> x0, waiting for transfers between devices: 7.01 us -> none  [local(): lax.psum_scatter(wide_partial, 'row', scatter_dimension=0, tiled=True)]
    all_to_all x2 -> x3, starting transfers between devices: 26.7 us -> 24.1 us  [gather(): lax.all_to_all(jnp.broadcast_to(x[None], (count,) + x.shape), axes, 0, 0,...]
    dot_general x3 -> x0, matrix products: 2.44 us -> none  [local(): lax.dot_general(buffer, piece, (((0,), (0,)), ((), ())), preferred_elemen...]
  transfers between devices with their start and end apart: 3 -> 3, of which waited for: 3 -> 3; matrix products, arithmetic and copies ran while one was open for 2% -> 1% of each run, Pallas kernels for 6% -> 0%
where the time goes in v3:
time: 179 us
  blocking collectives  105 us (59%)
  waiting for transfers between devices  26.1 us (15%)
  starting transfers between devices  24.1 us (13%)
  Pallas kernels  11.8 us (7%)
  matrix products  4.55 us (3%)
  other arithmetic  3.46 us (2%)
  local copies, waits for them, and re-layouts  2.96 us (2%)
    all_to_all x1, blocking collectives, local(): lax.all_to_all(blocks, 'row', 0, 0, axis_index_groups=adjacent, tiled=True)  30.1 us
    all_to_all x1, blocking collectives, local(): lax.all_to_all(blocks, 'row', 0, 0, axis_index_groups=strided, tiled=True)  29.2 us
    all_to_all x3, waiting for transfers between devices, gather(): lax.all_to_all(jnp.broadcast_to(x[None], (count,) + x.shape), axes, 0, 0,...  26.1 us
    all_gather x1, blocking collectives, local(): right_low = lax.all_gather(right_rows, 'row', axis=0, tiled=True)  24.5 us
    all_to_all x3, starting transfers between devices, gather(): lax.all_to_all(jnp.broadcast_to(x[None], (count,) + x.shape), axes, 0, 0,...  24.1 us
    all_to_all x1, blocking collectives, scatter_sum(): return jnp.sum(lax.all_to_all(parts, axes, 0, 0, tiled=True), axis=0)  21 us
    pallas_call x1, Pallas kernels, inverse_factor(): pl.pallas_call(inverse_factor_kernel, out_shape=jax.ShapeDtypeStruct((RAN...  10.8 us
  transfers between devices with their start and end apart: 3, of which 3 were waited for; matrix products, arithmetic and copies ran while one was open for 1% of the time, Pallas kernels for 0%

profile of v3, /device:TPU:1, one launch (start us, length us, event | category | flops | bytes accessed | tf_op | source)
XLA Modules:
  0.0 178.6 jit_solution(14315672120399407149)
XLA Ops:
  0.6 2.0 %add_convert_fusion.buffer_ref = bf16[512,1024]{1,0:T(8,128)(2,1)S(1)} fusion(bf16[512,1024]{1,0:T(8,128)(2,1)} %param.4, bf16[512,1024]{1,0:T(8,128)(2,1)} %param.3), kind=kLoop, calls=%fused_computation.1 | loop fusion | flops 2097152 | bytes 3145728 | tf_op jit(solution)/shard_map/convert_element_type | solution.py:154
  2.7 0.4 fusion.5
  3.1 21.0 %all_to_all.30 = f32[32,16,256]{2,1,0:T(8,128)S(1)} all-to-all(f32[32,16,256]{2,1,0:T(8,128)S(1)} %bitcast.15), channel_id=1, replica_groups=mesh['row'=16,'col'=8,'rep'=4] {'col','rep'}, dimensions={0} | all-to-all | bytes 1048576 | tf_op jit(solution)/shard_map/all_to_all | solution.py:102
  24.2 0.9 broadcast_in_dim.8
  25.0 4.4 %all-to-all-start.1 = ((f32[32,16,256]{2,1,0:T(8,128)}), f32[32,16,256]{2,1,0:T(8,128)S(1)}, u32[]{:S(2)}, u32[]{:S(2)}) async-start(f32[32,16,256]{2,1,0:T(8,128)} %broadcast_in_dim.8), calls=%async_computation.1 | async-start | bytes 1048576 | tf_op jit(solution)/shard_map/all_to_all | solution.py:106
  29.4 11.4 %all-to-all-done.1 = f32[32,16,256]{2,1,0:T(8,128)S(1)} async-done(((f32[32,16,256]{2,1,0:T(8,128)}), f32[32,16,256]{2,1,0:T(8,128)S(1)}, u32[]{:S(2)}, u32[]{:S(2)}) %all-to-all-start.1) | async-done | bytes 524320 | tf_op jit(solution)/shard_map/all_to_all | solution.py:106
  40.8 0.6 fusion.2.gram_ref
  41.4 1.0 project.1
  42.5 30.1 %all_to_all.31 = f32[4,264,256]{2,1,0:T(8,128)S(1)} all-to-all(f32[4,264,256]{2,1,0:T(8,128)S(1)} %project.1), channel_id=1, replica_groups={{0,32,64,96},{128,160,192,224},{256,288,320,352},{384,416,448,480},{1,3..., dimensions={0} | all-to-all | bytes 2162688 | tf_op jit(solution)/shard_map/all_to_all | solution.py:163
  72.8 29.2 %all_to_all.32 = f32[4,72,256]{2,1,0:T(8,128)S(1)} all-to-all(f32[4,72,256]{2,1,0:T(8,128)S(1)} %pad_maximum_fusion), channel_id=1, replica_groups={{0,128,256,384},{32,160,288,416},{64,192,320,448},{96,224,352,480},{1,1..., dimensions={0} | all-to-all | bytes 589824 | tf_op jit(solution)/shard_map/all_to_all | solution.py:172
  102.0 0.7 broadcast_in_dim.10
  102.7 8.4 %all-to-all-start.4 = ((f32[32,8,256]{2,1,0:T(8,128)}), f32[32,8,256]{2,1,0:T(8,128)S(1)}, u32[]{:S(2)}, u32[]{:S(2)}) async-start(f32[32,8,256]{2,1,0:T(8,128)} %broadcast_in_dim.10), calls=%async_computation.4 | async-start | bytes 524288 | tf_op jit(solution)/shard_map/all_to_all | solution.py:106
  111.1 9.0 %all-to-all-done.4 = f32[32,8,256]{2,1,0:T(8,128)S(1)} async-done(((f32[32,8,256]{2,1,0:T(8,128)}), f32[32,8,256]{2,1,0:T(8,128)S(1)}, u32[]{:S(2)}, u32[]{:S(2)}) %all-to-all-start.4) | async-done | bytes 262176 | tf_op jit(solution)/shard_map/all_to_all | solution.py:106
  120.1 0.7 copy-done.3
  120.8 10.8 %inverse_factor.1 = f32[256,256]{1,0:T(8,128)} custom-call(f32[256,256]{1,0:T(8,128)} %bitcast.17), custom_call_target="tpu_custom_call" | custom-call | flops 400000000 | bytes 524288 | tf_op jit(solution)/shard_map/inverse_factor/pallas_call | solution.py:89
  131.5 1.6 fusion.6
  133.2 0.4 convolution_convert_fusion
  133.6 24.5 %all_gather.3 = bf16[1024,256]{1,0:T(8,128)(2,1)S(1)} all-gather(bf16[64,256]{1,0:T(8,128)(2,1)S(1)} %convolution_convert_fusion), channel_id=1, replica_groups=mesh['row'=16,'col'=8,'rep'=4] {'row'}, dimensions={0}, use_global_device_ids=true | all-gather | bytes 557056 | tf_op jit(solution)/shard_map/all_gather | solution.py:181
  158.1 0.2 fusion
  158.2 0.6 broadcast_in_dim.11
  158.9 11.4 %all-to-all-start.5 = ((f32[32,1,256]{2,1,0:T(1,128)}), f32[32,1,256]{2,1,0:T(1,128)S(1)}, u32[]{:S(2)}, u32[]{:S(2)}) async-start(f32[32,1,256]{2,1,0:T(1,128)} %broadcast_in_dim.11), calls=%async_computation.5 | async-start | bytes 65536 | tf_op jit(solution)/shard_map/all_to_all | solution.py:106
  170.3 1.5 subtract_convert_fusion
  171.8 5.8 %all-to-all-done.5 = f32[32,1,256]{2,1,0:T(1,128)S(1)} async-done(((f32[32,1,256]{2,1,0:T(1,128)}), f32[32,1,256]{2,1,0:T(1,128)S(1)}, u32[]{:S(2)}, u32[]{:S(2)}) %all-to-all-start.5) | async-done | bytes 32800 | tf_op jit(solution)/shard_map/all_to_all | solution.py:106
  177.6 1.1 convert_divide_fusion
  (17 shorter events, 0.3 us)
Async XLA Ops:
  0.6 2.0 %copy-start = (bf16[1024,256]{1,0:T(8,128)(2,1)S(1)}, bf16[1024,256]{1,0:T(8,128)(2,1)}, u32[]{:S(2)}) copy-start(bf16[1024,256]{1,0:T(8,128)(2,1)} %param.5) | copy-start | bytes 1572868
  25.0 15.7 %all-to-all-start.1 = ((f32[32,16,256]{2,1,0:T(8,128)}), f32[32,16,256]{2,1,0:T(8,128)S(1)}, u32[]{:S(2)}, u32[]{:S(2)}) async-start(f32[32,16,256]{2,1,0:T(8,128)} %broadcast_in_dim.8), calls=%async_computation.1 | async-start | bytes 1048576 | tf_op jit(solution)/shard_map/all_to_all | solution.py:106
  102.7 17.4 %all-to-all-start.4 = ((f32[32,8,256]{2,1,0:T(8,128)}), f32[32,8,256]{2,1,0:T(8,128)S(1)}, u32[]{:S(2)}, u32[]{:S(2)}) async-start(f32[32,8,256]{2,1,0:T(8,128)} %broadcast_in_dim.10), calls=%async_computation.4 | async-start | bytes 524288 | tf_op jit(solution)/shard_map/all_to_all | solution.py:106
  120.1 0.7 copy-start.3
  131.5 1.7 copy-start.2
  133.2 38.6 %copy-start.1 = (f32[512,256]{1,0:T(8,128)}, f32[512,256]{1,0:T(8,128)S(1)}, u32[]{:S(2)}) copy-start(f32[512,256]{1,0:T(8,128)S(1)} %fusion.6) | copy-start | bytes 1572868
  158.9 18.7 %all-to-all-start.5 = ((f32[32,1,256]{2,1,0:T(1,128)}), f32[32,1,256]{2,1,0:T(1,128)S(1)}, u32[]{:S(2)}, u32[]{:S(2)}) async-start(f32[32,1,256]{2,1,0:T(1,128)} %broadcast_in_dim.11), calls=%async_computation.5 | async-start | bytes 65536 | tf_op jit(solution)/shard_map/all_to_all | solution.py:106

commit v4 on v3

--- a/solution.py
+++ b/solution.py
@@ -108,7 +108,7 @@
     )
 
 
-def project_kernel(buffer_ref, left_ref, gram_ref, out_ref):
+def project_kernel(buffer_ref, left_ref, out_ref):
     left = left_ref[...]
     high = left.astype(jnp.bfloat16)
     rest = left - high.astype(jnp.float32)
@@ -125,24 +125,21 @@
         )
         for j in range(near):
             out_ref[j, i * SPAN : (i + 1) * SPAN, :] = part[j * SPAN : (j + 1) * SPAN, :]
-    for j in range(near):
-        out_ref[j, far * SPAN :, :] = gram_ref[...]
-
-
-def project(buffer, left_raw, gram_rows, near):
+
+
+def project(buffer, left_raw, near):
     columns = buffer.shape[1]
-    share = gram_rows.shape[0]
     return pl.pallas_call(
         project_kernel,
-        out_shape=jax.ShapeDtypeStruct((near, columns // near + share, RANK), jnp.float32),
-        in_specs=[pl.BlockSpec(memory_space=pltpu.VMEM)] * 3,
+        out_shape=jax.ShapeDtypeStruct((near, columns // near, RANK), jnp.float32),
+        in_specs=[pl.BlockSpec(memory_space=pltpu.VMEM)] * 2,
         out_specs=pl.BlockSpec(memory_space=pltpu.VMEM),
         compiler_params=pltpu.CompilerParams(vmem_limit_bytes=32 * 1024 * 1024),
         cost_estimate=pl.CostEstimate(
             flops=6 * buffer.size * RANK, bytes_accessed=3_000_000, transcendentals=0
         ),
         name="project",
-    )(buffer, left_raw, gram_rows)
+    )(buffer, left_raw)
 
 
 def local(wide, tall, momentum, gradient, right_prev):
@@ -159,21 +156,24 @@
 
     share = RANK // wide
     own = lax.dynamic_slice(left_raw, (0, place * share), (rows, share))
-    blocks = project(buffer, left_raw, dot32(own, left_raw, 0, 0), near)
+    gram_rows = jnp.sum(gather(dot32(own, left_raw, 0, 0), "row", tall), axis=0)
+    blocks = project(buffer, left_raw, near)
+
+    gram_rows, blocks = lax.optimization_barrier((gram_rows, blocks))
     blocks = lax.all_to_all(blocks, "row", 0, 0, axis_index_groups=adjacent, tiled=True)
-    summed = jnp.sum(blocks, axis=0)
-    blocks = jnp.concatenate(
-        [
-            summed[: far * SPAN].reshape(far, SPAN, RANK),
-            jnp.broadcast_to(summed[None, far * SPAN :], (far, share, RANK)),
-        ],
-        axis=1,
-    )
+    gram_matrix = lax.all_gather(gram_rows, "rep", axis=0, tiled=True)
+    gram_matrix = lax.all_gather(
+        gram_matrix, "col", axis=0, axis_index_groups=[[0, 1], [2, 3], [4, 5], [6, 7]], tiled=True
+    )
+    gram_matrix = lax.all_gather(
+        gram_matrix, "col", axis=0, axis_index_groups=[[0, 2, 4, 6], [1, 3, 5, 7]], tiled=True
+    )
+    blocks = jnp.sum(blocks, axis=0).reshape(far, SPAN, RANK)
+
+    gram_matrix, blocks = lax.optimization_barrier((gram_matrix, blocks))
     blocks = lax.all_to_all(blocks, "row", 0, 0, axis_index_groups=strided, tiled=True)
-    right_raw = jnp.sum(blocks[:, :SPAN], axis=0)
-    gram_rows = jnp.sum(blocks[:, SPAN:], axis=0)
-    gram_matrix = gather(gram_rows, WIDE, wide).reshape(RANK, RANK)
     inverse = inverse_factor(gram_matrix)
+    right_raw = jnp.sum(blocks, axis=0)
 
     left_factor = dot32(left_raw, inverse, 1, 1)
     left_low = left_factor.astype(jnp.bfloat16)

time: 179 us -> 170 us (0.950)
  blocking collectives: 105 us -> 75.5 us
  starting transfers between devices: 24.1 us -> 39.5 us
  waiting for transfers between devices: 26.1 us -> 29.8 us
    all_to_all x2 -> x0, blocking collectives: 59.3 us -> none  [the longest x1 30.1 us: local(): lax.all_to_all(blocks, 'row', 0, 0, axis_index_groups=adjacent, tiled=True)]
    all_gather x0 -> x3, blocking collectives: none -> 26.4 us  [the longest x1 10.1 us: local(): lax.all_gather(gram_matrix, 'col', axis=0, axis_index_groups=[[0, 2, 4, 6...]
    all_to_all x0 -> x2, starting transfers between devices: none -> 8.72 us  [the longest x1 4.39 us: local(): lax.all_to_all(blocks, 'row', 0, 0, axis_index_groups=strided, tiled=True)]
    all_to_all x3, starting transfers between devices: 24.1 us -> 30.8 us  [gather(): lax.all_to_all(jnp.broadcast_to(x[None], (count,) + x.shape), axes, 0, 0,...]
    all_gather x1, blocking collectives: 24.5 us -> 28.1 us  [local(): right_low = lax.all_gather(right_rows, 'row', axis=0, tiled=True)]
    all_to_all x0 -> x2, waiting for transfers between devices: none -> 2.64 us  [the longest x1 2.64 us: local(): lax.all_to_all(blocks, 'row', 0, 0, axis_index_groups=strided, tiled=True)]
  transfers between devices with their start and end apart: 3 -> 5, of which waited for: 3 -> 4; matrix products, arithmetic and copies ran while one was open for 1% -> 2% of each run, Pallas kernels for 0% -> 8%
where the time goes in v4:
time: 170 us; the launch traced here: 169 us
  blocking collectives  75.5 us (44%)
  starting transfers between devices  39.5 us (23%)
  waiting for transfers between devices  29.8 us (18%)
  Pallas kernels  12.8 us (8%)
  matrix products  4.54 us (3%)
  other arithmetic  4.15 us (2%)
  local copies, waits for them, and re-layouts  2.19 us (1%)
    all_to_all x3, starting transfers between devices, gather(): lax.all_to_all(jnp.broadcast_to(x[None], (count,) + x.shape), axes, 0, 0,...  30.8 us
    all_gather x1, blocking collectives, local(): right_low = lax.all_gather(right_rows, 'row', axis=0, tiled=True)  28.1 us
    all_to_all x3, waiting for transfers between devices, gather(): lax.all_to_all(jnp.broadcast_to(x[None], (count,) + x.shape), axes, 0, 0,...  27.2 us
    all_to_all x1, blocking collectives, scatter_sum(): return jnp.sum(lax.all_to_all(parts, axes, 0, 0, tiled=True), axis=0)  21 us
    pallas_call x1, Pallas kernels, inverse_factor(): pl.pallas_call(inverse_factor_kernel, out_shape=jax.ShapeDtypeStruct((RAN...  10.8 us
    all_gather x1, blocking collectives, local(): lax.all_gather(gram_matrix, 'col', axis=0, axis_index_groups=[[0, 2, 4, 6...  10.1 us
    all_gather x1, blocking collectives, local(): gram_matrix = lax.all_gather(gram_rows, 'rep', axis=0, tiled=True)  9.26 us
    all_gather x1, blocking collectives, local(): lax.all_gather(gram_matrix, 'col', axis=0, axis_index_groups=[[0, 1], [2,...  6.98 us
  transfers between devices with their start and end apart: 5, of which 4 were waited for; matrix products, arithmetic and copies ran while one was open for 2% of the time, Pallas kernels for 8%

profile of v4, /device:TPU:1, one launch (start us, length us, event | category | flops | bytes accessed | tf_op | source)
XLA Modules:
  0.0 169.3 jit_solution(14216326024264196130)
XLA Ops:
  0.6 2.0 %add_convert_fusion.buffer_ref = bf16[512,1024]{1,0:T(8,128)(2,1)S(1)} fusion(bf16[512,1024]{1,0:T(8,128)(2,1)} %param.4, bf16[512,1024]{1,0:T(8,128)(2,1)} %param.3), kind=kLoop, calls=%fused_computation.1 | loop fusion | flops 2097152 | bytes 3145728 | tf_op jit(solution)/shard_map/convert_element_type | solution.py:151
  3.1 21.0 %all_to_all.30 = f32[32,16,256]{2,1,0:T(8,128)S(1)} all-to-all(f32[32,16,256]{2,1,0:T(8,128)S(1)} %bitcast.14), channel_id=1, replica_groups=mesh['row'=16,'col'=8,'rep'=4] {'col','rep'}, dimensions={0} | all-to-all | bytes 1048576 | tf_op jit(solution)/shard_map/all_to_all | solution.py:102
  24.2 0.9 broadcast_in_dim.6
  25.0 4.4 %all-to-all-start.1 = ((f32[32,16,256]{2,1,0:T(8,128)}), f32[32,16,256]{2,1,0:T(8,128)S(1)}, u32[]{:S(2)}, u32[]{:S(2)}) async-start(f32[32,16,256]{2,1,0:T(8,128)} %broadcast_in_dim.6), calls=%async_computation.1 | async-start | bytes 1048576 | tf_op jit(solution)/shard_map/all_to_all | solution.py:106
  29.4 11.4 %all-to-all-done.1 = f32[32,16,256]{2,1,0:T(8,128)S(1)} async-done(((f32[32,16,256]{2,1,0:T(8,128)}), f32[32,16,256]{2,1,0:T(8,128)S(1)}, u32[]{:S(2)}, u32[]{:S(2)}) %all-to-all-start.1) | async-done | bytes 524320 | tf_op jit(solution)/shard_map/all_to_all | solution.py:106
  40.8 0.6 fusion.2
  41.4 0.7 broadcast_in_dim.7
  42.1 13.7 %all-to-all-start.2 = ((f32[16,8,256]{2,1,0:T(8,128)}), f32[16,8,256]{2,1,0:T(8,128)S(1)}, u32[]{:S(2)}, u32[]{:S(2)}) async-start(f32[16,8,256]{2,1,0:T(8,128)} %broadcast_in_dim.7), calls=%async_computation.2 | async-start | bytes 262144 | tf_op jit(solution)/shard_map/all_to_all | solution.py:106
  55.8 2.0 %project.1 = f32[4,256,256]{2,1,0:T(8,128)} custom-call(bf16[512,1024]{1,0:T(8,128)(2,1)S(1)} %add_convert_fusion.buffer_ref, f32[512,256]{1,0:T(8,128)S(1)} %bitcast.12), custom_call_target="tpu_custom_call" | custom-call | flops 805306368 | bytes 3000000 | tf_op jit(solution)/shard_map/project/pallas_call | solution.py:132
  57.8 10.1 %all-to-all-done.2 = f32[16,8,256]{2,1,0:T(8,128)S(1)} async-done(((f32[16,8,256]{2,1,0:T(8,128)}), f32[16,8,256]{2,1,0:T(8,128)S(1)}, u32[]{:S(2)}, u32[]{:S(2)}) %all-to-all-start.2) | async-done | bytes 131104 | tf_op jit(solution)/shard_map/all_to_all | solution.py:106
  67.9 4.3 %all-to-all-start.3 = ((f32[4,256,256]{2,1,0:T(8,128)}), f32[4,256,256]{2,1,0:T(8,128)S(1)}, u32[]{:S(2)}, u32[]{:S(2)}) async-start(f32[4,256,256]{2,1,0:T(8,128)} %project.1), calls=%async_computation.3 | async-start | bytes 2097152 | tf_op jit(solution)/shard_map/all_to_all | solution.py:163
  72.2 9.3 %all_gather.12 = f32[32,256]{1,0:T(8,128)S(1)} all-gather(f32[8,256]{1,0:T(8,128)S(1)} %reduce_sum.55), channel_id=1, replica_groups=mesh['row'=16,'col'=8,'rep'=4] {'rep'}, dimensions={0}, use_global_device_ids=true | all-gather | bytes 40960 | tf_op jit(solution)/shard_map/all_gather | solution.py:164
  81.5 7.0 %all_gather.13 = f32[64,256]{1,0:T(8,128)S(1)} all-gather(f32[32,256]{1,0:T(8,128)S(1)} %all_gather.12), channel_id=1, replica_groups={{0,4},{8,12},{16,20},{24,28},{1,5},{9,13},{17,21},{25,29},{2,6},{10,14}..., dimensions={0}, use_global_device_ids=true | all-gather | bytes 98304 | tf_op jit(solution)/shard_map/all_gather | solution.py:165
  88.4 10.1 %all_gather.14.gram_ref = f32[256,256]{1,0:T(8,128)} all-gather(f32[64,256]{1,0:T(8,128)S(1)} %all_gather.13), channel_id=1, replica_groups={{0,8,16,24},{4,12,20,28},{1,9,17,25},{5,13,21,29},{2,10,18,26},{6,14,22..., dimensions={0}, use_global_device_ids=true | all-gather | bytes 327680 | tf_op jit(solution)/shard_map/all_gather | solution.py:168
  98.6 0.8 reduce_sum.56
  99.4 4.4 %all-to-all-start.4 = ((f32[4,64,256]{2,1,0:T(8,128)}), f32[4,64,256]{2,1,0:T(8,128)S(1)}, u32[]{:S(2)}, u32[]{:S(2)}) async-start(f32[4,64,256]{2,1,0:T(8,128)} %bitcast.2), calls=%async_computation.4 | async-start | bytes 524288 | tf_op jit(solution)/shard_map/all_to_all | solution.py:174
  103.8 10.8 %inverse_factor.1 = f32[256,256]{1,0:T(8,128)} custom-call(f32[256,256]{1,0:T(8,128)} %all_gather.14.gram_ref), custom_call_target="tpu_custom_call" | custom-call | flops 400000000 | bytes 524288 | tf_op jit(solution)/shard_map/inverse_factor/pallas_call | solution.py:89
  114.5 1.6 fusion.6
  116.2 2.6 %all-to-all-done.4 = f32[4,64,256]{2,1,0:T(8,128)S(1)} async-done(((f32[4,64,256]{2,1,0:T(8,128)}), f32[4,64,256]{2,1,0:T(8,128)S(1)}, u32[]{:S(2)}, u32[]{:S(2)}) %all-to-all-start.4) | async-done | bytes 262176 | tf_op jit(solution)/shard_map/all_to_all | solution.py:174
  119.2 28.1 %all_gather.15 = bf16[1024,256]{1,0:T(8,128)(2,1)S(1)} all-gather(bf16[64,256]{1,0:T(8,128)(2,1)S(1)} %convolution_convert_fusion), channel_id=1, replica_groups=mesh['row'=16,'col'=8,'rep'=4] {'row'}, dimensions={0}, use_global_device_ids=true | all-gather | bytes 557056 | tf_op jit(solution)/shard_map/all_gather | solution.py:181
  148.2 12.8 %all-to-all-start.5 = ((f32[32,1,256]{2,1,0:T(1,128)}), f32[32,1,256]{2,1,0:T(1,128)S(1)}, u32[]{:S(2)}, u32[]{:S(2)}) async-start(f32[32,1,256]{2,1,0:T(1,128)} %broadcast_in_dim.8), calls=%async_computation.5 | async-start | bytes 65536 | tf_op jit(solution)/shard_map/all_to_all | solution.py:106
  161.0 1.4 subtract_convert_fusion
  162.4 5.8 %all-to-all-done.5 = f32[32,1,256]{2,1,0:T(1,128)S(1)} async-done(((f32[32,1,256]{2,1,0:T(1,128)}), f32[32,1,256]{2,1,0:T(1,128)S(1)}, u32[]{:S(2)}, u32[]{:S(2)}) %all-to-all-start.5) | async-done | bytes 32800 | tf_op jit(solution)/shard_map/all_to_all | solution.py:106
  168.3 1.1 convert_divide_fusion
  (16 shorter events, 1.8 us)
Async XLA Ops:
  0.6 2.0 %copy-start = (bf16[1024,256]{1,0:T(8,128)(2,1)S(1)}, bf16[1024,256]{1,0:T(8,128)(2,1)}, u32[]{:S(2)}) copy-start(bf16[1024,256]{1,0:T(8,128)(2,1)} %param.5) | copy-start | bytes 1572868
  25.0 15.7 %all-to-all-start.1 = ((f32[32,16,256]{2,1,0:T(8,128)}), f32[32,16,256]{2,1,0:T(8,128)S(1)}, u32[]{:S(2)}, u32[]{:S(2)}) async-start(f32[32,16,256]{2,1,0:T(8,128)} %broadcast_in_dim.6), calls=%async_computation.1 | async-start | bytes 1048576 | tf_op jit(solution)/shard_map/all_to_all | solution.py:106
  42.1 25.7 %all-to-all-start.2 = ((f32[16,8,256]{2,1,0:T(8,128)}), f32[16,8,256]{2,1,0:T(8,128)S(1)}, u32[]{:S(2)}, u32[]{:S(2)}) async-start(f32[16,8,256]{2,1,0:T(8,128)} %broadcast_in_dim.7), calls=%async_computation.2 | async-start | bytes 262144 | tf_op jit(solution)/shard_map/all_to_all | solution.py:106
  67.9 30.7 %all-to-all-start.3 = ((f32[4,256,256]{2,1,0:T(8,128)}), f32[4,256,256]{2,1,0:T(8,128)S(1)}, u32[]{:S(2)}, u32[]{:S(2)}) async-start(f32[4,256,256]{2,1,0:T(8,128)} %project.1), calls=%async_computation.3 | async-start | bytes 2097152 | tf_op jit(solution)/shard_map/all_to_all | solution.py:163
  99.4 19.4 %all-to-all-start.4 = ((f32[4,64,256]{2,1,0:T(8,128)}), f32[4,64,256]{2,1,0:T(8,128)S(1)}, u32[]{:S(2)}, u32[]{:S(2)}) async-start(f32[4,64,256]{2,1,0:T(8,128)} %bitcast.2), calls=%async_computation.4 | async-start | bytes 524288 | tf_op jit(solution)/shard_map/all_to_all | solution.py:174
  114.5 4.3 %copy-start.2 = (f32[256,256]{1,0:T(8,128)S(1)}, f32[256,256]{1,0:T(8,128)}, u32[]{:S(2)}) copy-start(f32[256,256]{1,0:T(8,128)} %inverse_factor.1) | copy-start | bytes 786436
  116.2 46.3 %copy-start.1 = (f32[512,256]{1,0:T(8,128)}, f32[512,256]{1,0:T(8,128)S(1)}, u32[]{:S(2)}) copy-start(f32[512,256]{1,0:T(8,128)S(1)} %fusion.6) | copy-start | bytes 1572868
  148.2 20.0 %all-to-all-start.5 = ((f32[32,1,256]{2,1,0:T(1,128)}), f32[32,1,256]{2,1,0:T(1,128)S(1)}, u32[]{:S(2)}, u32[]{:S(2)}) async-start(f32[32,1,256]{2,1,0:T(1,128)} %broadcast_in_dim.8), calls=%async_computation.5 | async-start | bytes 65536 | tf_op jit(solution)/shard_map/all_to_all | solution.py:106

commit v5 on v4

--- a/solution.py
+++ b/solution.py
@@ -8,6 +8,7 @@
 RANK = 256
 BLOCK = 64
 SPAN = 64
+NEAR = 4
 WIDE = ("col", "rep")
 
 
@@ -108,46 +109,48 @@
     )
 
 
-def project_kernel(buffer_ref, left_ref, out_ref):
+def project_kernel(near_ref, buffer_ref, left_ref, *refs):
+    out_refs, part_ref = refs[:-1], refs[-1]
     left = left_ref[...]
     high = left.astype(jnp.bfloat16)
     rest = left - high.astype(jnp.float32)
     middle = rest.astype(jnp.bfloat16)
     low = (rest - middle.astype(jnp.float32)).astype(jnp.bfloat16)
-    far, near = buffer_ref.shape[1] // SPAN // out_ref.shape[0], out_ref.shape[0]
-    for i in range(far):
-        block = buffer_ref[:, i * near * SPAN : (i + 1) * near * SPAN]
-        part = sum(
+    own = near_ref[0]
+    for i in range(buffer_ref.shape[1] // RANK):
+        block = buffer_ref[:, i * RANK : (i + 1) * RANK]
+        part_ref[i] = sum(
             lax.dot_general(
                 block, piece, (((0,), (0,)), ((), ())), preferred_element_type=jnp.float32
             )
             for piece in (low, middle, high)
         )
-        for j in range(near):
-            out_ref[j, i * SPAN : (i + 1) * SPAN, :] = part[j * SPAN : (j + 1) * SPAN, :]
-
-
-def project(buffer, left_raw, near):
+        for shift in range(NEAR):
+            start = pl.multiple_of(lax.rem(own + shift, NEAR) * SPAN, SPAN)
+            out_refs[shift][i * SPAN : (i + 1) * SPAN, :] = part_ref[i, pl.ds(start, SPAN), :]
+
+
+def project(buffer, left_raw, own):
     columns = buffer.shape[1]
     return pl.pallas_call(
         project_kernel,
-        out_shape=jax.ShapeDtypeStruct((near, columns // near, RANK), jnp.float32),
-        in_specs=[pl.BlockSpec(memory_space=pltpu.VMEM)] * 2,
-        out_specs=pl.BlockSpec(memory_space=pltpu.VMEM),
+        out_shape=[jax.ShapeDtypeStruct((columns // NEAR, RANK), jnp.float32)] * NEAR,
+        in_specs=[pl.BlockSpec(memory_space=pltpu.SMEM)]
+        + [pl.BlockSpec(memory_space=pltpu.VMEM)] * 2,
+        out_specs=[pl.BlockSpec(memory_space=pltpu.VMEM)] * NEAR,
+        scratch_shapes=[pltpu.VMEM((columns // RANK, RANK, RANK), jnp.float32)],
         compiler_params=pltpu.CompilerParams(vmem_limit_bytes=32 * 1024 * 1024),
         cost_estimate=pl.CostEstimate(
             flops=6 * buffer.size * RANK, bytes_accessed=3_000_000, transcendentals=0
         ),
         name="project",
-    )(buffer, left_raw)
+    )(own.reshape(1), buffer, left_raw)
 
 
 def local(wide, tall, momentum, gradient, right_prev):
     place = lax.axis_index(WIDE)
-    near = 4
-    far = tall // near
-    adjacent = [[i * near + j for j in range(near)] for i in range(far)]
-    strided = [[i * near + j for i in range(far)] for j in range(near)]
+    far = tall // NEAR
+    strided = [[i * NEAR + j for i in range(far)] for j in range(NEAR)]
     buffer = (momentum.astype(jnp.float32) + gradient.astype(jnp.float32)).astype(jnp.bfloat16)
     left_partial = jnp.dot(buffer, right_prev, preferred_element_type=jnp.float32)
     rows = left_partial.shape[0]
@@ -157,18 +160,14 @@
     share = RANK // wide
     own = lax.dynamic_slice(left_raw, (0, place * share), (rows, share))
     gram_rows = jnp.sum(gather(dot32(own, left_raw, 0, 0), "row", tall), axis=0)
-    blocks = project(buffer, left_raw, near)
-
-    gram_rows, blocks = lax.optimization_barrier((gram_rows, blocks))
-    blocks = lax.all_to_all(blocks, "row", 0, 0, axis_index_groups=adjacent, tiled=True)
-    gram_matrix = lax.all_gather(gram_rows, "rep", axis=0, tiled=True)
-    gram_matrix = lax.all_gather(
-        gram_matrix, "col", axis=0, axis_index_groups=[[0, 1], [2, 3], [4, 5], [6, 7]], tiled=True
-    )
-    gram_matrix = lax.all_gather(
-        gram_matrix, "col", axis=0, axis_index_groups=[[0, 2, 4, 6], [1, 3, 5, 7]], tiled=True
-    )
-    blocks = jnp.sum(blocks, axis=0).reshape(far, SPAN, RANK)
+    blocks = project(buffer, left_raw, lax.rem(lax.axis_index("row"), NEAR))
+
+    gram_rows, *blocks = lax.optimization_barrier((gram_rows, *blocks))
+    for shift in range(1, NEAR):
+        ring = [(i, i // NEAR * NEAR + (i + shift) % NEAR) for i in range(tall)]
+        blocks[shift] = lax.ppermute(blocks[shift], "row", ring)
+    gram_matrix = gather(gram_rows, WIDE, wide).reshape(RANK, RANK)
+    blocks = sum(blocks).reshape(far, SPAN, RANK)
 
     gram_matrix, blocks = lax.optimization_barrier((gram_matrix, blocks))
     blocks = lax.all_to_all(blocks, "row", 0, 0, axis_index_groups=strided, tiled=True)

time: 170 us -> 168 us (0.988)
  blocking collectives: 75.5 us -> 53.3 us
  starting transfers between devices: 39.5 us -> 51.6 us
  waiting for transfers between devices: 29.8 us -> 36.6 us
    all_gather x3 -> x0, blocking collectives: 26.4 us -> none  [the longest x1 10.1 us: local(): lax.all_gather(gram_matrix, 'col', axis=0, axis_index_groups=[[0, 2, 4, 6...]
    ppermute x0 -> x3, starting transfers between devices: none -> 10.4 us  [local(): blocks[shift] = lax.ppermute(blocks[shift], 'row', ring)]
    all_to_all x3 -> x4, starting transfers between devices: 30.8 us -> 37.1 us  [gather(): lax.all_to_all(jnp.broadcast_to(x[None], (count,) + x.shape), axes, 0, 0,...]
    all_to_all x1 -> x0, starting transfers between devices: 4.33 us -> none  [local(): lax.all_to_all(blocks, 'row', 0, 0, axis_index_groups=adjacent, tiled=True)]
    ppermute x0 -> x3, waiting for transfers between devices: none -> 4.19 us  [local(): blocks[shift] = lax.ppermute(blocks[shift], 'row', ring)]
    all_gather x1, blocking collectives: 28.1 us -> 32.3 us  [local(): right_low = lax.all_gather(right_rows, 'row', axis=0, tiled=True)]
    all_to_all x3 -> x4, waiting for transfers between devices: 27.2 us -> 31.1 us  [gather(): lax.all_to_all(jnp.broadcast_to(x[None], (count,) + x.shape), axes, 0, 0,...]
    add x0 -> x1, other arithmetic: none -> 1.8 us  [local(): blocks = sum(blocks).reshape(far, SPAN, RANK)]
  transfers between devices with their start and end apart: 5 -> 8, of which waited for: 4 -> 6; matrix products, arithmetic and copies ran while one was open for 2% -> 3% of each run, Pallas kernels for 8% -> 7%
where the time goes in v5:
time: 168 us; the launch traced here: 167 us
  blocking collectives  53.3 us (32%)
  starting transfers between devices  51.6 us (31%)
  waiting for transfers between devices  36.6 us (22%)
  Pallas kernels  11.9 us (7%)
  other arithmetic  5.16 us (3%)
  matrix products  4.54 us (3%)
  local copies, waits for them, and re-layouts  2.91 us (2%)
    all_to_all x4, starting transfers between devices, gather(): lax.all_to_all(jnp.broadcast_to(x[None], (count,) + x.shape), axes, 0, 0,...  37.1 us
    all_gather x1, blocking collectives, local(): right_low = lax.all_gather(right_rows, 'row', axis=0, tiled=True)  32.3 us
    all_to_all x4, waiting for transfers between devices, gather(): lax.all_to_all(jnp.broadcast_to(x[None], (count,) + x.shape), axes, 0, 0,...  31.1 us
    all_to_all x1, blocking collectives, scatter_sum(): return jnp.sum(lax.all_to_all(parts, axes, 0, 0, tiled=True), axis=0)  21 us
    pallas_call x1, Pallas kernels, inverse_factor(): pl.pallas_call(inverse_factor_kernel, out_shape=jax.ShapeDtypeStruct((RAN...  10.8 us
    ppermute x3, starting transfers between devices, local(): blocks[shift] = lax.ppermute(blocks[shift], 'row', ring)  10.4 us
    ppermute x3, waiting for transfers between devices, local(): blocks[shift] = lax.ppermute(blocks[shift], 'row', ring)  4.19 us
    all_to_all x1, starting transfers between devices, local(): lax.all_to_all(blocks, 'row', 0, 0, axis_index_groups=strided, tiled=True)  4.15 us
  transfers between devices with their start and end apart: 8, of which 6 were waited for; matrix products, arithmetic and copies ran while one was open for 3% of the time, Pallas kernels for 7%

profile of v5, /device:TPU:1, one launch (start us, length us, event | category | flops | bytes accessed | tf_op | source)
XLA Modules:
  0.0 166.9 jit_solution(13151050094040749080)
XLA Ops:
  0.6 2.0 %add_convert_fusion.buffer_ref = bf16[512,1024]{1,0:T(8,128)(2,1)S(1)} fusion(bf16[512,1024]{1,0:T(8,128)(2,1)} %param.4, bf16[512,1024]{1,0:T(8,128)(2,1)} %param.3), kind=kLoop, calls=%fused_computation.1 | loop fusion | flops 2097152 | bytes 3145728 | tf_op jit(solution)/shard_map/convert_element_type | solution.py:154
  3.1 21.0 %all_to_all.30 = f32[32,16,256]{2,1,0:T(8,128)S(1)} all-to-all(f32[32,16,256]{2,1,0:T(8,128)S(1)} %bitcast.16), channel_id=1, replica_groups=mesh['row'=16,'col'=8,'rep'=4] {'col','rep'}, dimensions={0} | all-to-all | bytes 1048576 | tf_op jit(solution)/shard_map/all_to_all | solution.py:103
  24.2 0.9 broadcast_in_dim.8
  25.0 4.4 %all-to-all-start.1 = ((f32[32,16,256]{2,1,0:T(8,128)}), f32[32,16,256]{2,1,0:T(8,128)S(1)}, u32[]{:S(2)}, u32[]{:S(2)}) async-start(f32[32,16,256]{2,1,0:T(8,128)} %broadcast_in_dim.8), calls=%async_computation.1 | async-start | bytes 1048576 | tf_op jit(solution)/shard_map/all_to_all | solution.py:107
  29.4 11.4 %all-to-all-done.1 = f32[32,16,256]{2,1,0:T(8,128)S(1)} async-done(((f32[32,16,256]{2,1,0:T(8,128)}), f32[32,16,256]{2,1,0:T(8,128)S(1)}, u32[]{:S(2)}, u32[]{:S(2)}) %all-to-all-start.1) | async-done | bytes 524320 | tf_op jit(solution)/shard_map/all_to_all | solution.py:107
  42.1 13.7 %all-to-all-start.2 = ((f32[16,8,256]{2,1,0:T(8,128)}), f32[16,8,256]{2,1,0:T(8,128)S(1)}, u32[]{:S(2)}, u32[]{:S(2)}) async-start(f32[16,8,256]{2,1,0:T(8,128)} %broadcast_in_dim.9), calls=%async_computation.2 | async-start | bytes 262144 | tf_op jit(solution)/shard_map/all_to_all | solution.py:107
  55.8 1.1 project.1
  56.9 10.9 %all-to-all-done.2 = f32[16,8,256]{2,1,0:T(8,128)S(1)} async-done(((f32[16,8,256]{2,1,0:T(8,128)}), f32[16,8,256]{2,1,0:T(8,128)S(1)}, u32[]{:S(2)}, u32[]{:S(2)}) %all-to-all-start.2) | async-done | bytes 131104 | tf_op jit(solution)/shard_map/all_to_all | solution.py:107
  67.9 3.8 %collective-permute-start = (f32[256,256]{1,0:T(8,128)S(1)}, f32[256,256]{1,0:T(8,128)S(1)}, u32[]{:S(2)}, u32[]{:S(2)}) collective-permute-start(f32[256,256]{1,0:T(8,128)S(1)} %get-tuple-element.20), channel_id=1, source_target_pairs={{0,32},{32,64},{64,96},{96,0},{128,160},{160,192},{192,224},{224,1... | collective-permute-start | bytes 786440 | tf_op jit(solution)/shard_map/ppermute | solution.py:168
  71.7 3.3 %collective-permute-start.1 = (f32[256,256]{1,0:T(8,128)S(1)}, f32[256,256]{1,0:T(8,128)}, u32[]{:S(2)}, u32[]{:S(2)}) collective-permute-start(f32[256,256]{1,0:T(8,128)S(1)} %get-tuple-element.21), channel_id=1, source_target_pairs={{0,64},{32,96},{64,0},{96,32},{128,192},{160,224},{192,128},{224,1... | collective-permute-start | bytes 786440 | tf_op jit(solution)/shard_map/ppermute | solution.py:168
  75.0 3.2 %collective-permute-start.2 = (f32[256,256]{1,0:T(8,128)S(1)}, f32[256,256]{1,0:T(8,128)}, u32[]{:S(2)}, u32[]{:S(2)}) collective-permute-start(f32[256,256]{1,0:T(8,128)S(1)} %get-tuple-element.22), channel_id=1, source_target_pairs={{0,96},{32,0},{64,32},{96,64},{128,224},{160,128},{192,160},{224,1... | collective-permute-start | bytes 786440 | tf_op jit(solution)/shard_map/ppermute | solution.py:168
  79.0 7.7 %all-to-all-start.3 = ((f32[32,8,256]{2,1,0:T(8,128)}), f32[32,8,256]{2,1,0:T(8,128)}, u32[]{:S(2)}, u32[]{:S(2)}) async-start(f32[32,8,256]{2,1,0:T(8,128)} %broadcast_in_dim.10), calls=%async_computation.3 | async-start | bytes 524288 | tf_op jit(solution)/shard_map/all_to_all | solution.py:107
  86.7 4.2 %collective-permute-done.1 = f32[256,256]{1,0:T(8,128)} collective-permute-done((f32[256,256]{1,0:T(8,128)S(1)}, f32[256,256]{1,0:T(8,128)}, u32[]{:S(2)}, u32[]{:S(2)}) %collective-permute-start.1) | collective-permute-done | bytes 262176 | tf_op jit(solution)/shard_map/ppermute | solution.py:168
  90.9 1.8 %add_add_fusion = f32[256,256]{1,0:T(8,128)} fusion(f32[256,256]{1,0:T(8,128)} %collective-permute-done.2, f32[256,256]{1,0:T(8,128)} %collective-permute-done.1, f32[256,256]{1,0:T(8,128)S(1)} %get-tuple-element.19, f32[256,256]{1,0:T(8,128)S(1)} %collective-permute-done), kind=kLoop, calls=%fused_computation.7 | loop fusion | flops 196608 | bytes 1310720 | tf_op jit(solution)/shard_map/add | solution.py:170
  92.7 3.0 %all-to-all-done.3 = f32[32,8,256]{2,1,0:T(8,128)} async-done(((f32[32,8,256]{2,1,0:T(8,128)}), f32[32,8,256]{2,1,0:T(8,128)}, u32[]{:S(2)}, u32[]{:S(2)}) %all-to-all-start.3) | async-done | bytes 262176 | tf_op jit(solution)/shard_map/all_to_all | solution.py:107
  95.7 4.2 %all-to-all-start.4 = ((f32[4,64,256]{2,1,0:T(8,128)}), f32[4,64,256]{2,1,0:T(8,128)S(1)}, u32[]{:S(2)}, u32[]{:S(2)}) async-start(f32[4,64,256]{2,1,0:T(8,128)} %bitcast.4), calls=%async_computation.4 | async-start | bytes 524288 | tf_op jit(solution)/shard_map/all_to_all | solution.py:173
  99.9 10.8 %inverse_factor.1 = f32[256,256]{1,0:T(8,128)} custom-call(f32[256,256]{1,0:T(8,128)} %bitcast.3.gram_ref), custom_call_target="tpu_custom_call" | custom-call | flops 400000000 | bytes 524288 | tf_op jit(solution)/shard_map/inverse_factor/pallas_call | solution.py:90
  110.7 1.6 fusion.6
  112.3 1.3 all-to-all-done.4
  114.0 32.3 %all_gather.3 = bf16[1024,256]{1,0:T(8,128)(2,1)S(1)} all-gather(bf16[64,256]{1,0:T(8,128)(2,1)S(1)} %convolution_convert_fusion), channel_id=1, replica_groups=mesh['row'=16,'col'=8,'rep'=4] {'row'}, dimensions={0}, use_global_device_ids=true | all-gather | bytes 557056 | tf_op jit(solution)/shard_map/all_gather | solution.py:180
  147.2 11.4 %all-to-all-start.5 = ((f32[32,1,256]{2,1,0:T(1,128)}), f32[32,1,256]{2,1,0:T(1,128)S(1)}, u32[]{:S(2)}, u32[]{:S(2)}) async-start(f32[32,1,256]{2,1,0:T(1,128)} %broadcast_in_dim.11), calls=%async_computation.5 | async-start | bytes 65536 | tf_op jit(solution)/shard_map/all_to_all | solution.py:107
  158.5 1.4 subtract_convert_fusion
  160.0 5.8 %all-to-all-done.5 = f32[32,1,256]{2,1,0:T(1,128)S(1)} async-done(((f32[32,1,256]{2,1,0:T(1,128)}), f32[32,1,256]{2,1,0:T(1,128)S(1)}, u32[]{:S(2)}, u32[]{:S(2)}) %all-to-all-start.5) | async-done | bytes 32800 | tf_op jit(solution)/shard_map/all_to_all | solution.py:107
  165.8 1.1 convert_divide_fusion
  (20 shorter events, 3.8 us)
Async XLA Ops:
  0.6 2.0 %copy-start = (bf16[1024,256]{1,0:T(8,128)(2,1)S(1)}, bf16[1024,256]{1,0:T(8,128)(2,1)}, u32[]{:S(2)}) copy-start(bf16[1024,256]{1,0:T(8,128)(2,1)} %param.5) | copy-start | bytes 1572868
  25.0 15.7 %all-to-all-start.1 = ((f32[32,16,256]{2,1,0:T(8,128)}), f32[32,16,256]{2,1,0:T(8,128)S(1)}, u32[]{:S(2)}, u32[]{:S(2)}) async-start(f32[32,16,256]{2,1,0:T(8,128)} %broadcast_in_dim.8), calls=%async_computation.1 | async-start | bytes 1048576 | tf_op jit(solution)/shard_map/all_to_all | solution.py:107
  42.1 25.7 %all-to-all-start.2 = ((f32[16,8,256]{2,1,0:T(8,128)}), f32[16,8,256]{2,1,0:T(8,128)S(1)}, u32[]{:S(2)}, u32[]{:S(2)}) async-start(f32[16,8,256]{2,1,0:T(8,128)} %broadcast_in_dim.9), calls=%async_computation.2 | async-start | bytes 262144 | tf_op jit(solution)/shard_map/all_to_all | solution.py:107
  67.9 18.8 %collective-permute-start = (f32[256,256]{1,0:T(8,128)S(1)}, f32[256,256]{1,0:T(8,128)S(1)}, u32[]{:S(2)}, u32[]{:S(2)}) collective-permute-start(f32[256,256]{1,0:T(8,128)S(1)} %get-tuple-element.20), channel_id=1, source_target_pairs={{0,32},{32,64},{64,96},{96,0},{128,160},{160,192},{192,224},{224,1... | collective-permute-start | bytes 786440 | tf_op jit(solution)/shard_map/ppermute | solution.py:168
  71.7 19.2 %collective-permute-start.1 = (f32[256,256]{1,0:T(8,128)S(1)}, f32[256,256]{1,0:T(8,128)}, u32[]{:S(2)}, u32[]{:S(2)}) collective-permute-start(f32[256,256]{1,0:T(8,128)S(1)} %get-tuple-element.21), channel_id=1, source_target_pairs={{0,64},{32,96},{64,0},{96,32},{128,192},{160,224},{192,128},{224,1... | collective-permute-start | bytes 786440 | tf_op jit(solution)/shard_map/ppermute | solution.py:168
  75.0 15.9 %collective-permute-start.2 = (f32[256,256]{1,0:T(8,128)S(1)}, f32[256,256]{1,0:T(8,128)}, u32[]{:S(2)}, u32[]{:S(2)}) collective-permute-start(f32[256,256]{1,0:T(8,128)S(1)} %get-tuple-element.22), channel_id=1, source_target_pairs={{0,96},{32,0},{64,32},{96,64},{128,224},{160,128},{192,160},{224,1... | collective-permute-start | bytes 786440 | tf_op jit(solution)/shard_map/ppermute | solution.py:168
  79.0 16.7 %all-to-all-start.3 = ((f32[32,8,256]{2,1,0:T(8,128)}), f32[32,8,256]{2,1,0:T(8,128)}, u32[]{:S(2)}, u32[]{:S(2)}) async-start(f32[32,8,256]{2,1,0:T(8,128)} %broadcast_in_dim.10), calls=%async_computation.3 | async-start | bytes 524288 | tf_op jit(solution)/shard_map/all_to_all | solution.py:107
  95.7 17.9 %all-to-all-start.4 = ((f32[4,64,256]{2,1,0:T(8,128)}), f32[4,64,256]{2,1,0:T(8,128)S(1)}, u32[]{:S(2)}, u32[]{:S(2)}) async-start(f32[4,64,256]{2,1,0:T(8,128)} %bitcast.4), calls=%async_computation.4 | async-start | bytes 524288 | tf_op jit(solution)/shard_map/all_to_all | solution.py:173
  110.6 3.0 %copy-start.2 = (f32[256,256]{1,0:T(8,128)S(1)}, f32[256,256]{1,0:T(8,128)}, u32[]{:S(2)}) copy-start(f32[256,256]{1,0:T(8,128)} %inverse_factor.1) | copy-start | bytes 786436
  112.3 47.7 %copy-start.1 = (f32[512,256]{1,0:T(8,128)}, f32[512,256]{1,0:T(8,128)S(1)}, u32[]{:S(2)}) copy-start(f32[512,256]{1,0:T(8,128)S(1)} %fusion.6) | copy-start | bytes 1572868
  147.2 18.6 %all-to-all-start.5 = ((f32[32,1,256]{2,1,0:T(1,128)}), f32[32,1,256]{2,1,0:T(1,128)S(1)}, u32[]{:S(2)}, u32[]{:S(2)}) async-start(f32[32,1,256]{2,1,0:T(1,128)} %broadcast_in_dim.11), calls=%async_computation.5 | async-start | bytes 65536 | tf_op jit(solution)/shard_map/all_to_all | solution.py:107

commit v6 on v5

--- a/solution.py
+++ b/solution.py
@@ -7,7 +7,6 @@
 
 RANK = 256
 BLOCK = 64
-SPAN = 64
 NEAR = 4
 WIDE = ("col", "rep")
 
@@ -109,25 +108,23 @@
     )
 
 
-def project_kernel(near_ref, buffer_ref, left_ref, *refs):
-    out_refs, part_ref = refs[:-1], refs[-1]
+def project_kernel(near_ref, buffer_ref, left_ref, *out_refs):
     left = left_ref[...]
     high = left.astype(jnp.bfloat16)
     rest = left - high.astype(jnp.float32)
     middle = rest.astype(jnp.bfloat16)
     low = (rest - middle.astype(jnp.float32)).astype(jnp.bfloat16)
-    own = near_ref[0]
-    for i in range(buffer_ref.shape[1] // RANK):
-        block = buffer_ref[:, i * RANK : (i + 1) * RANK]
-        part_ref[i] = sum(
+    count = len(out_refs)
+    span = buffer_ref.shape[1] // count
+    for shift in range(count):
+        start = pl.multiple_of(lax.rem(near_ref[0] + shift, count) * span, span)
+        block = buffer_ref[:, pl.ds(start, span)]
+        out_refs[shift][...] = sum(
             lax.dot_general(
                 block, piece, (((0,), (0,)), ((), ())), preferred_element_type=jnp.float32
             )
             for piece in (low, middle, high)
         )
-        for shift in range(NEAR):
-            start = pl.multiple_of(lax.rem(own + shift, NEAR) * SPAN, SPAN)
-            out_refs[shift][i * SPAN : (i + 1) * SPAN, :] = part_ref[i, pl.ds(start, SPAN), :]
 
 
 def project(buffer, left_raw, own):
@@ -138,7 +135,6 @@
         in_specs=[pl.BlockSpec(memory_space=pltpu.SMEM)]
         + [pl.BlockSpec(memory_space=pltpu.VMEM)] * 2,
         out_specs=[pl.BlockSpec(memory_space=pltpu.VMEM)] * NEAR,
-        scratch_shapes=[pltpu.VMEM((columns // RANK, RANK, RANK), jnp.float32)],
         compiler_params=pltpu.CompilerParams(vmem_limit_bytes=32 * 1024 * 1024),
         cost_estimate=pl.CostEstimate(
             flops=6 * buffer.size * RANK, bytes_accessed=3_000_000, transcendentals=0
@@ -150,6 +146,7 @@
 def local(wide, tall, momentum, gradient, right_prev):
     place = lax.axis_index(WIDE)
     far = tall // NEAR
+    adjacent = [[i * NEAR + j for j in range(NEAR)] for i in range(far)]
     strided = [[i * NEAR + j for i in range(far)] for j in range(NEAR)]
     buffer = (momentum.astype(jnp.float32) + gradient.astype(jnp.float32)).astype(jnp.bfloat16)
     left_partial = jnp.dot(buffer, right_prev, preferred_element_type=jnp.float32)
@@ -163,21 +160,27 @@
     blocks = project(buffer, left_raw, lax.rem(lax.axis_index("row"), NEAR))
 
     gram_rows, *blocks = lax.optimization_barrier((gram_rows, *blocks))
+    gram_matrix = gather(gram_rows, WIDE, wide).reshape(RANK, RANK)
     for shift in range(1, NEAR):
         ring = [(i, i // NEAR * NEAR + (i + shift) % NEAR) for i in range(tall)]
         blocks[shift] = lax.ppermute(blocks[shift], "row", ring)
-    gram_matrix = gather(gram_rows, WIDE, wide).reshape(RANK, RANK)
-    blocks = sum(blocks).reshape(far, SPAN, RANK)
-
-    gram_matrix, blocks = lax.optimization_barrier((gram_matrix, blocks))
-    blocks = lax.all_to_all(blocks, "row", 0, 0, axis_index_groups=strided, tiled=True)
     inverse = inverse_factor(gram_matrix)
-    right_raw = jnp.sum(blocks, axis=0)
 
     left_factor = dot32(left_raw, inverse, 1, 1)
     left_low = left_factor.astype(jnp.bfloat16)
-    right_rows = dot32(right_raw, inverse, 1, 1).astype(jnp.bfloat16)
-    right_low = lax.all_gather(right_rows, "row", axis=0, tiled=True)
+    part = dot32(sum(blocks), inverse, 1, 1).astype(jnp.bfloat16)
+    parts = lax.all_to_all(
+        jnp.broadcast_to(part[None], (far,) + part.shape),
+        "row",
+        0,
+        0,
+        axis_index_groups=strided,
+        tiled=True,
+    )
+    right_rows = jnp.sum(parts.astype(jnp.float32), axis=0).astype(jnp.bfloat16)
+    right_low = lax.all_gather(
+        right_rows, "row", axis=0, axis_index_groups=adjacent, tiled=True
+    )
     right_wide = right_low.astype(jnp.float32)
     own_sums = jnp.sum(right_wide * right_wide, axis=0, keepdims=True)
     column_sums = jnp.sum(gather(own_sums, WIDE, wide), axis=0)

time: 168 us -> 174 us (1.036)
  waiting for transfers between devices: 36.6 us -> 62.3 us
  blocking collectives: 53.3 us -> 36.7 us
  starting transfers between devices: 51.6 us -> 49 us
    all_to_all x1, waiting for transfers between devices: 1.33 us -> 26.9 us  [local(): lax.all_to_all(jnp.broadcast_to(part[None], (far,) + part.shape), 'row',...]
    all_gather x1, blocking collectives: 32.3 us -> 15.7 us  [local(): lax.all_gather(right_rows, 'row', axis=0, axis_index_groups=adjacent, til...]
    ppermute x3, waiting for transfers between devices: 4.19 us -> 7 us  [local(): blocks[shift] = lax.ppermute(blocks[shift], 'row', ring)]
    all_to_all x4, waiting for transfers between devices: 31.1 us -> 28.4 us  [gather(): lax.all_to_all(jnp.broadcast_to(x[None], (count,) + x.shape), axes, 0, 0,...]
    add x1 -> x0, other arithmetic: 1.8 us -> none  [local(): blocks = sum(blocks).reshape(far, SPAN, RANK)]
  transfers between devices with their start and end apart: 8 -> 8, of which waited for: 6 -> 6; matrix products, arithmetic and copies ran while one was open for 3% -> 1% of each run, Pallas kernels for 7% -> 7%
where the time goes in v6:
time: 174 us; the launch traced here: 173 us
  waiting for transfers between devices  62.3 us (36%)
  starting transfers between devices  49 us (28%)
  blocking collectives  36.7 us (21%)
  Pallas kernels  11.8 us (7%)
  matrix products  4.76 us (3%)
  local copies, waits for them, and re-layouts  4.44 us (3%)
  other arithmetic  3.43 us (2%)
    all_to_all x4, starting transfers between devices, gather(): lax.all_to_all(jnp.broadcast_to(x[None], (count,) + x.shape), axes, 0, 0,...  36.8 us
    all_to_all x4, waiting for transfers between devices, gather(): lax.all_to_all(jnp.broadcast_to(x[None], (count,) + x.shape), axes, 0, 0,...  28.4 us
    all_to_all x1, waiting for transfers between devices, local(): lax.all_to_all(jnp.broadcast_to(part[None], (far,) + part.shape), 'row',...  26.9 us
    all_to_all x1, blocking collectives, scatter_sum(): return jnp.sum(lax.all_to_all(parts, axes, 0, 0, tiled=True), axis=0)  21 us
    all_gather x1, blocking collectives, local(): lax.all_gather(right_rows, 'row', axis=0, axis_index_groups=adjacent, til...  15.7 us
    pallas_call x1, Pallas kernels, inverse_factor(): pl.pallas_call(inverse_factor_kernel, out_shape=jax.ShapeDtypeStruct((RAN...  10.8 us
    ppermute x3, starting transfers between devices, local(): blocks[shift] = lax.ppermute(blocks[shift], 'row', ring)  8.69 us
    ppermute x3, waiting for transfers between devices, local(): blocks[shift] = lax.ppermute(blocks[shift], 'row', ring)  7 us
  transfers between devices with their start and end apart: 8, of which 6 were waited for; matrix products, arithmetic and copies ran while one was open for 1% of the time, Pallas kernels for 7%

profile of v6, /device:TPU:1, one launch (start us, length us, event | category | flops | bytes accessed | tf_op | source)
XLA Modules:
  0.0 173.3 jit_solution(7308528225467532341)
XLA Ops:
  0.6 2.0 %add_convert_fusion.buffer_ref = bf16[512,1024]{1,0:T(8,128)(2,1)S(1)} fusion(bf16[512,1024]{1,0:T(8,128)(2,1)} %param.4, bf16[512,1024]{1,0:T(8,128)(2,1)} %param.3), kind=kLoop, calls=%fused_computation.1 | loop fusion | flops 2097152 | bytes 3145728 | tf_op jit(solution)/shard_map/convert_element_type | solution.py:151
  3.1 21.0 %all_to_all.30 = f32[32,16,256]{2,1,0:T(8,128)S(1)} all-to-all(f32[32,16,256]{2,1,0:T(8,128)S(1)} %bitcast.14), channel_id=1, replica_groups=mesh['row'=16,'col'=8,'rep'=4] {'col','rep'}, dimensions={0} | all-to-all | bytes 1048576 | tf_op jit(solution)/shard_map/all_to_all | solution.py:102
  24.2 0.9 broadcast_in_dim.10
  25.0 4.4 %all-to-all-start.1 = ((f32[32,16,256]{2,1,0:T(8,128)}), f32[32,16,256]{2,1,0:T(8,128)S(1)}, u32[]{:S(2)}, u32[]{:S(2)}) async-start(f32[32,16,256]{2,1,0:T(8,128)} %broadcast_in_dim.10), calls=%async_computation.1 | async-start | bytes 1048576 | tf_op jit(solution)/shard_map/all_to_all | solution.py:106
  29.4 11.4 %all-to-all-done.1 = f32[32,16,256]{2,1,0:T(8,128)S(1)} async-done(((f32[32,16,256]{2,1,0:T(8,128)}), f32[32,16,256]{2,1,0:T(8,128)S(1)}, u32[]{:S(2)}, u32[]{:S(2)}) %all-to-all-start.1) | async-done | bytes 524320 | tf_op jit(solution)/shard_map/all_to_all | solution.py:106
  42.1 13.7 %all-to-all-start.2 = ((f32[16,8,256]{2,1,0:T(8,128)}), f32[16,8,256]{2,1,0:T(8,128)S(1)}, u32[]{:S(2)}, u32[]{:S(2)}) async-start(f32[16,8,256]{2,1,0:T(8,128)} %broadcast_in_dim.11), calls=%async_computation.2 | async-start | bytes 262144 | tf_op jit(solution)/shard_map/all_to_all | solution.py:106
  55.8 1.1 project.1
  56.8 11.0 %all-to-all-done.2 = f32[16,8,256]{2,1,0:T(8,128)S(1)} async-done(((f32[16,8,256]{2,1,0:T(8,128)}), f32[16,8,256]{2,1,0:T(8,128)S(1)}, u32[]{:S(2)}, u32[]{:S(2)}) %all-to-all-start.2) | async-done | bytes 131104 | tf_op jit(solution)/shard_map/all_to_all | solution.py:106
  67.9 0.7 broadcast_in_dim.12
  68.6 7.2 %all-to-all-start.3 = ((f32[32,8,256]{2,1,0:T(8,128)}), f32[32,8,256]{2,1,0:T(8,128)S(1)}, u32[]{:S(2)}, u32[]{:S(2)}) async-start(f32[32,8,256]{2,1,0:T(8,128)} %broadcast_in_dim.12), calls=%async_computation.3 | async-start | bytes 524288 | tf_op jit(solution)/shard_map/all_to_all | solution.py:106
  75.8 3.6 %collective-permute-start.2 = (f32[256,256]{1,0:T(8,128)S(1)}, f32[256,256]{1,0:T(8,128)}, u32[]{:S(2)}, u32[]{:S(2)}) collective-permute-start(f32[256,256]{1,0:T(8,128)S(1)} %get-tuple-element.20), channel_id=1, source_target_pairs={{0,96},{32,0},{64,32},{96,64},{128,224},{160,128},{192,160},{224,1... | collective-permute-start | bytes 786440 | tf_op jit(solution)/shard_map/ppermute | solution.py:166
  79.4 2.7 %collective-permute-start.1 = (f32[256,256]{1,0:T(8,128)S(1)}, f32[256,256]{1,0:T(8,128)}, u32[]{:S(2)}, u32[]{:S(2)}) collective-permute-start(f32[256,256]{1,0:T(8,128)S(1)} %get-tuple-element.19), channel_id=1, source_target_pairs={{0,64},{32,96},{64,0},{96,32},{128,192},{160,224},{192,128},{224,1... | collective-permute-start | bytes 786440 | tf_op jit(solution)/shard_map/ppermute | solution.py:166
  82.1 2.4 %collective-permute-start = (f32[256,256]{1,0:T(8,128)S(1)}, f32[256,256]{1,0:T(8,128)}, u32[]{:S(2)}, u32[]{:S(2)}) collective-permute-start(f32[256,256]{1,0:T(8,128)S(1)} %get-tuple-element.18), channel_id=1, source_target_pairs={{0,32},{32,64},{64,96},{96,0},{128,160},{160,192},{192,224},{224,1... | collective-permute-start | bytes 786440 | tf_op jit(solution)/shard_map/ppermute | solution.py:166
  85.5 10.8 %inverse_factor.1 = f32[256,256]{1,0:T(8,128)} custom-call(f32[256,256]{1,0:T(8,128)} %bitcast.15), custom_call_target="tpu_custom_call" | custom-call | flops 400000000 | bytes 524288 | tf_op jit(solution)/shard_map/inverse_factor/pallas_call | solution.py:89
  96.2 7.0 %collective-permute-done.1 = f32[256,256]{1,0:T(8,128)} collective-permute-done((f32[256,256]{1,0:T(8,128)S(1)}, f32[256,256]{1,0:T(8,128)}, u32[]{:S(2)}, u32[]{:S(2)}) %collective-permute-start.1) | collective-permute-done | bytes 262176 | tf_op jit(solution)/shard_map/ppermute | solution.py:166
  103.2 1.6 convolution_convert_fusion
  104.8 0.8 broadcast_in_dim.13
  105.7 3.5 %all-to-all-start.4 = ((bf16[4,256,256]{2,1,0:T(8,128)(2,1)}), bf16[4,256,256]{2,1,0:T(8,128)(2,1)S(1)}, u32[]{:S(2)}, u32[]{:S(2)}) async-start(bf16[4,256,256]{2,1,0:T(8,128)(2,1)} %broadcast_in_dim.13), calls=%async_computation.4 | async-start | bytes 1048576 | tf_op jit(solution)/shard_map/all_to_all | solution.py:172
  109.8 26.9 %all-to-all-done.4 = bf16[4,256,256]{2,1,0:T(8,128)(2,1)S(1)} async-done(((bf16[4,256,256]{2,1,0:T(8,128)(2,1)}), bf16[4,256,256]{2,1,0:T(8,128)(2,1)S(1)}, u32[]{:S(2)}, u32[]{:S(2)}) %all-to-all-start.4) | async-done | bytes 524320 | tf_op jit(solution)/shard_map/all_to_all | solution.py:172
  136.8 15.7 %all_gather.3 = bf16[1024,256]{1,0:T(8,128)(2,1)S(1)} all-gather(bf16[256,256]{1,0:T(8,128)(2,1)S(1)} %reduce_sum.50), channel_id=1, replica_groups={{0,32,64,96},{128,160,192,224},{256,288,320,352},{384,416,448,480},{1,3..., dimensions={0}, use_global_device_ids=true | all-gather | bytes 655360 | tf_op jit(solution)/shard_map/all_gather | solution.py:181
  153.3 11.6 %all-to-all-start.5 = ((f32[32,1,256]{2,1,0:T(1,128)}), f32[32,1,256]{2,1,0:T(1,128)S(1)}, u32[]{:S(2)}, u32[]{:S(2)}) async-start(f32[32,1,256]{2,1,0:T(1,128)} %broadcast_in_dim.14), calls=%async_computation.5 | async-start | bytes 65536 | tf_op jit(solution)/shard_map/all_to_all | solution.py:106
  164.9 1.4 subtract_convert_fusion
  166.4 5.8 %all-to-all-done.5 = f32[32,1,256]{2,1,0:T(1,128)S(1)} async-done(((f32[32,1,256]{2,1,0:T(1,128)}), f32[32,1,256]{2,1,0:T(1,128)S(1)}, u32[]{:S(2)}, u32[]{:S(2)}) %all-to-all-start.5) | async-done | bytes 32800 | tf_op jit(solution)/shard_map/all_to_all | solution.py:106
  172.2 1.1 convert_divide_fusion
  (22 shorter events, 4.4 us)
Async XLA Ops:
  0.6 2.0 %copy-start = (bf16[1024,256]{1,0:T(8,128)(2,1)S(1)}, bf16[1024,256]{1,0:T(8,128)(2,1)}, u32[]{:S(2)}) copy-start(bf16[1024,256]{1,0:T(8,128)(2,1)} %param.5) | copy-start | bytes 1572868
  25.0 15.7 %all-to-all-start.1 = ((f32[32,16,256]{2,1,0:T(8,128)}), f32[32,16,256]{2,1,0:T(8,128)S(1)}, u32[]{:S(2)}, u32[]{:S(2)}) async-start(f32[32,16,256]{2,1,0:T(8,128)} %broadcast_in_dim.10), calls=%async_computation.1 | async-start | bytes 1048576 | tf_op jit(solution)/shard_map/all_to_all | solution.py:106
  42.1 25.7 %all-to-all-start.2 = ((f32[16,8,256]{2,1,0:T(8,128)}), f32[16,8,256]{2,1,0:T(8,128)S(1)}, u32[]{:S(2)}, u32[]{:S(2)}) async-start(f32[16,8,256]{2,1,0:T(8,128)} %broadcast_in_dim.11), calls=%async_computation.2 | async-start | bytes 262144 | tf_op jit(solution)/shard_map/all_to_all | solution.py:106
  68.6 16.2 %all-to-all-start.3 = ((f32[32,8,256]{2,1,0:T(8,128)}), f32[32,8,256]{2,1,0:T(8,128)S(1)}, u32[]{:S(2)}, u32[]{:S(2)}) async-start(f32[32,8,256]{2,1,0:T(8,128)} %broadcast_in_dim.12), calls=%async_computation.3 | async-start | bytes 524288 | tf_op jit(solution)/shard_map/all_to_all | solution.py:106
  75.8 20.5 %collective-permute-start.2 = (f32[256,256]{1,0:T(8,128)S(1)}, f32[256,256]{1,0:T(8,128)}, u32[]{:S(2)}, u32[]{:S(2)}) collective-permute-start(f32[256,256]{1,0:T(8,128)S(1)} %get-tuple-element.20), channel_id=1, source_target_pairs={{0,96},{32,0},{64,32},{96,64},{128,224},{160,128},{192,160},{224,1... | collective-permute-start | bytes 786440 | tf_op jit(solution)/shard_map/ppermute | solution.py:166
  79.4 23.9 %collective-permute-start.1 = (f32[256,256]{1,0:T(8,128)S(1)}, f32[256,256]{1,0:T(8,128)}, u32[]{:S(2)}, u32[]{:S(2)}) collective-permute-start(f32[256,256]{1,0:T(8,128)S(1)} %get-tuple-element.19), channel_id=1, source_target_pairs={{0,64},{32,96},{64,0},{96,32},{128,192},{160,224},{192,128},{224,1... | collective-permute-start | bytes 786440 | tf_op jit(solution)/shard_map/ppermute | solution.py:166
  82.1 21.1 %collective-permute-start = (f32[256,256]{1,0:T(8,128)S(1)}, f32[256,256]{1,0:T(8,128)}, u32[]{:S(2)}, u32[]{:S(2)}) collective-permute-start(f32[256,256]{1,0:T(8,128)S(1)} %get-tuple-element.18), channel_id=1, source_target_pairs={{0,32},{32,64},{64,96},{96,0},{128,160},{160,192},{192,224},{224,1... | collective-permute-start | bytes 786440 | tf_op jit(solution)/shard_map/ppermute | solution.py:166
  84.8 0.7 copy-start.3
  104.8 4.3 %copy-start.2 = (f32[256,256]{1,0:T(8,128)S(1)}, f32[256,256]{1,0:T(8,128)}, u32[]{:S(2)}) copy-start(f32[256,256]{1,0:T(8,128)} %inverse_factor.1) | copy-start | bytes 786436
  105.7 31.0 %all-to-all-start.4 = ((bf16[4,256,256]{2,1,0:T(8,128)(2,1)}), bf16[4,256,256]{2,1,0:T(8,128)(2,1)S(1)}, u32[]{:S(2)}, u32[]{:S(2)}) async-start(bf16[4,256,256]{2,1,0:T(8,128)(2,1)} %broadcast_in_dim.13), calls=%async_computation.4 | async-start | bytes 1048576 | tf_op jit(solution)/shard_map/all_to_all | solution.py:172
  109.8 56.6 %copy-start.1 = (f32[512,256]{1,0:T(8,128)}, f32[512,256]{1,0:T(8,128)S(1)}, u32[]{:S(2)}) copy-start(f32[512,256]{1,0:T(8,128)S(1)} %fusion.9) | copy-start | bytes 1572868
  153.3 18.9 %all-to-all-start.5 = ((f32[32,1,256]{2,1,0:T(1,128)}), f32[32,1,256]{2,1,0:T(1,128)S(1)}, u32[]{:S(2)}, u32[]{:S(2)}) async-start(f32[32,1,256]{2,1,0:T(1,128)} %broadcast_in_dim.14), calls=%async_computation.5 | async-start | bytes 65536 | tf_op jit(solution)/shard_map/all_to_all | solution.py:106

commit v7 on v5

--- a/solution.py
+++ b/solution.py
@@ -160,9 +160,8 @@
     share = RANK // wide
     own = lax.dynamic_slice(left_raw, (0, place * share), (rows, share))
     gram_rows = jnp.sum(gather(dot32(own, left_raw, 0, 0), "row", tall), axis=0)
-    blocks = project(buffer, left_raw, lax.rem(lax.axis_index("row"), NEAR))
-
-    gram_rows, *blocks = lax.optimization_barrier((gram_rows, *blocks))
+    blocks = list(project(buffer, left_raw, lax.rem(lax.axis_index("row"), NEAR)))
+
     for shift in range(1, NEAR):
         ring = [(i, i // NEAR * NEAR + (i + shift) % NEAR) for i in range(tall)]
         blocks[shift] = lax.ppermute(blocks[shift], "row", ring)

time: 168 us -> 162 us (0.964)
  waiting for transfers between devices: 36.6 us -> 25.9 us
  starting transfers between devices: 51.6 us -> 55.9 us
    all_to_all x4, waiting for transfers between devices: 31.1 us -> 18.7 us  [gather(): lax.all_to_all(jnp.broadcast_to(x[None], (count,) + x.shape), axes, 0, 0,...]
    all_to_all x1, starting transfers between devices: 4.15 us -> 7.79 us  [local(): lax.all_to_all(blocks, 'row', 0, 0, axis_index_groups=strided, tiled=True)]
    ppermute x3, waiting for transfers between devices: 4.19 us -> 6.35 us  [local(): blocks[shift] = lax.ppermute(blocks[shift], 'row', ring)]
where the time goes in v7:
time: 162 us; the launch traced here: 161 us
  starting transfers between devices  55.9 us (35%)
  blocking collectives  53.9 us (33%)
  waiting for transfers between devices  25.9 us (16%)
  Pallas kernels  11.9 us (7%)
  other arithmetic  5.16 us (3%)
  matrix products  4.54 us (3%)
  local copies, waits for them, and re-layouts  2.91 us (2%)
    all_to_all x4, starting transfers between devices, gather(): lax.all_to_all(jnp.broadcast_to(x[None], (count,) + x.shape), axes, 0, 0,...  37.7 us
    all_gather x1, blocking collectives, local(): right_low = lax.all_gather(right_rows, 'row', axis=0, tiled=True)  32.9 us
    all_to_all x1, blocking collectives, scatter_sum(): return jnp.sum(lax.all_to_all(parts, axes, 0, 0, tiled=True), axis=0)  21 us
    all_to_all x4, waiting for transfers between devices, gather(): lax.all_to_all(jnp.broadcast_to(x[None], (count,) + x.shape), axes, 0, 0,...  18.7 us
    pallas_call x1, Pallas kernels, inverse_factor(): pl.pallas_call(inverse_factor_kernel, out_shape=jax.ShapeDtypeStruct((RAN...  10.8 us
    ppermute x3, starting transfers between devices, local(): blocks[shift] = lax.ppermute(blocks[shift], 'row', ring)  10.3 us
    all_to_all x1, starting transfers between devices, local(): lax.all_to_all(blocks, 'row', 0, 0, axis_index_groups=strided, tiled=True)  7.79 us
    ppermute x3, waiting for transfers between devices, local(): blocks[shift] = lax.ppermute(blocks[shift], 'row', ring)  6.35 us
  transfers between devices with their start and end apart: 8, of which 6 were waited for; matrix products, arithmetic and copies ran while one was open for 3% of the time, Pallas kernels for 7%

profile of v7, /device:TPU:1, one launch (start us, length us, event | category | flops | bytes accessed | tf_op | source)
XLA Modules:
  0.0 160.9 jit_solution(895579203618098024)
XLA Ops:
  0.6 2.0 %add_convert_fusion.buffer_ref = bf16[512,1024]{1,0:T(8,128)(2,1)S(1)} fusion(bf16[512,1024]{1,0:T(8,128)(2,1)} %param.4, bf16[512,1024]{1,0:T(8,128)(2,1)} %param.3), kind=kLoop, calls=%fused_computation.1 | loop fusion | flops 2097152 | bytes 3145728 | tf_op jit(solution)/shard_map/convert_element_type | solution.py:154
  3.1 21.0 %all_to_all.30 = f32[32,16,256]{2,1,0:T(8,128)S(1)} all-to-all(f32[32,16,256]{2,1,0:T(8,128)S(1)} %bitcast.16), channel_id=1, replica_groups=mesh['row'=16,'col'=8,'rep'=4] {'col','rep'}, dimensions={0} | all-to-all | bytes 1048576 | tf_op jit(solution)/shard_map/all_to_all | solution.py:103
  24.2 0.9 broadcast_in_dim.8
  25.0 4.4 %all-to-all-start.1 = ((f32[32,16,256]{2,1,0:T(8,128)}), f32[32,16,256]{2,1,0:T(8,128)S(1)}, u32[]{:S(2)}, u32[]{:S(2)}) async-start(f32[32,16,256]{2,1,0:T(8,128)} %broadcast_in_dim.8), calls=%async_computation.1 | async-start | bytes 1048576 | tf_op jit(solution)/shard_map/all_to_all | solution.py:107
  29.4 11.4 %all-to-all-done.1 = f32[32,16,256]{2,1,0:T(8,128)S(1)} async-done(((f32[32,16,256]{2,1,0:T(8,128)}), f32[32,16,256]{2,1,0:T(8,128)S(1)}, u32[]{:S(2)}, u32[]{:S(2)}) %all-to-all-start.1) | async-done | bytes 524320 | tf_op jit(solution)/shard_map/all_to_all | solution.py:107
  42.1 13.7 %all-to-all-start.2 = ((f32[16,8,256]{2,1,0:T(8,128)}), f32[16,8,256]{2,1,0:T(8,128)S(1)}, u32[]{:S(2)}, u32[]{:S(2)}) async-start(f32[16,8,256]{2,1,0:T(8,128)} %broadcast_in_dim.9), calls=%async_computation.2 | async-start | bytes 262144 | tf_op jit(solution)/shard_map/all_to_all | solution.py:107
  55.8 1.1 project.1
  56.9 3.3 %collective-permute-start = (f32[256,256]{1,0:T(8,128)S(1)}, f32[256,256]{1,0:T(8,128)S(1)}, u32[]{:S(2)}, u32[]{:S(2)}) collective-permute-start(f32[256,256]{1,0:T(8,128)S(1)} %get-tuple-element.10), channel_id=1, source_target_pairs={{0,32},{32,64},{64,96},{96,0},{128,160},{160,192},{192,224},{224,1... | collective-permute-start | bytes 786440 | tf_op jit(solution)/shard_map/ppermute | solution.py:167
  60.2 4.0 %collective-permute-start.1 = (f32[256,256]{1,0:T(8,128)S(1)}, f32[256,256]{1,0:T(8,128)}, u32[]{:S(2)}, u32[]{:S(2)}) collective-permute-start(f32[256,256]{1,0:T(8,128)S(1)} %get-tuple-element.11), channel_id=1, source_target_pairs={{0,64},{32,96},{64,0},{96,32},{128,192},{160,224},{192,128},{224,1... | collective-permute-start | bytes 786440 | tf_op jit(solution)/shard_map/ppermute | solution.py:167
  64.2 3.1 %collective-permute-start.2 = (f32[256,256]{1,0:T(8,128)S(1)}, f32[256,256]{1,0:T(8,128)}, u32[]{:S(2)}, u32[]{:S(2)}) collective-permute-start(f32[256,256]{1,0:T(8,128)S(1)} %get-tuple-element.12), channel_id=1, source_target_pairs={{0,96},{32,0},{64,32},{96,64},{128,224},{160,128},{192,160},{224,1... | collective-permute-start | bytes 786440 | tf_op jit(solution)/shard_map/ppermute | solution.py:167
  67.9 0.7 broadcast_in_dim.10
  68.6 8.0 %all-to-all-start.3 = ((f32[32,8,256]{2,1,0:T(8,128)}), f32[32,8,256]{2,1,0:T(8,128)}, u32[]{:S(2)}, u32[]{:S(2)}) async-start(f32[32,8,256]{2,1,0:T(8,128)} %broadcast_in_dim.10), calls=%async_computation.3 | async-start | bytes 524288 | tf_op jit(solution)/shard_map/all_to_all | solution.py:107
  76.6 6.3 %collective-permute-done.1 = f32[256,256]{1,0:T(8,128)} collective-permute-done((f32[256,256]{1,0:T(8,128)S(1)}, f32[256,256]{1,0:T(8,128)}, u32[]{:S(2)}, u32[]{:S(2)}) %collective-permute-start.1) | collective-permute-done | bytes 262176 | tf_op jit(solution)/shard_map/ppermute | solution.py:167
  83.0 1.8 %add_add_fusion = f32[256,256]{1,0:T(8,128)} fusion(f32[256,256]{1,0:T(8,128)} %collective-permute-done.2, f32[256,256]{1,0:T(8,128)} %collective-permute-done.1, f32[256,256]{1,0:T(8,128)S(1)} %get-tuple-element.9, f32[256,256]{1,0:T(8,128)S(1)} %collective-permute-done), kind=kLoop, calls=%fused_computation.7 | loop fusion | flops 196608 | bytes 1310720 | tf_op jit(solution)/shard_map/add | solution.py:169
  84.8 0.9 all-to-all-done.3
  85.7 7.8 %all-to-all-start.4 = ((f32[4,64,256]{2,1,0:T(8,128)}), f32[4,64,256]{2,1,0:T(8,128)S(1)}, u32[]{:S(2)}, u32[]{:S(2)}) async-start(f32[4,64,256]{2,1,0:T(8,128)} %bitcast.4), calls=%async_computation.4 | async-start | bytes 524288 | tf_op jit(solution)/shard_map/all_to_all | solution.py:172
  93.5 10.8 %inverse_factor.1 = f32[256,256]{1,0:T(8,128)} custom-call(f32[256,256]{1,0:T(8,128)} %bitcast.2.gram_ref), custom_call_target="tpu_custom_call" | custom-call | flops 400000000 | bytes 524288 | tf_op jit(solution)/shard_map/inverse_factor/pallas_call | solution.py:90
  104.2 1.6 %fusion.6 = f32[512,256]{1,0:T(8,128)S(1)} fusion(f32[512,256]{1,0:T(8,128)S(1)} %bitcast.15, f32[256,256]{1,0:T(8,128)} %inverse_factor.1), kind=kOutput, calls=%fused_computation.13 | convolution fusion | flops 402653184 | bytes 1310720 | tf_op jit(solution)/shard_map/dot_general | solution.py:16
  105.9 0.9 all-to-all-done.4
  107.1 32.9 %all_gather.3 = bf16[1024,256]{1,0:T(8,128)(2,1)S(1)} all-gather(bf16[64,256]{1,0:T(8,128)(2,1)S(1)} %convolution_convert_fusion), channel_id=1, replica_groups=mesh['row'=16,'col'=8,'rep'=4] {'row'}, dimensions={0}, use_global_device_ids=true | all-gather | bytes 557056 | tf_op jit(solution)/shard_map/all_gather | solution.py:179
  140.8 11.7 %all-to-all-start.5 = ((f32[32,1,256]{2,1,0:T(1,128)}), f32[32,1,256]{2,1,0:T(1,128)S(1)}, u32[]{:S(2)}, u32[]{:S(2)}) async-start(f32[32,1,256]{2,1,0:T(1,128)} %broadcast_in_dim.11), calls=%async_computation.5 | async-start | bytes 65536 | tf_op jit(solution)/shard_map/all_to_all | solution.py:107
  152.5 1.4 subtract_convert_fusion
  153.9 5.9 %all-to-all-done.5 = f32[32,1,256]{2,1,0:T(1,128)S(1)} async-done(((f32[32,1,256]{2,1,0:T(1,128)}), f32[32,1,256]{2,1,0:T(1,128)S(1)}, u32[]{:S(2)}, u32[]{:S(2)}) %all-to-all-start.5) | async-done | bytes 32800 | tf_op jit(solution)/shard_map/all_to_all | solution.py:107
  159.9 1.1 convert_divide_fusion
  (20 shorter events, 3.7 us)
Async XLA Ops:
  0.6 2.0 %copy-start = (bf16[1024,256]{1,0:T(8,128)(2,1)S(1)}, bf16[1024,256]{1,0:T(8,128)(2,1)}, u32[]{:S(2)}) copy-start(bf16[1024,256]{1,0:T(8,128)(2,1)} %param.5) | copy-start | bytes 1572868
  25.0 15.7 %all-to-all-start.1 = ((f32[32,16,256]{2,1,0:T(8,128)}), f32[32,16,256]{2,1,0:T(8,128)S(1)}, u32[]{:S(2)}, u32[]{:S(2)}) async-start(f32[32,16,256]{2,1,0:T(8,128)} %broadcast_in_dim.8), calls=%async_computation.1 | async-start | bytes 1048576 | tf_op jit(solution)/shard_map/all_to_all | solution.py:107
  42.1 25.8 %all-to-all-start.2 = ((f32[16,8,256]{2,1,0:T(8,128)}), f32[16,8,256]{2,1,0:T(8,128)S(1)}, u32[]{:S(2)}, u32[]{:S(2)}) async-start(f32[16,8,256]{2,1,0:T(8,128)} %broadcast_in_dim.9), calls=%async_computation.2 | async-start | bytes 262144 | tf_op jit(solution)/shard_map/all_to_all | solution.py:107
  56.9 19.7 %collective-permute-start = (f32[256,256]{1,0:T(8,128)S(1)}, f32[256,256]{1,0:T(8,128)S(1)}, u32[]{:S(2)}, u32[]{:S(2)}) collective-permute-start(f32[256,256]{1,0:T(8,128)S(1)} %get-tuple-element.10), channel_id=1, source_target_pairs={{0,32},{32,64},{64,96},{96,0},{128,160},{160,192},{192,224},{224,1... | collective-permute-start | bytes 786440 | tf_op jit(solution)/shard_map/ppermute | solution.py:167
  60.2 22.8 %collective-permute-start.1 = (f32[256,256]{1,0:T(8,128)S(1)}, f32[256,256]{1,0:T(8,128)}, u32[]{:S(2)}, u32[]{:S(2)}) collective-permute-start(f32[256,256]{1,0:T(8,128)S(1)} %get-tuple-element.11), channel_id=1, source_target_pairs={{0,64},{32,96},{64,0},{96,32},{128,192},{160,224},{192,128},{224,1... | collective-permute-start | bytes 786440 | tf_op jit(solution)/shard_map/ppermute | solution.py:167
  64.2 18.8 %collective-permute-start.2 = (f32[256,256]{1,0:T(8,128)S(1)}, f32[256,256]{1,0:T(8,128)}, u32[]{:S(2)}, u32[]{:S(2)}) collective-permute-start(f32[256,256]{1,0:T(8,128)S(1)} %get-tuple-element.12), channel_id=1, source_target_pairs={{0,96},{32,0},{64,32},{96,64},{128,224},{160,128},{192,160},{224,1... | collective-permute-start | bytes 786440 | tf_op jit(solution)/shard_map/ppermute | solution.py:167
  68.6 17.1 %all-to-all-start.3 = ((f32[32,8,256]{2,1,0:T(8,128)}), f32[32,8,256]{2,1,0:T(8,128)}, u32[]{:S(2)}, u32[]{:S(2)}) async-start(f32[32,8,256]{2,1,0:T(8,128)} %broadcast_in_dim.10), calls=%async_computation.3 | async-start | bytes 524288 | tf_op jit(solution)/shard_map/all_to_all | solution.py:107
  85.7 21.1 %all-to-all-start.4 = ((f32[4,64,256]{2,1,0:T(8,128)}), f32[4,64,256]{2,1,0:T(8,128)S(1)}, u32[]{:S(2)}, u32[]{:S(2)}) async-start(f32[4,64,256]{2,1,0:T(8,128)} %bitcast.4), calls=%async_computation.4 | async-start | bytes 524288 | tf_op jit(solution)/shard_map/all_to_all | solution.py:172
  104.2 2.5 %copy-start.2 = (f32[256,256]{1,0:T(8,128)S(1)}, f32[256,256]{1,0:T(8,128)}, u32[]{:S(2)}) copy-start(f32[256,256]{1,0:T(8,128)} %inverse_factor.1) | copy-start | bytes 786436
  105.9 48.1 %copy-start.1 = (f32[512,256]{1,0:T(8,128)}, f32[512,256]{1,0:T(8,128)S(1)}, u32[]{:S(2)}) copy-start(f32[512,256]{1,0:T(8,128)S(1)} %fusion.6) | copy-start | bytes 1572868
  140.8 19.0 %all-to-all-start.5 = ((f32[32,1,256]{2,1,0:T(1,128)}), f32[32,1,256]{2,1,0:T(1,128)S(1)}, u32[]{:S(2)}, u32[]{:S(2)}) async-start(f32[32,1,256]{2,1,0:T(1,128)} %broadcast_in_dim.11), calls=%async_computation.5 | async-start | bytes 65536 | tf_op jit(solution)/shard_map/all_to_all | solution.py:107

commit v8 on v7

--- a/solution.py
+++ b/solution.py
@@ -98,6 +98,64 @@
     )(gram_matrix)
 
 
+def accumulate_kernel(momentum_ref, gradient_ref, right_ref, buffer_ref, left_ref, *scratch):
+    momentum, gradient, right, sems = scratch
+    count = sems.shape[0] - 1
+    rows = momentum.shape[0] // count
+    fetch_right = pltpu.make_async_copy(right_ref, right, sems.at[count, 0])
+    fetches = []
+    for i in range(count):
+        part = pl.ds(i * rows, rows)
+        fetches.append(
+            [
+                pltpu.make_async_copy(source.at[part], target.at[part], sems.at[i, j])
+                for j, (source, target) in enumerate(
+                    [(momentum_ref, momentum), (gradient_ref, gradient)]
+                )
+            ]
+        )
+    for fetch in fetches[0]:
+        fetch.start()
+    fetch_right.start()
+    for pair in fetches[1:]:
+        for fetch in pair:
+            fetch.start()
+    for i in range(count):
+        part = slice(i * rows, (i + 1) * rows)
+        for fetch in fetches[i]:
+            fetch.wait()
+        total = momentum[part, :].astype(jnp.float32) + gradient[part, :].astype(jnp.float32)
+        total = total.astype(jnp.bfloat16)
+        buffer_ref[part, :] = total
+        if i == 0:
+            fetch_right.wait()
+        left_ref[part, :] = jnp.dot(total, right[...], preferred_element_type=jnp.float32)
+
+
+def accumulate(momentum, gradient, right_prev):
+    rows, columns = momentum.shape
+    chunks = 4
+    return pl.pallas_call(
+        accumulate_kernel,
+        out_shape=[
+            jax.ShapeDtypeStruct((rows, columns), jnp.bfloat16),
+            jax.ShapeDtypeStruct((rows, RANK), jnp.float32),
+        ],
+        in_specs=[pl.BlockSpec(memory_space=pl.ANY)] * 3,
+        out_specs=[pl.BlockSpec(memory_space=pltpu.VMEM)] * 2,
+        scratch_shapes=[
+            pltpu.VMEM((rows, columns), jnp.bfloat16),
+            pltpu.VMEM((rows, columns), jnp.bfloat16),
+            pltpu.VMEM((columns, RANK), jnp.bfloat16),
+            pltpu.SemaphoreType.DMA((chunks + 1, 2)),
+        ],
+        cost_estimate=pl.CostEstimate(
+            flops=2 * rows * columns * RANK, bytes_accessed=4_000_000, transcendentals=0
+        ),
+        name="accumulate",
+    )(momentum, gradient, right_prev)
+
+
 def scatter_sum(x, axes, count):
     parts = x.reshape(count, x.shape[0] // count, x.shape[1])
     return jnp.sum(lax.all_to_all(parts, axes, 0, 0, tiled=True), axis=0)
@@ -147,12 +205,50 @@
     )(own.reshape(1), buffer, left_raw)
 
 
+def finish_kernel(left_ref, inverse_ref, right_ref, buffer_ref, factor_ref, next_ref):
+    factor = dot32(left_ref[...], inverse_ref[...], 1, 1)
+    factor_ref[...] = factor
+    outer = lax.dot_general(
+        factor.astype(jnp.bfloat16),
+        right_ref[...],
+        (((1,), (1,)), ((), ())),
+        preferred_element_type=jnp.float32,
+    )
+    next_ref[...] = (buffer_ref[...].astype(jnp.float32) - 0.1 * outer).astype(jnp.bfloat16)
+
+
+def finish(left_raw, inverse, right_low, buffer):
+    rows, columns = buffer.shape
+    tile = rows // 4
+    return pl.pallas_call(
+        finish_kernel,
+        out_shape=[
+            jax.ShapeDtypeStruct((rows, RANK), jnp.float32),
+            jax.ShapeDtypeStruct((rows, columns), jnp.bfloat16),
+        ],
+        grid=(rows // tile,),
+        in_specs=[
+            pl.BlockSpec((tile, RANK), lambda i: (i, 0)),
+            pl.BlockSpec((RANK, RANK), lambda i: (0, 0)),
+            pl.BlockSpec((columns, RANK), lambda i: (0, 0)),
+            pl.BlockSpec((tile, columns), lambda i: (i, 0)),
+        ],
+        out_specs=[
+            pl.BlockSpec((tile, RANK), lambda i: (i, 0)),
+            pl.BlockSpec((tile, columns), lambda i: (i, 0)),
+        ],
+        cost_estimate=pl.CostEstimate(
+            flops=2 * rows * columns * RANK, bytes_accessed=4_000_000, transcendentals=0
+        ),
+        name="finish",
+    )(left_raw, inverse, right_low, buffer)
+
+
 def local(wide, tall, momentum, gradient, right_prev):
     place = lax.axis_index(WIDE)
     far = tall // NEAR
     strided = [[i * NEAR + j for i in range(far)] for j in range(NEAR)]
-    buffer = (momentum.astype(jnp.float32) + gradient.astype(jnp.float32)).astype(jnp.bfloat16)
-    left_partial = jnp.dot(buffer, right_prev, preferred_element_type=jnp.float32)
+    buffer, left_partial = accumulate(momentum, gradient, right_prev)
     rows = left_partial.shape[0]
     left_rows = scatter_sum(left_partial, WIDE, wide)
     left_raw = gather(left_rows, WIDE, wide).reshape(rows, RANK)
@@ -166,24 +262,20 @@
         ring = [(i, i // NEAR * NEAR + (i + shift) % NEAR) for i in range(tall)]
         blocks[shift] = lax.ppermute(blocks[shift], "row", ring)
     gram_matrix = gather(gram_rows, WIDE, wide).reshape(RANK, RANK)
-    blocks = sum(blocks).reshape(far, SPAN, RANK)
+    early = lax.optimization_barrier(sum(blocks[:-1]))
+    blocks = (early + blocks[-1]).reshape(far, SPAN, RANK)
 
     gram_matrix, blocks = lax.optimization_barrier((gram_matrix, blocks))
     blocks = lax.all_to_all(blocks, "row", 0, 0, axis_index_groups=strided, tiled=True)
     inverse = inverse_factor(gram_matrix)
     right_raw = jnp.sum(blocks, axis=0)
 
-    left_factor = dot32(left_raw, inverse, 1, 1)
-    left_low = left_factor.astype(jnp.bfloat16)
     right_rows = dot32(right_raw, inverse, 1, 1).astype(jnp.bfloat16)
     right_low = lax.all_gather(right_rows, "row", axis=0, tiled=True)
     right_wide = right_low.astype(jnp.float32)
     own_sums = jnp.sum(right_wide * right_wide, axis=0, keepdims=True)
     column_sums = jnp.sum(gather(own_sums, WIDE, wide), axis=0)
-    outer = lax.dot_general(
-        left_low, right_low, (((1,), (1,)), ((), ())), preferred_element_type=jnp.float32
-    )
-    momentum_next = (buffer.astype(jnp.float32) - 0.1 * outer).astype(jnp.bfloat16)
+    left_factor, momentum_next = finish(left_raw, inverse, right_low, buffer)
     right_factor = right_wide / (jnp.sqrt(column_sums) + 1e-08)
     return (momentum_next, left_factor, right_factor)
 

time: 162 us -> 164 us (1.012)
  Pallas kernels: 11.9 us -> 21 us
  matrix products: 4.54 us -> 1.02 us
  other arithmetic: 5.16 us -> 3.2 us
  waiting for transfers between devices: 25.9 us -> 24.2 us
    pallas_call x0 -> x2, Pallas kernels: none -> 9.1 us  [the longest x1 5.71 us: finish(): pl.pallas_call(finish_kernel, out_shape=[jax.ShapeDtypeStruct((rows, RANK...]
    all_to_all x4, waiting for transfers between devices: 18.7 us -> 14.7 us  [gather(): lax.all_to_all(jnp.broadcast_to(x[None], (count,) + x.shape), axes, 0, 0,...]
    convert_element_type x1 -> x0, other arithmetic: 2 us -> none  [local(): (momentum.astype(jnp.float32) + gradient.astype(jnp.float32)).astype(jnp....]
    dot_general x2 -> x0, matrix products: 1.89 us -> none  [the longest x1 1.45 us: local(): lax.dot_general(left_low, right_low, (((1,), (1,)), ((), ())), preferred_...]
    all_to_all x1, waiting for transfers between devices: 0.86 us -> 2.59 us  [local(): lax.all_to_all(blocks, 'row', 0, 0, axis_index_groups=strided, tiled=True)]
  transfers between devices with their start and end apart: 8 -> 8, of which waited for: 6 -> 6; matrix products, arithmetic and copies ran while one was open for 3% -> 1% of each run, Pallas kernels for 7% -> 11%
where the time goes in v8:
time: 164 us; the launch traced here: 163 us
  blocking collectives  54.7 us (33%)
  starting transfers between devices  54.4 us (33%)
  waiting for transfers between devices  24.2 us (15%)
  Pallas kernels  21 us (13%)
  local copies, waits for them, and re-layouts  3.6 us (2%)
  other arithmetic  3.2 us (2%)
    all_to_all x4, starting transfers between devices, gather(): lax.all_to_all(jnp.broadcast_to(x[None], (count,) + x.shape), axes, 0, 0,...  36.5 us
    all_gather x1, blocking collectives, local(): right_low = lax.all_gather(right_rows, 'row', axis=0, tiled=True)  32.8 us
    all_to_all x1, blocking collectives, scatter_sum(): return jnp.sum(lax.all_to_all(parts, axes, 0, 0, tiled=True), axis=0)  21.9 us
    all_to_all x4, waiting for transfers between devices, gather(): lax.all_to_all(jnp.broadcast_to(x[None], (count,) + x.shape), axes, 0, 0,...  14.7 us
    pallas_call x1, Pallas kernels, inverse_factor(): pl.pallas_call(inverse_factor_kernel, out_shape=jax.ShapeDtypeStruct((RAN...  10.8 us
    ppermute x3, starting transfers between devices, local(): blocks[shift] = lax.ppermute(blocks[shift], 'row', ring)  10.3 us
    all_to_all x1, starting transfers between devices, local(): lax.all_to_all(blocks, 'row', 0, 0, axis_index_groups=strided, tiled=True)  7.48 us
    ppermute x3, waiting for transfers between devices, local(): blocks[shift] = lax.ppermute(blocks[shift], 'row', ring)  6.89 us
  transfers between devices with their start and end apart: 8, of which 6 were waited for; matrix products, arithmetic and copies ran while one was open for 1% of the time, Pallas kernels for 11%

profile of v8, /device:TPU:1, one launch (start us, length us, event | category | flops | bytes accessed | tf_op | source)
XLA Modules:
  0.0 162.8 jit_solution(818787933838624378)
XLA Ops:
  0.6 3.4 %accumulate.1 = (bf16[512,1024]{1,0:T(8,128)(2,1)}, f32[512,256]{1,0:T(8,128)}) custom-call(bf16[512,1024]{1,0:T(8,128)(2,1)} %momentum_ref.1, bf16[512,1024]{1,0:T(8,128)(2,1)} %gradient_ref.1, bf16[1024,256]{1,0:T(8,128)(2,1)} %right_ref.1), custom_call_target="tpu_custom_call" | custom-call | flops 268435456 | bytes 4000000 | tf_op jit(solution)/shard_map/accumulate/pallas_call | solution.py:138
  4.0 21.9 %all_to_all.30 = f32[32,16,256]{2,1,0:T(8,128)S(1)} all-to-all(f32[32,16,256]{2,1,0:T(8,128)} %bitcast.11), channel_id=1, replica_groups=mesh['row'=16,'col'=8,'rep'=4] {'col','rep'}, dimensions={0} | all-to-all | bytes 1048576 | tf_op jit(solution)/shard_map/all_to_all | solution.py:161
  26.0 0.9 broadcast_in_dim.8
  26.8 4.5 %all-to-all-start.1 = ((f32[32,16,256]{2,1,0:T(8,128)}), f32[32,16,256]{2,1,0:T(8,128)S(1)}, u32[]{:S(2)}, u32[]{:S(2)}) async-start(f32[32,16,256]{2,1,0:T(8,128)} %broadcast_in_dim.8), calls=%async_computation.1 | async-start | bytes 1048576 | tf_op jit(solution)/shard_map/all_to_all | solution.py:165
  31.3 11.4 %all-to-all-done.1 = f32[32,16,256]{2,1,0:T(8,128)S(1)} async-done(((f32[32,16,256]{2,1,0:T(8,128)}), f32[32,16,256]{2,1,0:T(8,128)S(1)}, u32[]{:S(2)}, u32[]{:S(2)}) %all-to-all-start.1) | async-done | bytes 524320 | tf_op jit(solution)/shard_map/all_to_all | solution.py:165
  44.1 13.0 %all-to-all-start.2 = ((f32[16,8,256]{2,1,0:T(8,128)}), f32[16,8,256]{2,1,0:T(8,128)S(1)}, u32[]{:S(2)}, u32[]{:S(2)}) async-start(f32[16,8,256]{2,1,0:T(8,128)} %broadcast_in_dim.9), calls=%async_computation.2 | async-start | bytes 262144 | tf_op jit(solution)/shard_map/all_to_all | solution.py:165
  57.1 1.1 project.1
  58.2 3.3 %collective-permute-start = (f32[256,256]{1,0:T(8,128)S(1)}, f32[256,256]{1,0:T(8,128)S(1)}, u32[]{:S(2)}, u32[]{:S(2)}) collective-permute-start(f32[256,256]{1,0:T(8,128)S(1)} %get-tuple-element.16), channel_id=1, source_target_pairs={{0,32},{32,64},{64,96},{96,0},{128,160},{160,192},{192,224},{224,1... | collective-permute-start | bytes 786440 | tf_op jit(solution)/shard_map/ppermute | solution.py:263
  61.5 4.0 %collective-permute-start.1 = (f32[256,256]{1,0:T(8,128)S(1)}, f32[256,256]{1,0:T(8,128)S(1)}, u32[]{:S(2)}, u32[]{:S(2)}) collective-permute-start(f32[256,256]{1,0:T(8,128)S(1)} %get-tuple-element.17), channel_id=1, source_target_pairs={{0,64},{32,96},{64,0},{96,32},{128,192},{160,224},{192,128},{224,1... | collective-permute-start | bytes 786440 | tf_op jit(solution)/shard_map/ppermute | solution.py:263
  65.5 3.1 %collective-permute-start.2 = (f32[256,256]{1,0:T(8,128)S(1)}, f32[256,256]{1,0:T(8,128)S(1)}, u32[]{:S(2)}, u32[]{:S(2)}) collective-permute-start(f32[256,256]{1,0:T(8,128)S(1)} %get-tuple-element.18), channel_id=1, source_target_pairs={{0,96},{32,0},{64,32},{96,64},{128,224},{160,128},{192,160},{224,1... | collective-permute-start | bytes 786440 | tf_op jit(solution)/shard_map/ppermute | solution.py:263
  69.1 0.7 broadcast_in_dim.10
  69.9 7.4 %all-to-all-start.3 = ((f32[32,8,256]{2,1,0:T(8,128)}), f32[32,8,256]{2,1,0:T(8,128)S(1)}, u32[]{:S(2)}, u32[]{:S(2)}) async-start(f32[32,8,256]{2,1,0:T(8,128)} %broadcast_in_dim.10), calls=%async_computation.3 | async-start | bytes 524288 | tf_op jit(solution)/shard_map/all_to_all | solution.py:165
  77.3 6.9 %collective-permute-done.1 = f32[256,256]{1,0:T(8,128)S(1)} collective-permute-done((f32[256,256]{1,0:T(8,128)S(1)}, f32[256,256]{1,0:T(8,128)S(1)}, u32[]{:S(2)}, u32[]{:S(2)}) %collective-permute-start.1) | collective-permute-done | bytes 262176 | tf_op jit(solution)/shard_map/ppermute | solution.py:263
  84.3 0.7 add.30
  85.0 1.2 all-to-all-done.3
  86.2 0.7 copy-done.4
  86.9 7.5 %all-to-all-start.4 = ((f32[4,64,256]{2,1,0:T(8,128)}), f32[4,64,256]{2,1,0:T(8,128)S(1)}, u32[]{:S(2)}, u32[]{:S(2)}) async-start(f32[4,64,256]{2,1,0:T(8,128)} %bitcast.4), calls=%async_computation.4 | async-start | bytes 524288 | tf_op jit(solution)/shard_map/all_to_all | solution.py:269
  94.4 10.8 %inverse_factor.1.inverse_ref = f32[256,256]{1,0:T(8,128)} custom-call(f32[256,256]{1,0:T(8,128)} %bitcast.12), custom_call_target="tpu_custom_call" | custom-call | flops 400000000 | bytes 524288 | tf_op jit(solution)/shard_map/inverse_factor/pallas_call | solution.py:90
  105.2 2.6 %all-to-all-done.4 = f32[4,64,256]{2,1,0:T(8,128)S(1)} async-done(((f32[4,64,256]{2,1,0:T(8,128)}), f32[4,64,256]{2,1,0:T(8,128)S(1)}, u32[]{:S(2)}, u32[]{:S(2)}) %all-to-all-start.4) | async-done | bytes 262176 | tf_op jit(solution)/shard_map/all_to_all | solution.py:269
  108.2 32.8 %all_gather.3.right_ref = bf16[1024,256]{1,0:T(8,128)(2,1)S(1)} all-gather(bf16[64,256]{1,0:T(8,128)(2,1)S(1)} %convolution_convert_fusion), channel_id=1, replica_groups=mesh['row'=16,'col'=8,'rep'=4] {'row'}, dimensions={0}, use_global_device_ids=true | all-gather | bytes 557056 | tf_op jit(solution)/shard_map/all_gather | solution.py:274
  141.7 11.7 %all-to-all-start.5 = ((f32[32,1,256]{2,1,0:T(1,128)}), f32[32,1,256]{2,1,0:T(1,128)S(1)}, u32[]{:S(2)}, u32[]{:S(2)}) async-start(f32[32,1,256]{2,1,0:T(1,128)} %broadcast_in_dim.11), calls=%async_computation.5 | async-start | bytes 65536 | tf_op jit(solution)/shard_map/all_to_all | solution.py:165
  153.4 5.7 %finish.1 = (f32[512,256]{1,0:T(8,128)}, bf16[512,1024]{1,0:T(8,128)(2,1)}) custom-call(f32[512,256]{1,0:T(8,128)} %bitcast.10, f32[256,256]{1,0:T(8,128)} %inverse_factor.1.inverse_ref, bf16[1024,256]{1,0:T(8,128)(2,1)} %copy-done.2, bf16[512,1024]{1,0:T(8,128)(2,1)} %get-tuple-element.14.buffer_ref), custom_call_target="tpu_custom_call" | custom-call | flops 268435456 | bytes 4000000 | tf_op jit(solution)/shard_map/finish/pallas_call | solution.py:223
  159.1 1.6 all-to-all-done.5
  160.8 2.1 %convert_divide_fusion = f32[1024,256]{1,0:T(8,128)} fusion(bf16[1024,256]{1,0:T(8,128)(2,1)} %copy-done.2, f32[256]{0:T(256)S(1)} %sqrt_add_fusion), kind=kLoop, calls=%fused_computation | loop fusion | flops 524288 | bytes 1573888 | tf_op jit(solution)/shard_map/div | solution.py:279
  (23 shorter events, 3.3 us)
Async XLA Ops:
  26.8 30.2 %copy-start.1 = (bf16[512,1024]{1,0:T(8,128)(2,1)S(1)}, bf16[512,1024]{1,0:T(8,128)(2,1)}, u32[]{:S(2)}) copy-start(bf16[512,1024]{1,0:T(8,128)(2,1)} %get-tuple-element.14.buffer_ref) | copy-start | bytes 3145732
  26.8 15.9 %all-to-all-start.1 = ((f32[32,16,256]{2,1,0:T(8,128)}), f32[32,16,256]{2,1,0:T(8,128)S(1)}, u32[]{:S(2)}, u32[]{:S(2)}) async-start(f32[32,16,256]{2,1,0:T(8,128)} %broadcast_in_dim.8), calls=%async_computation.1 | async-start | bytes 1048576 | tf_op jit(solution)/shard_map/all_to_all | solution.py:165
  42.7 15.5 %copy-start = (f32[32,16,256]{2,1,0:T(8,128)}, f32[32,16,256]{2,1,0:T(8,128)S(1)}, u32[]{:S(2)}) copy-start(f32[32,16,256]{2,1,0:T(8,128)S(1)} %all-to-all-done.1) | copy-start | bytes 1572868
  44.1 25.1 %all-to-all-start.2 = ((f32[16,8,256]{2,1,0:T(8,128)}), f32[16,8,256]{2,1,0:T(8,128)S(1)}, u32[]{:S(2)}, u32[]{:S(2)}) async-start(f32[16,8,256]{2,1,0:T(8,128)} %broadcast_in_dim.9), calls=%async_computation.2 | async-start | bytes 262144 | tf_op jit(solution)/shard_map/all_to_all | solution.py:165
  58.2 19.1 %collective-permute-start = (f32[256,256]{1,0:T(8,128)S(1)}, f32[256,256]{1,0:T(8,128)S(1)}, u32[]{:S(2)}, u32[]{:S(2)}) collective-permute-start(f32[256,256]{1,0:T(8,128)S(1)} %get-tuple-element.16), channel_id=1, source_target_pairs={{0,32},{32,64},{64,96},{96,0},{128,160},{160,192},{192,224},{224,1... | collective-permute-start | bytes 786440 | tf_op jit(solution)/shard_map/ppermute | solution.py:263
  61.5 22.7 %collective-permute-start.1 = (f32[256,256]{1,0:T(8,128)S(1)}, f32[256,256]{1,0:T(8,128)S(1)}, u32[]{:S(2)}, u32[]{:S(2)}) collective-permute-start(f32[256,256]{1,0:T(8,128)S(1)} %get-tuple-element.17), channel_id=1, source_target_pairs={{0,64},{32,96},{64,0},{96,32},{128,192},{160,224},{192,128},{224,1... | collective-permute-start | bytes 786440 | tf_op jit(solution)/shard_map/ppermute | solution.py:263
  65.5 18.8 %collective-permute-start.2 = (f32[256,256]{1,0:T(8,128)S(1)}, f32[256,256]{1,0:T(8,128)S(1)}, u32[]{:S(2)}, u32[]{:S(2)}) collective-permute-start(f32[256,256]{1,0:T(8,128)S(1)} %get-tuple-element.18), channel_id=1, source_target_pairs={{0,96},{32,0},{64,32},{96,64},{128,224},{160,128},{192,160},{224,1... | collective-permute-start | bytes 786440 | tf_op jit(solution)/shard_map/ppermute | solution.py:263
  69.9 16.4 %all-to-all-start.3 = ((f32[32,8,256]{2,1,0:T(8,128)}), f32[32,8,256]{2,1,0:T(8,128)S(1)}, u32[]{:S(2)}, u32[]{:S(2)}) async-start(f32[32,8,256]{2,1,0:T(8,128)} %broadcast_in_dim.10), calls=%async_computation.3 | async-start | bytes 524288 | tf_op jit(solution)/shard_map/all_to_all | solution.py:165
  86.2 0.7 copy-start.4
  86.9 20.8 %all-to-all-start.4 = ((f32[4,64,256]{2,1,0:T(8,128)}), f32[4,64,256]{2,1,0:T(8,128)S(1)}, u32[]{:S(2)}, u32[]{:S(2)}) async-start(f32[4,64,256]{2,1,0:T(8,128)} %bitcast.4), calls=%async_computation.4 | async-start | bytes 524288 | tf_op jit(solution)/shard_map/all_to_all | solution.py:269
  105.2 2.6 %copy-start.3 = (f32[256,256]{1,0:T(8,128)S(1)}, f32[256,256]{1,0:T(8,128)}, u32[]{:S(2)}) copy-start(f32[256,256]{1,0:T(8,128)} %inverse_factor.1.inverse_ref) | copy-start | bytes 786436
  140.9 12.5 %copy-start.2 = (bf16[1024,256]{1,0:T(8,128)(2,1)}, bf16[1024,256]{1,0:T(8,128)(2,1)S(1)}, u32[]{:S(2)}) copy-start(bf16[1024,256]{1,0:T(8,128)(2,1)S(1)} %all_gather.3.right_ref) | copy-start | bytes 1572868
  141.7 19.0 %all-to-all-start.5 = ((f32[32,1,256]{2,1,0:T(1,128)}), f32[32,1,256]{2,1,0:T(1,128)S(1)}, u32[]{:S(2)}, u32[]{:S(2)}) async-start(f32[32,1,256]{2,1,0:T(1,128)} %broadcast_in_dim.11), calls=%async_computation.5 | async-start | bytes 65536 | tf_op jit(solution)/shard_map/all_to_all | solution.py:165

commit v9 on v6

--- a/solution.py
+++ b/solution.py
@@ -56,45 +56,57 @@
     return done
 
 
-def inverse_factor_kernel(gram_ref, out_ref, rest_ref):
+def factor_kernel(gram_ref, left_ref, total_ref, factor_ref, part_ref, rest_ref, inv_ref):
     sub = lax.broadcasted_iota(jnp.int32, (8, 128), 0)
     lane = lax.broadcasted_iota(jnp.int32, (8, 128), 1)
     rest_ref[...] = gram_ref[...]
-    out_ref[...] = jnp.zeros((RANK, RANK), jnp.float32)
+    inv_ref[...] = jnp.zeros((RANK, RANK), jnp.float32)
+    held = gram_ref[0:BLOCK, 0:128]
     for low in range(0, RANK, BLOCK):
         high = low + BLOCK
-        base = low // 128 * 128
-        offset = low - base
+        offset = low % 128
         other = BLOCK - offset
         rows = []
         for r in range(BLOCK // 8):
-            held = rest_ref[low + 8 * r : low + 8 * r + 8, base : base + 128]
             unit = jnp.where(lane == other + 8 * r + sub, 1.0, 0.0)
-            rows.append(jnp.where((lane >= offset) & (lane < offset + BLOCK), held, unit))
+            inside = (lane >= offset) & (lane < offset + BLOCK)
+            rows.append(jnp.where(inside, held[8 * r : 8 * r + 8, :], unit))
         block = jnp.concatenate(eliminate(rows, offset, sub), axis=0)
         inverse = block[:, other : other + BLOCK]
+        if high < RANK:
+            base = high // 128 * 128
+            near = dot32(inverse, rest_ref[low:high, base : base + 128], 1, 0)
+            held = rest_ref[high : high + BLOCK, base : base + 128] - dot32(
+                near[:, high - base : high - base + BLOCK], near, 0, 0
+            )
         if low:
-            out_ref[low:high, 0:low] = dot32(inverse, out_ref[low:high, 0:low], 1, 0)
-        out_ref[low:high, low:high] = inverse
+            inv_ref[low:high, 0:low] = dot32(inverse, inv_ref[low:high, 0:low], 1, 0)
+        inv_ref[low:high, low:high] = inverse
         if high < RANK:
             upper = dot32(inverse, rest_ref[low:high, high:RANK], 1, 0)
-            solved = out_ref[low:high, 0:high]
+            solved = inv_ref[low:high, 0:high]
             rest_ref[high:RANK, high:RANK] = rest_ref[high:RANK, high:RANK] - dot32(
                 upper, upper, 0, 0
             )
-            out_ref[high:RANK, 0:high] = out_ref[high:RANK, 0:high] - dot32(upper, solved, 0, 0)
-
-
-def inverse_factor(gram_matrix):
+            inv_ref[high:RANK, 0:high] = inv_ref[high:RANK, 0:high] - dot32(upper, solved, 0, 0)
+    part_ref[...] = dot32(total_ref[...], inv_ref[...], 1, 1).astype(jnp.bfloat16)
+    factor_ref[...] = dot32(left_ref[...], inv_ref[...], 1, 1)
+
+
+def apply_factor(gram_matrix, left_raw, total):
     return pl.pallas_call(
-        inverse_factor_kernel,
-        out_shape=jax.ShapeDtypeStruct((RANK, RANK), jnp.float32),
-        in_specs=[pl.BlockSpec(memory_space=pltpu.VMEM)],
-        out_specs=pl.BlockSpec(memory_space=pltpu.VMEM),
-        scratch_shapes=[pltpu.VMEM((RANK, RANK), jnp.float32)],
-        cost_estimate=pl.CostEstimate(flops=400_000_000, bytes_accessed=524288, transcendentals=0),
-        name="inverse_factor",
-    )(gram_matrix)
+        factor_kernel,
+        out_shape=[
+            jax.ShapeDtypeStruct(left_raw.shape, jnp.float32),
+            jax.ShapeDtypeStruct(total.shape, jnp.bfloat16),
+        ],
+        in_specs=[pl.BlockSpec(memory_space=pltpu.VMEM)] * 3,
+        out_specs=[pl.BlockSpec(memory_space=pltpu.VMEM)] * 2,
+        scratch_shapes=[pltpu.VMEM((RANK, RANK), jnp.float32)] * 2,
+        compiler_params=pltpu.CompilerParams(vmem_limit_bytes=32 * 1024 * 1024),
+        cost_estimate=pl.CostEstimate(flops=600_000_000, bytes_accessed=2_000_000, transcendentals=0),
+        name="apply_factor",
+    )(gram_matrix, left_raw, total)
 
 
 def scatter_sum(x, axes, count):
@@ -157,26 +169,16 @@
     share = RANK // wide
     own = lax.dynamic_slice(left_raw, (0, place * share), (rows, share))
     gram_rows = jnp.sum(gather(dot32(own, left_raw, 0, 0), "row", tall), axis=0)
-    blocks = project(buffer, left_raw, lax.rem(lax.axis_index("row"), NEAR))
-
-    gram_rows, *blocks = lax.optimization_barrier((gram_rows, *blocks))
+    blocks = list(project(buffer, left_raw, lax.rem(lax.axis_index("row"), NEAR)))
+
     gram_matrix = gather(gram_rows, WIDE, wide).reshape(RANK, RANK)
     for shift in range(1, NEAR):
         ring = [(i, i // NEAR * NEAR + (i + shift) % NEAR) for i in range(tall)]
         blocks[shift] = lax.ppermute(blocks[shift], "row", ring)
-    inverse = inverse_factor(gram_matrix)
-
-    left_factor = dot32(left_raw, inverse, 1, 1)
+    gram_matrix, total = lax.optimization_barrier((gram_matrix, sum(blocks)))
+    left_factor, part = apply_factor(gram_matrix, left_raw, total)
     left_low = left_factor.astype(jnp.bfloat16)
-    part = dot32(sum(blocks), inverse, 1, 1).astype(jnp.bfloat16)
-    parts = lax.all_to_all(
-        jnp.broadcast_to(part[None], (far,) + part.shape),
-        "row",
-        0,
-        0,
-        axis_index_groups=strided,
-        tiled=True,
-    )
+    parts = lax.all_gather(part, "row", axis=0, axis_index_groups=strided)
     right_rows = jnp.sum(parts.astype(jnp.float32), axis=0).astype(jnp.bfloat16)
     right_low = lax.all_gather(
         right_rows, "row", axis=0, axis_index_groups=adjacent, tiled=True

time: 174 us -> 156 us (0.90)
  waiting for transfers between devices: 62.3 us -> 25.5 us
  blocking collectives: 36.7 us -> 61.2 us
  starting transfers between devices: 49 us -> 46.2 us
  matrix products: 4.76 us -> 2.54 us
    all_to_all x1 -> x0, waiting for transfers between devices: 26.9 us -> none  [local(): lax.all_to_all(jnp.broadcast_to(part[None], (far,) + part.shape), 'row',...]
    all_gather x0 -> x1, blocking collectives: none -> 19.7 us  [local(): parts = lax.all_gather(part, 'row', axis=0, axis_index_groups=strided)]
    all_to_all x4, waiting for transfers between devices: 28.4 us -> 18.8 us  [gather(): lax.all_to_all(jnp.broadcast_to(x[None], (count,) + x.shape), axes, 0, 0,...]
    all_gather x1, blocking collectives: 15.7 us -> 20.5 us  [local(): lax.all_gather(right_rows, 'row', axis=0, axis_index_groups=adjacent, til...]
    all_to_all x1 -> x0, starting transfers between devices: 3.47 us -> none  [local(): lax.all_to_all(jnp.broadcast_to(part[None], (far,) + part.shape), 'row',...]
    dot_general x3 -> x1, matrix products: 2.87 us -> 0.65 us  [dot32(): lax.dot_general(a, b, (((a_dim,), (b_dim,)), ((), ())), precision=lax.Pre...]
  transfers between devices with their start and end apart: 8 -> 7, of which waited for: 6 -> 5; matrix products, arithmetic and copies ran while one was open for 1% -> 2% of each run, Pallas kernels for 7% -> 1%
where the time goes in v9:
time: 156 us; the launch traced here: 155 us
  blocking collectives  61.2 us (39%)
  starting transfers between devices  46.2 us (30%)
  waiting for transfers between devices  25.5 us (16%)
  Pallas kernels  11.6 us (7%)
  other arithmetic  4.6 us (3%)
  local copies, waits for them, and re-layouts  2.9 us (2%)
  matrix products  2.54 us (2%)
    all_to_all x4, starting transfers between devices, gather(): lax.all_to_all(jnp.broadcast_to(x[None], (count,) + x.shape), axes, 0, 0,...  35.9 us
    all_to_all x1, blocking collectives, scatter_sum(): return jnp.sum(lax.all_to_all(parts, axes, 0, 0, tiled=True), axis=0)  21 us
    all_gather x1, blocking collectives, local(): lax.all_gather(right_rows, 'row', axis=0, axis_index_groups=adjacent, til...  20.5 us
    all_gather x1, blocking collectives, local(): parts = lax.all_gather(part, 'row', axis=0, axis_index_groups=strided)  19.7 us
    all_to_all x4, waiting for transfers between devices, gather(): lax.all_to_all(jnp.broadcast_to(x[None], (count,) + x.shape), axes, 0, 0,...  18.8 us
    pallas_call x1, Pallas kernels, apply_factor(): pl.pallas_call(factor_kernel, out_shape=[jax.ShapeDtypeStruct(left_raw.sh...  10.5 us
    ppermute x3, starting transfers between devices, local(): blocks[shift] = lax.ppermute(blocks[shift], 'row', ring)  10.3 us
    ppermute x3, waiting for transfers between devices, local(): blocks[shift] = lax.ppermute(blocks[shift], 'row', ring)  6.7 us
  transfers between devices with their start and end apart: 7, of which 5 were waited for; matrix products, arithmetic and copies ran while one was open for 2% of the time, Pallas kernels for 1%

profile of v9, /device:TPU:1, one launch (start us, length us, event | category | flops | bytes accessed | tf_op | source)
XLA Modules:
  0.0 155.4 jit_solution(17829618377759785897)
XLA Ops:
  0.6 2.0 %add_convert_fusion.buffer_ref = bf16[512,1024]{1,0:T(8,128)(2,1)S(1)} fusion(bf16[512,1024]{1,0:T(8,128)(2,1)} %param.4, bf16[512,1024]{1,0:T(8,128)(2,1)} %param.3), kind=kLoop, calls=%fused_computation.1 | loop fusion | flops 2097152 | bytes 3145728 | tf_op jit(solution)/shard_map/convert_element_type | solution.py:163
  3.1 21.0 %all_to_all.25 = f32[32,16,256]{2,1,0:T(8,128)S(1)} all-to-all(f32[32,16,256]{2,1,0:T(8,128)S(1)} %bitcast.14), channel_id=1, replica_groups=mesh['row'=16,'col'=8,'rep'=4] {'col','rep'}, dimensions={0} | all-to-all | bytes 1048576 | tf_op jit(solution)/shard_map/all_to_all | solution.py:114
  24.2 0.9 broadcast_in_dim.8
  25.0 4.4 %all-to-all-start.1 = ((f32[32,16,256]{2,1,0:T(8,128)}), f32[32,16,256]{2,1,0:T(8,128)S(1)}, u32[]{:S(2)}, u32[]{:S(2)}) async-start(f32[32,16,256]{2,1,0:T(8,128)} %broadcast_in_dim.8), calls=%async_computation.1 | async-start | bytes 1048576 | tf_op jit(solution)/shard_map/all_to_all | solution.py:118
  29.4 11.4 %all-to-all-done.1 = f32[32,16,256]{2,1,0:T(8,128)S(1)} async-done(((f32[32,16,256]{2,1,0:T(8,128)}), f32[32,16,256]{2,1,0:T(8,128)S(1)}, u32[]{:S(2)}, u32[]{:S(2)}) %all-to-all-start.1) | async-done | bytes 524320 | tf_op jit(solution)/shard_map/all_to_all | solution.py:118
  40.8 0.6 fusion.2
  41.4 0.7 broadcast_in_dim.9
  42.1 13.7 %all-to-all-start.2 = ((f32[16,8,256]{2,1,0:T(8,128)}), f32[16,8,256]{2,1,0:T(8,128)S(1)}, u32[]{:S(2)}, u32[]{:S(2)}) async-start(f32[16,8,256]{2,1,0:T(8,128)} %broadcast_in_dim.9), calls=%async_computation.2 | async-start | bytes 262144 | tf_op jit(solution)/shard_map/all_to_all | solution.py:118
  55.8 1.1 project.1
  56.9 3.3 %collective-permute-start = (f32[256,256]{1,0:T(8,128)S(1)}, f32[256,256]{1,0:T(8,128)}, u32[]{:S(2)}, u32[]{:S(2)}) collective-permute-start(f32[256,256]{1,0:T(8,128)S(1)} %get-tuple-element.12), channel_id=1, source_target_pairs={{0,32},{32,64},{64,96},{96,0},{128,160},{160,192},{192,224},{224,1... | collective-permute-start | bytes 786440 | tf_op jit(solution)/shard_map/ppermute | solution.py:177
  60.1 4.0 %collective-permute-start.1 = (f32[256,256]{1,0:T(8,128)S(1)}, f32[256,256]{1,0:T(8,128)}, u32[]{:S(2)}, u32[]{:S(2)}) collective-permute-start(f32[256,256]{1,0:T(8,128)S(1)} %get-tuple-element.13), channel_id=1, source_target_pairs={{0,64},{32,96},{64,0},{96,32},{128,192},{160,224},{192,128},{224,1... | collective-permute-start | bytes 786440 | tf_op jit(solution)/shard_map/ppermute | solution.py:177
  64.1 3.1 %collective-permute-start.2 = (f32[256,256]{1,0:T(8,128)S(1)}, f32[256,256]{1,0:T(8,128)}, u32[]{:S(2)}, u32[]{:S(2)}) collective-permute-start(f32[256,256]{1,0:T(8,128)S(1)} %get-tuple-element.14), channel_id=1, source_target_pairs={{0,96},{32,0},{64,32},{96,64},{128,224},{160,128},{192,160},{224,1... | collective-permute-start | bytes 786440 | tf_op jit(solution)/shard_map/ppermute | solution.py:177
  67.9 0.7 broadcast_in_dim.10
  68.6 7.5 %all-to-all-start.3 = ((f32[32,8,256]{2,1,0:T(8,128)}), f32[32,8,256]{2,1,0:T(8,128)S(1)}, u32[]{:S(2)}, u32[]{:S(2)}) async-start(f32[32,8,256]{2,1,0:T(8,128)} %broadcast_in_dim.10), calls=%async_computation.3 | async-start | bytes 524288 | tf_op jit(solution)/shard_map/all_to_all | solution.py:118
  76.1 6.7 %collective-permute-done.1 = f32[256,256]{1,0:T(8,128)} collective-permute-done((f32[256,256]{1,0:T(8,128)S(1)}, f32[256,256]{1,0:T(8,128)}, u32[]{:S(2)}, u32[]{:S(2)}) %collective-permute-start.1) | collective-permute-done | bytes 262176 | tf_op jit(solution)/shard_map/ppermute | solution.py:177
  82.8 1.2 add_add_fusion.total_ref
  83.9 1.1 all-to-all-done.3
  85.0 10.5 %apply_factor.1 = (f32[512,256]{1,0:T(8,128)}, bf16[256,256]{1,0:T(8,128)(2,1)S(1)}) custom-call(f32[256,256]{1,0:T(8,128)S(1)} %bitcast.12, f32[512,256]{1,0:T(8,128)S(1)} %bitcast.11, f32[256,256]{1,0:T(8,128)S(1)} %add_add_fusion.total_ref), custom_call_target="tpu_custom_call" | custom-call | flops 600000000 | bytes 2000000 | tf_op jit(solution)/shard_map/apply_factor/pallas_call | solution.py:97
  95.5 19.7 %all-gather = bf16[1024,256]{1,0:T(8,128)(2,1)S(1)} all-gather(bf16[256,256]{1,0:T(8,128)(2,1)S(1)} %get-tuple-element.18), channel_id=2, replica_groups={{0,128,256,384},{32,160,288,416},{64,192,320,448},{96,224,352,480},{1,1..., dimensions={0}, use_global_device_ids=true | all-gather | bytes 655360 | tf_op jit(solution)/shard_map/all_gather | solution.py:181
  115.3 20.5 %all_gather.11 = bf16[1024,256]{1,0:T(8,128)(2,1)S(1)} all-gather(bf16[256,256]{1,0:T(8,128)(2,1)S(1)} %reduce_sum.50), channel_id=1, replica_groups={{0,32,64,96},{128,160,192,224},{256,288,320,352},{384,416,448,480},{1,3..., dimensions={0}, use_global_device_ids=true | all-gather | bytes 655360 | tf_op jit(solution)/shard_map/all_gather | solution.py:183
  136.6 10.4 %all-to-all-start.4 = ((f32[32,1,256]{2,1,0:T(1,128)}), f32[32,1,256]{2,1,0:T(1,128)S(1)}, u32[]{:S(2)}, u32[]{:S(2)}) async-start(f32[32,1,256]{2,1,0:T(1,128)} %broadcast_in_dim.11), calls=%async_computation.4 | async-start | bytes 65536 | tf_op jit(solution)/shard_map/all_to_all | solution.py:118
  147.0 1.4 subtract_convert_fusion
  148.5 5.8 %all-to-all-done.4 = f32[32,1,256]{2,1,0:T(1,128)S(1)} async-done(((f32[32,1,256]{2,1,0:T(1,128)}), f32[32,1,256]{2,1,0:T(1,128)S(1)}, u32[]{:S(2)}, u32[]{:S(2)}) %all-to-all-start.4) | async-done | bytes 32800 | tf_op jit(solution)/shard_map/all_to_all | solution.py:118
  154.3 1.1 convert_divide_fusion
  (15 shorter events, 2.1 us)
Async XLA Ops:
  0.6 2.0 %copy-start = (bf16[1024,256]{1,0:T(8,128)(2,1)S(1)}, bf16[1024,256]{1,0:T(8,128)(2,1)}, u32[]{:S(2)}) copy-start(bf16[1024,256]{1,0:T(8,128)(2,1)} %param.5) | copy-start | bytes 1572868
  25.0 15.7 %all-to-all-start.1 = ((f32[32,16,256]{2,1,0:T(8,128)}), f32[32,16,256]{2,1,0:T(8,128)S(1)}, u32[]{:S(2)}, u32[]{:S(2)}) async-start(f32[32,16,256]{2,1,0:T(8,128)} %broadcast_in_dim.8), calls=%async_computation.1 | async-start | bytes 1048576 | tf_op jit(solution)/shard_map/all_to_all | solution.py:118
  42.1 25.8 %all-to-all-start.2 = ((f32[16,8,256]{2,1,0:T(8,128)}), f32[16,8,256]{2,1,0:T(8,128)S(1)}, u32[]{:S(2)}, u32[]{:S(2)}) async-start(f32[16,8,256]{2,1,0:T(8,128)} %broadcast_in_dim.9), calls=%async_computation.2 | async-start | bytes 262144 | tf_op jit(solution)/shard_map/all_to_all | solution.py:118
  56.9 19.2 %collective-permute-start = (f32[256,256]{1,0:T(8,128)S(1)}, f32[256,256]{1,0:T(8,128)}, u32[]{:S(2)}, u32[]{:S(2)}) collective-permute-start(f32[256,256]{1,0:T(8,128)S(1)} %get-tuple-element.12), channel_id=1, source_target_pairs={{0,32},{32,64},{64,96},{96,0},{128,160},{160,192},{192,224},{224,1... | collective-permute-start | bytes 786440 | tf_op jit(solution)/shard_map/ppermute | solution.py:177
  60.1 22.6 %collective-permute-start.1 = (f32[256,256]{1,0:T(8,128)S(1)}, f32[256,256]{1,0:T(8,128)}, u32[]{:S(2)}, u32[]{:S(2)}) collective-permute-start(f32[256,256]{1,0:T(8,128)S(1)} %get-tuple-element.13), channel_id=1, source_target_pairs={{0,64},{32,96},{64,0},{96,32},{128,192},{160,224},{192,128},{224,1... | collective-permute-start | bytes 786440 | tf_op jit(solution)/shard_map/ppermute | solution.py:177
  64.1 18.6 %collective-permute-start.2 = (f32[256,256]{1,0:T(8,128)S(1)}, f32[256,256]{1,0:T(8,128)}, u32[]{:S(2)}, u32[]{:S(2)}) collective-permute-start(f32[256,256]{1,0:T(8,128)S(1)} %get-tuple-element.14), channel_id=1, source_target_pairs={{0,96},{32,0},{64,32},{96,64},{128,224},{160,128},{192,160},{224,1... | collective-permute-start | bytes 786440 | tf_op jit(solution)/shard_map/ppermute | solution.py:177
  68.6 16.4 %all-to-all-start.3 = ((f32[32,8,256]{2,1,0:T(8,128)}), f32[32,8,256]{2,1,0:T(8,128)S(1)}, u32[]{:S(2)}, u32[]{:S(2)}) async-start(f32[32,8,256]{2,1,0:T(8,128)} %broadcast_in_dim.10), calls=%async_computation.3 | async-start | bytes 524288 | tf_op jit(solution)/shard_map/all_to_all | solution.py:118
  115.3 31.8 %copy-start.1 = (f32[512,256]{1,0:T(8,128)S(1)}, f32[512,256]{1,0:T(8,128)}, u32[]{:S(2)}) copy-start(f32[512,256]{1,0:T(8,128)} %get-tuple-element.9) | copy-start | bytes 1572868
  136.6 17.6 %all-to-all-start.4 = ((f32[32,1,256]{2,1,0:T(1,128)}), f32[32,1,256]{2,1,0:T(1,128)S(1)}, u32[]{:S(2)}, u32[]{:S(2)}) async-start(f32[32,1,256]{2,1,0:T(1,128)} %broadcast_in_dim.11), calls=%async_computation.4 | async-start | bytes 65536 | tf_op jit(solution)/shard_map/all_to_all | solution.py:118

commit v10 on v9

--- a/solution.py
+++ b/solution.py
@@ -56,7 +56,7 @@
     return done
 
 
-def factor_kernel(gram_ref, left_ref, total_ref, factor_ref, part_ref, rest_ref, inv_ref):
+def factor_kernel(gram_ref, left_ref, factor_ref, inv_ref, rest_ref):
     sub = lax.broadcasted_iota(jnp.int32, (8, 128), 0)
     lane = lax.broadcasted_iota(jnp.int32, (8, 128), 1)
     rest_ref[...] = gram_ref[...]
@@ -89,24 +89,23 @@
                 upper, upper, 0, 0
             )
             inv_ref[high:RANK, 0:high] = inv_ref[high:RANK, 0:high] - dot32(upper, solved, 0, 0)
-    part_ref[...] = dot32(total_ref[...], inv_ref[...], 1, 1).astype(jnp.bfloat16)
     factor_ref[...] = dot32(left_ref[...], inv_ref[...], 1, 1)
 
 
-def apply_factor(gram_matrix, left_raw, total):
+def apply_factor(gram_matrix, left_raw):
     return pl.pallas_call(
         factor_kernel,
         out_shape=[
             jax.ShapeDtypeStruct(left_raw.shape, jnp.float32),
-            jax.ShapeDtypeStruct(total.shape, jnp.bfloat16),
+            jax.ShapeDtypeStruct((RANK, RANK), jnp.float32),
         ],
-        in_specs=[pl.BlockSpec(memory_space=pltpu.VMEM)] * 3,
+        in_specs=[pl.BlockSpec(memory_space=pltpu.VMEM)] * 2,
         out_specs=[pl.BlockSpec(memory_space=pltpu.VMEM)] * 2,
-        scratch_shapes=[pltpu.VMEM((RANK, RANK), jnp.float32)] * 2,
+        scratch_shapes=[pltpu.VMEM((RANK, RANK), jnp.float32)],
         compiler_params=pltpu.CompilerParams(vmem_limit_bytes=32 * 1024 * 1024),
         cost_estimate=pl.CostEstimate(flops=600_000_000, bytes_accessed=2_000_000, transcendentals=0),
         name="apply_factor",
-    )(gram_matrix, left_raw, total)
+    )(gram_matrix, left_raw)
 
 
 def scatter_sum(x, axes, count):
@@ -175,9 +174,10 @@
     for shift in range(1, NEAR):
         ring = [(i, i // NEAR * NEAR + (i + shift) % NEAR) for i in range(tall)]
         blocks[shift] = lax.ppermute(blocks[shift], "row", ring)
-    gram_matrix, total = lax.optimization_barrier((gram_matrix, sum(blocks)))
-    left_factor, part = apply_factor(gram_matrix, left_raw, total)
+    gram_matrix, early = lax.optimization_barrier((gram_matrix, sum(blocks[:-1])))
+    left_factor, inverse = apply_factor(gram_matrix, left_raw)
     left_low = left_factor.astype(jnp.bfloat16)
+    part = dot32(early + blocks[-1], inverse, 1, 1).astype(jnp.bfloat16)
     parts = lax.all_gather(part, "row", axis=0, axis_index_groups=strided)
     right_rows = jnp.sum(parts.astype(jnp.float32), axis=0).astype(jnp.bfloat16)
     right_low = lax.all_gather(

time: 156 us -> 160 us (1.026)
  blocking collectives: 61.2 us -> 63.7 us
    all_gather x1, blocking collectives: 19.7 us -> 26.3 us  [local(): parts = lax.all_gather(part, 'row', axis=0, axis_index_groups=strided)]
    all_gather x1, blocking collectives: 20.5 us -> 16.4 us  [local(): lax.all_gather(right_rows, 'row', axis=0, axis_index_groups=adjacent, til...]
    ppermute x3, waiting for transfers between devices: 6.7 us -> 3.45 us  [local(): blocks[shift] = lax.ppermute(blocks[shift], 'row', ring)]
    all_to_all x4, waiting for transfers between devices: 18.8 us -> 22 us  [gather(): lax.all_to_all(jnp.broadcast_to(x[None], (count,) + x.shape), axes, 0, 0,...]
  transfers between devices with their start and end apart: 7 -> 7, of which waited for: 5 -> 5; matrix products, arithmetic and copies ran while one was open for 2% -> 2% of each run, Pallas kernels for 1% -> 7%
where the time goes in v10:
time: 160 us; the launch traced here: 159 us
  blocking collectives  63.7 us (40%)
  starting transfers between devices  46.8 us (29%)
  waiting for transfers between devices  25.4 us (16%)
  Pallas kernels  11.4 us (7%)
  other arithmetic  4.51 us (3%)
  matrix products  3.9 us (2%)
  local copies, waits for them, and re-layouts  2.9 us (2%)
    all_to_all x4, starting transfers between devices, gather(): lax.all_to_all(jnp.broadcast_to(x[None], (count,) + x.shape), axes, 0, 0,...  36.3 us
    all_gather x1, blocking collectives, local(): parts = lax.all_gather(part, 'row', axis=0, axis_index_groups=strided)  26.3 us
    all_to_all x4, waiting for transfers between devices, gather(): lax.all_to_all(jnp.broadcast_to(x[None], (count,) + x.shape), axes, 0, 0,...  22 us
    all_to_all x1, blocking collectives, scatter_sum(): return jnp.sum(lax.all_to_all(parts, axes, 0, 0, tiled=True), axis=0)  21 us
    all_gather x1, blocking collectives, local(): lax.all_gather(right_rows, 'row', axis=0, axis_index_groups=adjacent, til...  16.4 us
    ppermute x3, starting transfers between devices, local(): blocks[shift] = lax.ppermute(blocks[shift], 'row', ring)  10.5 us
    pallas_call x1, Pallas kernels, apply_factor(): pl.pallas_call(factor_kernel, out_shape=[jax.ShapeDtypeStruct(left_raw.sh...  10.3 us
    ppermute x3, waiting for transfers between devices, local(): blocks[shift] = lax.ppermute(blocks[shift], 'row', ring)  3.45 us
  transfers between devices with their start and end apart: 7, of which 5 were waited for; matrix products, arithmetic and copies ran while one was open for 2% of the time, Pallas kernels for 7%

profile of v10, /device:TPU:1, one launch (start us, length us, event | category | flops | bytes accessed | tf_op | source)
XLA Modules:
  0.0 159.4 jit_solution(11380668994342841427)
XLA Ops:
  0.6 2.0 %add_convert_fusion.buffer_ref = bf16[512,1024]{1,0:T(8,128)(2,1)S(1)} fusion(bf16[512,1024]{1,0:T(8,128)(2,1)} %param.4, bf16[512,1024]{1,0:T(8,128)(2,1)} %param.3), kind=kLoop, calls=%fused_computation.1 | loop fusion | flops 2097152 | bytes 3145728 | tf_op jit(solution)/shard_map/convert_element_type | solution.py:162
  3.1 21.0 %all_to_all.25 = f32[32,16,256]{2,1,0:T(8,128)S(1)} all-to-all(f32[32,16,256]{2,1,0:T(8,128)S(1)} %bitcast.15), channel_id=1, replica_groups=mesh['row'=16,'col'=8,'rep'=4] {'col','rep'}, dimensions={0} | all-to-all | bytes 1048576 | tf_op jit(solution)/shard_map/all_to_all | solution.py:113
  24.2 0.9 broadcast_in_dim.8
  25.0 4.4 %all-to-all-start.1 = ((f32[32,16,256]{2,1,0:T(8,128)}), f32[32,16,256]{2,1,0:T(8,128)S(1)}, u32[]{:S(2)}, u32[]{:S(2)}) async-start(f32[32,16,256]{2,1,0:T(8,128)} %broadcast_in_dim.8), calls=%async_computation.1 | async-start | bytes 1048576 | tf_op jit(solution)/shard_map/all_to_all | solution.py:117
  29.4 11.4 %all-to-all-done.1 = f32[32,16,256]{2,1,0:T(8,128)S(1)} async-done(((f32[32,16,256]{2,1,0:T(8,128)}), f32[32,16,256]{2,1,0:T(8,128)S(1)}, u32[]{:S(2)}, u32[]{:S(2)}) %all-to-all-start.1) | async-done | bytes 524320 | tf_op jit(solution)/shard_map/all_to_all | solution.py:117
  42.1 13.7 %all-to-all-start.2 = ((f32[16,8,256]{2,1,0:T(8,128)}), f32[16,8,256]{2,1,0:T(8,128)S(1)}, u32[]{:S(2)}, u32[]{:S(2)}) async-start(f32[16,8,256]{2,1,0:T(8,128)} %broadcast_in_dim.9), calls=%async_computation.2 | async-start | bytes 262144 | tf_op jit(solution)/shard_map/all_to_all | solution.py:117
  55.8 1.1 project.1
  56.9 3.3 %collective-permute-start = (f32[256,256]{1,0:T(8,128)S(1)}, f32[256,256]{1,0:T(8,128)}, u32[]{:S(2)}, u32[]{:S(2)}) collective-permute-start(f32[256,256]{1,0:T(8,128)S(1)} %get-tuple-element.12), channel_id=1, source_target_pairs={{0,32},{32,64},{64,96},{96,0},{128,160},{160,192},{192,224},{224,1... | collective-permute-start | bytes 786440 | tf_op jit(solution)/shard_map/ppermute | solution.py:176
  60.1 4.0 %collective-permute-start.1 = (f32[256,256]{1,0:T(8,128)S(1)}, f32[256,256]{1,0:T(8,128)}, u32[]{:S(2)}, u32[]{:S(2)}) collective-permute-start(f32[256,256]{1,0:T(8,128)S(1)} %get-tuple-element.13), channel_id=1, source_target_pairs={{0,64},{32,96},{64,0},{96,32},{128,192},{160,224},{192,128},{224,1... | collective-permute-start | bytes 786440 | tf_op jit(solution)/shard_map/ppermute | solution.py:176
  64.1 3.7 %all-to-all-done.2 = f32[16,8,256]{2,1,0:T(8,128)S(1)} async-done(((f32[16,8,256]{2,1,0:T(8,128)}), f32[16,8,256]{2,1,0:T(8,128)S(1)}, u32[]{:S(2)}, u32[]{:S(2)}) %all-to-all-start.2) | async-done | bytes 131104 | tf_op jit(solution)/shard_map/all_to_all | solution.py:117
  67.9 0.7 broadcast_in_dim.10
  68.6 7.5 %all-to-all-start.3 = ((f32[32,8,256]{2,1,0:T(8,128)}), f32[32,8,256]{2,1,0:T(8,128)S(1)}, u32[]{:S(2)}, u32[]{:S(2)}) async-start(f32[32,8,256]{2,1,0:T(8,128)} %broadcast_in_dim.10), calls=%async_computation.3 | async-start | bytes 524288 | tf_op jit(solution)/shard_map/all_to_all | solution.py:117
  76.1 3.3 %collective-permute-start.2 = (f32[256,256]{1,0:T(8,128)S(1)}, f32[256,256]{1,0:T(8,128)}, u32[]{:S(2)}, u32[]{:S(2)}) collective-permute-start(f32[256,256]{1,0:T(8,128)S(1)} %get-tuple-element.17), channel_id=1, source_target_pairs={{0,96},{32,0},{64,32},{96,64},{128,224},{160,128},{192,160},{224,1... | collective-permute-start | bytes 786440 | tf_op jit(solution)/shard_map/ppermute | solution.py:176
  79.4 3.4 %collective-permute-done.1 = f32[256,256]{1,0:T(8,128)} collective-permute-done((f32[256,256]{1,0:T(8,128)S(1)}, f32[256,256]{1,0:T(8,128)}, u32[]{:S(2)}, u32[]{:S(2)}) %collective-permute-start.1) | collective-permute-done | bytes 262176 | tf_op jit(solution)/shard_map/ppermute | solution.py:176
  82.8 1.1 add_add_fusion
  83.9 1.1 all-to-all-done.3
  85.0 10.3 %apply_factor.1 = (f32[512,256]{1,0:T(8,128)}, f32[256,256]{1,0:T(8,128)S(1)}) custom-call(f32[256,256]{1,0:T(8,128)S(1)} %bitcast.13, f32[512,256]{1,0:T(8,128)S(1)} %bitcast.12), custom_call_target="tpu_custom_call" | custom-call | flops 600000000 | bytes 2000000 | tf_op jit(solution)/shard_map/apply_factor/pallas_call | solution.py:96
  95.3 1.4 convolution_convert_fusion
  96.7 26.3 %all-gather = bf16[1024,256]{1,0:T(8,128)(2,1)S(1)} all-gather(bf16[256,256]{1,0:T(8,128)(2,1)S(1)} %convolution_convert_fusion), channel_id=2, replica_groups={{0,128,256,384},{32,160,288,416},{64,192,320,448},{96,224,352,480},{1,1..., dimensions={0}, use_global_device_ids=true | all-gather | bytes 655360 | tf_op jit(solution)/shard_map/all_gather | solution.py:181
  123.1 16.4 %all_gather.11 = bf16[1024,256]{1,0:T(8,128)(2,1)S(1)} all-gather(bf16[256,256]{1,0:T(8,128)(2,1)S(1)} %reduce_sum.50), channel_id=1, replica_groups={{0,32,64,96},{128,160,192,224},{256,288,320,352},{384,416,448,480},{1,3..., dimensions={0}, use_global_device_ids=true | all-gather | bytes 655360 | tf_op jit(solution)/shard_map/all_gather | solution.py:183
  140.3 10.8 %all-to-all-start.4 = ((f32[32,1,256]{2,1,0:T(1,128)}), f32[32,1,256]{2,1,0:T(1,128)S(1)}, u32[]{:S(2)}, u32[]{:S(2)}) async-start(f32[32,1,256]{2,1,0:T(1,128)} %broadcast_in_dim.11), calls=%async_computation.4 | async-start | bytes 65536 | tf_op jit(solution)/shard_map/all_to_all | solution.py:117
  151.1 1.4 subtract_convert_fusion
  152.6 5.8 %all-to-all-done.4 = f32[32,1,256]{2,1,0:T(1,128)S(1)} async-done(((f32[32,1,256]{2,1,0:T(1,128)}), f32[32,1,256]{2,1,0:T(1,128)S(1)}, u32[]{:S(2)}, u32[]{:S(2)}) %all-to-all-start.4) | async-done | bytes 32800 | tf_op jit(solution)/shard_map/all_to_all | solution.py:117
  158.4 1.1 convert_divide_fusion
  (16 shorter events, 2.8 us)
Async XLA Ops:
  0.6 2.0 %copy-start = (bf16[1024,256]{1,0:T(8,128)(2,1)S(1)}, bf16[1024,256]{1,0:T(8,128)(2,1)}, u32[]{:S(2)}) copy-start(bf16[1024,256]{1,0:T(8,128)(2,1)} %param.5) | copy-start | bytes 1572868
  25.0 15.7 %all-to-all-start.1 = ((f32[32,16,256]{2,1,0:T(8,128)}), f32[32,16,256]{2,1,0:T(8,128)S(1)}, u32[]{:S(2)}, u32[]{:S(2)}) async-start(f32[32,16,256]{2,1,0:T(8,128)} %broadcast_in_dim.8), calls=%async_computation.1 | async-start | bytes 1048576 | tf_op jit(solution)/shard_map/all_to_all | solution.py:117
  42.1 25.8 %all-to-all-start.2 = ((f32[16,8,256]{2,1,0:T(8,128)}), f32[16,8,256]{2,1,0:T(8,128)S(1)}, u32[]{:S(2)}, u32[]{:S(2)}) async-start(f32[16,8,256]{2,1,0:T(8,128)} %broadcast_in_dim.9), calls=%async_computation.2 | async-start | bytes 262144 | tf_op jit(solution)/shard_map/all_to_all | solution.py:117
  56.9 22.5 %collective-permute-start = (f32[256,256]{1,0:T(8,128)S(1)}, f32[256,256]{1,0:T(8,128)}, u32[]{:S(2)}, u32[]{:S(2)}) collective-permute-start(f32[256,256]{1,0:T(8,128)S(1)} %get-tuple-element.12), channel_id=1, source_target_pairs={{0,32},{32,64},{64,96},{96,0},{128,160},{160,192},{192,224},{224,1... | collective-permute-start | bytes 786440 | tf_op jit(solution)/shard_map/ppermute | solution.py:176
  60.1 22.7 %collective-permute-start.1 = (f32[256,256]{1,0:T(8,128)S(1)}, f32[256,256]{1,0:T(8,128)}, u32[]{:S(2)}, u32[]{:S(2)}) collective-permute-start(f32[256,256]{1,0:T(8,128)S(1)} %get-tuple-element.13), channel_id=1, source_target_pairs={{0,64},{32,96},{64,0},{96,32},{128,192},{160,224},{192,128},{224,1... | collective-permute-start | bytes 786440 | tf_op jit(solution)/shard_map/ppermute | solution.py:176
  68.6 16.4 %all-to-all-start.3 = ((f32[32,8,256]{2,1,0:T(8,128)}), f32[32,8,256]{2,1,0:T(8,128)S(1)}, u32[]{:S(2)}, u32[]{:S(2)}) async-start(f32[32,8,256]{2,1,0:T(8,128)} %broadcast_in_dim.10), calls=%async_computation.3 | async-start | bytes 524288 | tf_op jit(solution)/shard_map/all_to_all | solution.py:117
  76.1 19.3 %collective-permute-start.2 = (f32[256,256]{1,0:T(8,128)S(1)}, f32[256,256]{1,0:T(8,128)}, u32[]{:S(2)}, u32[]{:S(2)}) collective-permute-start(f32[256,256]{1,0:T(8,128)S(1)} %get-tuple-element.17), channel_id=1, source_target_pairs={{0,96},{32,0},{64,32},{96,64},{128,224},{160,128},{192,160},{224,1... | collective-permute-start | bytes 786440 | tf_op jit(solution)/shard_map/ppermute | solution.py:176
  123.0 28.1 %copy-start.1 = (f32[512,256]{1,0:T(8,128)S(1)}, f32[512,256]{1,0:T(8,128)}, u32[]{:S(2)}) copy-start(f32[512,256]{1,0:T(8,128)} %get-tuple-element.9) | copy-start | bytes 1572868
  140.3 18.0 %all-to-all-start.4 = ((f32[32,1,256]{2,1,0:T(1,128)}), f32[32,1,256]{2,1,0:T(1,128)S(1)}, u32[]{:S(2)}, u32[]{:S(2)}) async-start(f32[32,1,256]{2,1,0:T(1,128)} %broadcast_in_dim.11), calls=%async_computation.4 | async-start | bytes 65536 | tf_op jit(solution)/shard_map/all_to_all | solution.py:117
